TPU v7x, 32 devices: a whole 2x2x4 slice. The times are simulated.
32 devices in a mesh: samp: 4 (over z), seq: 8 (over y, x, core).
Axes of the slice: x: 2, y: 2, z: 4, core: 2. Of those that a mesh axis runs over, the one named last changes fastest.
Arguments:
- atom_input: bfloat16 [32, 4096, 128], P('samp', 'seq'), may hold values from -6 to 6
- token_input: bfloat16 [32, 512, 768], P('samp', 'seq'), may hold values from -6 to 6
- atom_counts: int32 [512], replicated, may hold values from 1 to 8
- key_offsets: int32 [128], P('seq'), may hold values from -96 to 0, as said below
- atom_pairs: bfloat16 [128, 32, 128, 16], P('seq'), may hold values from -6 to 6
- pair_features: bfloat16 [512, 512, 128], P('seq'), may hold values from -6 to 6
- single_features: bfloat16 [512, 384], P('seq'), may hold values from -6 to 6
- noise_levels: float32 [32], P('samp'), may hold values from 0.5 to 160
- noise_direction: float32 [384], replicated, may hold values from -6 to 6
- atom_proj: bfloat16 [128, 512], P('samp'), may hold values from -0.5 to 0.5
- atom_qbias: bfloat16 [128], P('samp'), may hold values from -4 to 4
- atom_pairw: bfloat16 [16, 4], P('samp'), may hold values from -1.5 to 1.5
- atom_outw: bfloat16 [128, 128], P('samp'), may hold values from -1 to 1
- atom_upw: bfloat16 [128, 512], P('samp'), may hold values from -0.5 to 0.5
- atom_downw: bfloat16 [256, 128], P('samp'), may hold values from -0.375 to 0.375
- pool_weight: bfloat16 [128, 768], P('samp'), may hold values from -0.5 to 0.5
- cond_weight: bfloat16 [384, 4608], P('samp'), may hold values from -0.3125 to 0.3125
- cond_bias: bfloat16 [4608], P('samp'), may hold values from -4 to 4
- token_proj: bfloat16 [768, 3072], P('samp'), may hold values from -0.21875 to 0.21875
- token_qbias: bfloat16 [768], P('samp'), may hold values from -4 to 4
- token_pairw: bfloat16 [128, 16], P('samp'), may hold values from -0.5 to 0.5
- token_outw: bfloat16 [768, 768], P('samp'), may hold values from -0.875 to 0.875
- token_upw: bfloat16 [768, 3072], P('samp'), may hold values from -0.21875 to 0.21875
- token_downw: bfloat16 [1536, 768], P('samp'), may hold values from -0.15625 to 0.15625
- cotangent: bfloat16 [32, 512, 768], P('samp', 'seq'), may hold values from -6 to 6
Outputs:
- block_out: bfloat16 [32, 512, 768], P('samp', 'seq')
- atom_grad: float32 [32, 4096, 128], P('samp', 'seq')
- token_grad: float32 [32, 512, 768], P('samp', 'seq')
- grad_atom_proj: float32 [128, 512], P('samp')
- grad_atom_qbias: float32 [128], P('samp')
- grad_atom_pairw: float32 [16, 4], P('samp')
- grad_atom_outw: float32 [128, 128], P('samp')
- grad_atom_upw: float32 [128, 512], P('samp')
- grad_atom_downw: float32 [256, 128], P('samp')
- grad_pool_weight: float32 [128, 768], P('samp')
- grad_cond_weight: float32 [384, 4608], P('samp')
- grad_cond_bias: float32 [4608], P('samp')
- grad_token_proj: float32 [768, 3072], P('samp')
- grad_token_qbias: float32 [768], P('samp')
- grad_token_pairw: float32 [128, 16], P('samp')
- grad_token_outw: float32 [768, 768], P('samp')
- grad_token_upw: float32 [768, 3072], P('samp')
- grad_token_downw: float32 [1536, 768], P('samp')
Inputs may be any that keep to these rules, and one draw needn't show every extreme that they name: `key_offsets`: both ends of the range occur.
All inputs are finite; a program needn't handle non-finite values.
Results may differ from a plain program's by a relative error of at most 0.03.
Values may be sent and summed in bfloat16 or wider, within the bound.
A program may use at most 384 MiB of HBM per device.

v0:
```python
import functools

import jax
import jax.numpy as jnp
from jax import lax
from jax.experimental import pallas as pl
from jax.experimental.pallas import tpu as pltpu
from jax.sharding import PartitionSpec as P

MAX_ATOMS = 8
WIN_Q = 32
WIN_K = 128
ATOM_HEADS = 4
RIM = 96
LANES = 128

norm_eps = 1e-05
sigma_data = 16.0
masked_score = -1000000000.0
bf16 = jnp.bfloat16
f32 = jnp.float32
vmem_bytes = 56 << 20


def dot_last(left_op, right_op):
    return jnp.einsum("...k,kn->...n", left_op, right_op, preferred_element_type=f32)


def dot_back(grad_op, weight):
    return jnp.einsum("...n,kn->...k", grad_op, weight, preferred_element_type=f32)


def weight_grad(left_op, grad_op):
    flat_left = left_op.reshape(-1, left_op.shape[-1])
    flat_grad = grad_op.reshape(-1, grad_op.shape[-1])
    return jnp.einsum("rk,rn->kn", flat_left, flat_grad, preferred_element_type=f32)


def mm(left_op, right_op):
    return lax.dot_general(left_op, right_op, (((1,), (0,)), ((), ())), preferred_element_type=f32)


def mm_nt(left_op, right_op):
    return lax.dot_general(left_op, right_op, (((1,), (1,)), ((), ())), preferred_element_type=f32)


def mm_tn(left_op, right_op):
    return lax.dot_general(left_op, right_op, (((0,), (0,)), ((), ())), preferred_element_type=f32)


def norm_stats(operand):
    center = operand - jnp.mean(operand, -1, keepdims=True)
    inv_std = lax.rsqrt(jnp.mean(center * center, -1, keepdims=True) + norm_eps)
    return (center * inv_std, inv_std)


def norm_back(normed, inv_std, grad_op):
    return inv_std * (
        grad_op
        - jnp.mean(grad_op, -1, keepdims=True)
        - normed * jnp.mean(grad_op * normed, -1, keepdims=True)
    )


def sigmoid(operand):
    return 1.0 / (1.0 + jnp.exp(-operand))


def whole(shape):
    return pl.BlockSpec(shape, lambda *_: (0,) * len(shape))


def per_sample(shape):
    return pl.BlockSpec((1,) + shape, lambda b, *_: (b,) + (0,) * len(shape))


def params():
    return pltpu.CompilerParams(vmem_limit_bytes=vmem_bytes)


def square_sums(ones_op, squares):
    upper = squares.astype(bf16)
    lower = (squares - upper.astype(f32)).astype(bf16)
    return upper, lower


def head_stack(rows, heads, head_dim, first):
    lane = lax.broadcasted_iota(jnp.int32, rows.shape, 1)
    parts = []
    for head in range(heads):
        low = first + head * head_dim
        parts.append(jnp.where((lane >= low) & (lane < low + head_dim), rows, jnp.zeros_like(rows)))
    return jnp.concatenate(parts, 0)


def head_fold(stacked, heads, head_dim, first):
    count = stacked.shape[0] // heads
    lane = lax.broadcasted_iota(jnp.int32, (count, stacked.shape[1]), 1)
    total = jnp.zeros((count, stacked.shape[1]), f32)
    for head in range(heads):
        low = first + head * head_dim
        part = stacked[head * count : (head + 1) * count]
        total = jnp.where((lane >= low) & (lane < low + head_dim), part, total)
    return total


def pair_stats(pairs, fold):
    upper, lower = square_sums(fold, pairs.astype(f32) * pairs.astype(f32))
    features = pairs.shape[0] // WIN_Q
    mean = mm(fold, pairs) * (1.0 / features)
    square = (mm(fold, upper) + mm(fold, lower)) * (1.0 / features)
    var = jnp.maximum(square - mean * mean, 0.0)
    inv_std = lax.rsqrt(var + norm_eps)
    return mean, inv_std


def pair_fold(features):
    shape = (WIN_Q, WIN_Q * features)
    row = lax.broadcasted_iota(jnp.int32, shape, 0)
    column = lax.broadcasted_iota(jnp.int32, shape, 1)
    return jnp.where(column // features == row, 1.0, 0.0).astype(bf16)


def atom_fwd_kernel(
    starts,
    ext_ref,
    pairs_ref,
    spread_ref,
    blocked_ref,
    share_ref,
    wide_ref,
    down_ref,
    qbias_ref,
    pooled_ref,
    query_ref,
    keyval_ref,
    gate_ref,
    probs_ref,
    attend_ref,
    mid_ref,
    bias_s,
    keys_s,
    values_s,
):
    width = ext_ref.shape[-1]
    head_dim = width // ATOM_HEADS
    scale = float(head_dim) ** (-0.5)
    slots = query_ref.shape[1]
    windows = slots // WIN_Q
    hidden_width = down_ref.shape[0]
    model_width = pooled_ref.shape[-1]
    features = pairs_ref.shape[1] // WIN_Q

    @pl.when(pl.program_id(0) == 0)
    def _():
        fold = pair_fold(features)
        spread = spread_ref[...]
        spread_sum = jnp.sum(spread.astype(f32), -1, keepdims=True)
        first_lane = jnp.where(
            lax.broadcasted_iota(jnp.int32, (ATOM_HEADS * WIN_Q, LANES), 1) == 0, 1.0, 0.0
        ).astype(bf16)

        def one(win, carry):
            pairs = pairs_ref[win]
            mean, inv_std = pair_stats(pairs, fold)
            mean = jnp.concatenate([mean] * ATOM_HEADS, 0)
            inv_std = jnp.concatenate([inv_std] * ATOM_HEADS, 0)
            blocked = blocked_ref[pl.ds(starts[win], WIN_K), :].astype(bf16)
            bias = inv_std * (mm(spread, pairs) - mean * spread_sum)
            bias_s[win] = bias + mm_nt(first_lane, blocked)
            return carry

        lax.fori_loop(0, windows, one, 0)

    rows = ext_ref[0].astype(f32)
    normed_low = norm_stats(rows)[0].astype(bf16)
    key_val = mm(normed_low, wide_ref[:, width : 3 * width]).astype(bf16)
    keyval_ref[0] = key_val
    keys_s[...] = key_val[:, :width].astype(f32)
    values_s[...] = key_val[:, width:].astype(f32)
    own_low = normed_low[RIM : RIM + slots]
    query_ref[0] = (mm(own_low, wide_ref[:, :width]) + qbias_ref[...]).astype(bf16)
    gate_ref[0] = mm(own_low, wide_ref[:, 3 * width : 4 * width])

    def one_window(win):
        first = pl.multiple_of(win * WIN_Q, WIN_Q)
        keys = keys_s[pl.ds(starts[win], WIN_K), :].astype(bf16)
        values = values_s[pl.ds(starts[win], WIN_K), :].astype(bf16)
        stacked = head_stack(query_ref[0, pl.ds(first, WIN_Q), :], ATOM_HEADS, head_dim, 0)
        scores = mm_nt(stacked, keys) * scale + bias_s[win]
        exp_scores = jnp.exp(scores - jnp.max(scores, -1, keepdims=True))
        probs = exp_scores * (1.0 / jnp.sum(exp_scores, -1, keepdims=True))
        probs_low = probs.astype(bf16)
        probs_ref[0, win] = probs_low
        attend = head_fold(mm(probs_low, values), ATOM_HEADS, head_dim, 0)
        attend_ref[0, pl.ds(first, WIN_Q), :] = attend

    def some_windows(step, carry):
        for part in range(4):
            one_window(step * 4 + part)
        return carry

    lax.fori_loop(0, windows // 4, some_windows, 0)

    gated_low = (attend_ref[0] * sigmoid(gate_ref[0])).astype(bf16)
    offset = 4 * width
    upw = wide_ref[:, offset : offset + 2 * hidden_width]
    offset += 2 * hidden_width
    pool_weight = wide_ref[:, offset : offset + model_width]
    outw = wide_ref[:, offset + model_width : offset + model_width + width]
    mid = rows[RIM : RIM + slots] + mm(gated_low, outw)
    mid_ref[0] = mid
    ffn_low = norm_stats(mid)[0].astype(bf16)
    upper = mm(ffn_low, upw)
    first_half, second_half = upper[:, :hidden_width], upper[:, hidden_width:]
    hidden = (first_half * sigmoid(first_half) * second_half).astype(bf16)
    final_low = (mid + mm(hidden, down_ref[...])).astype(bf16)
    pool_pre = mm(final_low, pool_weight)
    share = share_ref[...]
    for lane in range(0, model_width, LANES):
        part = pool_pre[:, lane : lane + LANES]
        part = part * sigmoid(part) * share
        pooled_ref[0, :, lane : lane + LANES] = jnp.sum(
            part.reshape(slots // MAX_ATOMS, MAX_ATOMS, LANES), 1
        )


def atom_forward(ext, starts, pairs, spread, blocked, share, wide, down, qbias):
    samples, ext_slots, width = ext.shape
    slots = ext_slots - 2 * RIM
    tokens = slots // MAX_ATOMS
    windows = slots // WIN_Q
    model_width = wide.shape[1] - 5 * width - 2 * down.shape[0]
    stack = ATOM_HEADS * WIN_Q
    outs = (
        ((tokens, model_width), f32),
        ((slots, width), bf16),
        ((ext_slots, 2 * width), bf16),
        ((slots, width), f32),
        ((windows, stack, WIN_K), bf16),
        ((slots, width), f32),
        ((slots, width), f32),
    )
    return pl.pallas_call(
        atom_fwd_kernel,
        out_shape=[jax.ShapeDtypeStruct((samples,) + shape, kind) for shape, kind in outs],
        grid_spec=pltpu.PrefetchScalarGridSpec(
            num_scalar_prefetch=1,
            grid=(samples,),
            in_specs=[
                per_sample((ext_slots, width)),
                whole(pairs.shape),
                whole(spread.shape),
                whole(blocked.shape),
                whole(share.shape),
                whole(wide.shape),
                whole(down.shape),
                whole(qbias.shape),
            ],
            out_specs=[per_sample(shape) for shape, _ in outs],
            scratch_shapes=[
                pltpu.VMEM((windows, stack, WIN_K), f32),
                pltpu.VMEM((ext_slots, width), f32),
                pltpu.VMEM((ext_slots, width), f32),
            ],
        ),
        compiler_params=params(),
        name="atom_forward",
    )(starts, ext, pairs, spread, blocked, share, wide, down, qbias)


def atom_bwd_kernel(
    starts,
    grad_ref,
    query_ref,
    keyval_ref,
    gate_ref,
    probs_ref,
    attend_ref,
    mid_ref,
    pairs_ref,
    share_ref,
    wide_ref,
    down_ref,
    mix_ref,
    own_ref,
    left_ref,
    right_ref,
    midgrad_ref,
    qbias_ref,
    outw_ref,
    upw_ref,
    downw_ref,
    pool_ref,
    pairw_ref,
    pairm_ref,
    keys_s,
    values_s,
    acck_s,
    accv_s,
    bias_s,
    attlow_s,
    dq_s,
):
    width = query_ref.shape[-1]
    head_dim = width // ATOM_HEADS
    scale = float(head_dim) ** (-0.5)
    slots = query_ref.shape[1]
    windows = slots // WIN_Q
    hidden_width = down_ref.shape[0]
    model_width = grad_ref.shape[-1]
    tokens = grad_ref.shape[1]
    sample = pl.program_id(0)

    @pl.when(sample == 0)
    def _():
        for ref in (qbias_ref, outw_ref, upw_ref, downw_ref, pool_ref, pairw_ref, pairm_ref, bias_s):
            ref[...] = jnp.zeros_like(ref)

    offset = 4 * width
    upw = wide_ref[:, offset : offset + 2 * hidden_width]
    offset += 2 * hidden_width
    pool_weight = wide_ref[:, offset : offset + model_width]
    outw = wide_ref[:, offset + model_width : offset + model_width + width]
    down = down_ref[...]

    mid = mid_ref[0]
    normed_mid, inv_mid = norm_stats(mid)
    ffn_low = normed_mid.astype(bf16)
    upper = mm(ffn_low, upw)
    first_half, second_half = upper[:, :hidden_width], upper[:, hidden_width:]
    sig_first = sigmoid(first_half)
    hidden = (first_half * sig_first * second_half).astype(bf16)
    final_low = (mid + mm(hidden, down)).astype(bf16)
    pool_pre = mm(final_low, pool_weight)
    share = share_ref[...]
    pool_parts = []
    for lane in range(0, model_width, LANES):
        part = pool_pre[:, lane : lane + LANES]
        grad = jnp.broadcast_to(
            grad_ref[0, :, lane : lane + LANES][:, None, :], (tokens, MAX_ATOMS, LANES)
        ).reshape(slots, LANES)
        sig_pool = sigmoid(part)
        pool_parts.append((grad * share * sig_pool * (1.0 + part * (1.0 - sig_pool))).astype(bf16))
    pool_grad = jnp.concatenate(pool_parts, 1)
    final_grad = mm_nt(pool_grad, pool_weight)
    pool_ref[...] += mm_tn(final_low, pool_grad)
    branch_low = final_grad.astype(bf16)
    hidden_grad = mm_nt(branch_low, down)
    first_grad = hidden_grad * second_half * sig_first * (1.0 + first_half * (1.0 - sig_first))
    second_grad = hidden_grad * first_half * sig_first
    upper_grad = jnp.concatenate([first_grad.astype(bf16), second_grad.astype(bf16)], 1)
    downw_ref[...] += mm_tn(hidden, branch_low)
    upw_ref[...] += mm_tn(ffn_low, upper_grad)
    mid_grad = final_grad + norm_back(normed_mid, inv_mid, mm_nt(upper_grad, upw))
    midgrad_ref[0] = mid_grad
    out_low = mid_grad.astype(bf16)
    gated_grad = mm_nt(out_low, outw)
    sig_gate = sigmoid(gate_ref[0])
    attend = attend_ref[0]
    gated_low = (attend * sig_gate).astype(bf16)
    outw_ref[...] += mm_tn(gated_low, out_low)
    attlow_s[...] = (gated_grad * sig_gate).astype(bf16)
    mix_ref[0, :, width:] = (gated_grad * attend * sig_gate * (1.0 - sig_gate)).astype(bf16)

    keys_s[...] = keyval_ref[0, :, :width].astype(f32)
    values_s[...] = keyval_ref[0, :, width:].astype(f32)
    acck_s[...] = jnp.zeros_like(acck_s)
    accv_s[...] = jnp.zeros_like(accv_s)

    def one_window(win):
        first = pl.multiple_of(win * WIN_Q, WIN_Q)
        start = starts[win]
        keys = keys_s[pl.ds(start, WIN_K), :].astype(bf16)
        values = values_s[pl.ds(start, WIN_K), :].astype(bf16)
        queries = head_stack(query_ref[0, pl.ds(first, WIN_Q), :], ATOM_HEADS, head_dim, 0)
        att = head_stack(attlow_s[pl.ds(first, WIN_Q), :], ATOM_HEADS, head_dim, 0)
        probs_low = probs_ref[0, win]
        probs = probs_low.astype(f32)
        prob_grad = mm_nt(att, values)
        delta = jnp.sum(prob_grad * probs, -1, keepdims=True)
        score_low = (probs * (prob_grad - delta)).astype(bf16)
        bias_s[win] += score_low.astype(f32)
        dq_s[pl.ds(first, WIN_Q), :] = (
            head_fold(mm(score_low, keys), ATOM_HEADS, head_dim, 0) * scale
        )
        acck_s[pl.ds(start, WIN_K), :] += mm_tn(score_low, queries) * scale
        accv_s[pl.ds(start, WIN_K), :] += mm_tn(probs_low, att)

    def some_windows(step, carry):
        for part in range(4):
            one_window(step * 4 + part)
        return carry

    lax.fori_loop(0, windows // 4, some_windows, 0)

    query_grad = dq_s[...]
    qbias_ref[...] += jnp.sum(query_grad, 0, keepdims=True)
    mix_ref[0, :, :width] = query_grad.astype(bf16)
    for ref, low, high in ((own_ref, RIM, RIM + slots), (left_ref, 0, RIM), (right_ref, RIM + slots, slots + 2 * RIM)):
        ref[0, :, :width] = acck_s[low:high, :].astype(ref.dtype)
        ref[0, :, width:] = accv_s[low:high, :].astype(ref.dtype)

    @pl.when(sample == pl.num_programs(0) - 1)
    def _():
        fold = pair_fold(pairs_ref.shape[1] // WIN_Q)

        def one(win, carry):
            pairs = pairs_ref[win]
            mean, inv_std = pair_stats(pairs, fold)
            scaled = bias_s[win] * jnp.concatenate([inv_std] * ATOM_HEADS, 0)
            pairm_ref[...] += scaled * jnp.concatenate([mean] * ATOM_HEADS, 0)
            upper = scaled.astype(bf16)
            lower = (scaled - upper.astype(f32)).astype(bf16)
            pairw_ref[...] += mm_nt(upper, pairs) + mm_nt(lower, pairs)
            return carry

        lax.fori_loop(0, windows, one, 0)


def atom_backward(grad, starts, stored, pairs, share, wide, down):
    query, keyval, gate, probs, attend, mid = stored
    samples, slots, width = query.shape
    ext_slots = slots + 2 * RIM
    windows = slots // WIN_Q
    model_width = grad.shape[-1]
    hidden_width = down.shape[0]
    stack = ATOM_HEADS * WIN_Q
    outs = (
        ((slots, 2 * width), bf16),
        ((slots, 2 * width), f32),
        ((RIM, 2 * width), bf16),
        ((RIM, 2 * width), bf16),
        ((slots, width), f32),
    )
    totals = (
        (1, width),
        (width, width),
        (width, 2 * hidden_width),
        (hidden_width, width),
        (width, model_width),
        (stack, pairs.shape[1]),
        (stack, WIN_K),
    )
    return pl.pallas_call(
        atom_bwd_kernel,
        out_shape=[jax.ShapeDtypeStruct((samples,) + shape, kind) for shape, kind in outs]
        + [jax.ShapeDtypeStruct(shape, f32) for shape in totals],
        grid_spec=pltpu.PrefetchScalarGridSpec(
            num_scalar_prefetch=1,
            grid=(samples,),
            in_specs=[per_sample(grad.shape[1:])]
            + [per_sample(part.shape[1:]) for part in stored]
            + [whole(part.shape) for part in (pairs, share, wide, down)],
            out_specs=[per_sample(shape) for shape, _ in outs] + [whole(shape) for shape in totals],
            scratch_shapes=[
                pltpu.VMEM((ext_slots, width), f32),
                pltpu.VMEM((ext_slots, width), f32),
                pltpu.VMEM((ext_slots, width), f32),
                pltpu.VMEM((ext_slots, width), f32),
                pltpu.VMEM((windows, stack, WIN_K), f32),
                pltpu.VMEM((slots, width), bf16),
                pltpu.VMEM((slots, width), f32),
            ],
        ),
        compiler_params=params(),
        name="atom_backward",
    )(starts, grad, *stored, pairs, share, wide, down)


def atom_input_kernel(
    rows_ref, mix_ref, own_ref, left_ref, right_ref, midgrad_ref, wide_ref, grad_ref, proj_ref
):
    width = rows_ref.shape[-1]

    @pl.when(pl.program_id(0) == 0)
    def _():
        proj_ref[...] = jnp.zeros_like(proj_ref)

    normed, inv_std = norm_stats(rows_ref[0].astype(f32))
    slots = normed.shape[0]
    own = own_ref[0]
    head = own[:RIM] + left_ref[0].astype(f32)
    tail = own[slots - RIM :] + right_ref[0].astype(f32)
    own = jnp.concatenate([head, own[RIM : slots - RIM], tail], 0).astype(bf16)
    mix = jnp.concatenate([mix_ref[0, :, :width], own, mix_ref[0, :, width:]], 1)
    proj_ref[...] += mm_tn(normed.astype(bf16), mix)
    normed_grad = mm_nt(mix, wide_ref[:, : 4 * width])
    grad_ref[0] = midgrad_ref[0] + norm_back(normed, inv_std, normed_grad)


def atom_input_backward(rows, mix, own, left, right, midgrad, wide):
    samples, slots, width = rows.shape
    return pl.pallas_call(
        atom_input_kernel,
        out_shape=[
            jax.ShapeDtypeStruct(rows.shape, f32),
            jax.ShapeDtypeStruct((width, 4 * width), f32),
        ],
        grid=(samples,),
        in_specs=[per_sample(part.shape[1:]) for part in (rows, mix, own, left, right, midgrad)]
        + [whole(wide.shape)],
        out_specs=[per_sample((slots, width)), whole((width, 4 * width))],
        compiler_params=params(),
        name="atom_input_backward",
    )(rows, mix, own, left, right, midgrad, wide)


def row_stats(pairs, ones_op, weights):
    count = weights.shape[0]
    both = mm_nt(jnp.concatenate([weights, ones_op], 0), pairs)
    upper, lower = square_sums(ones_op, pairs.astype(f32) * pairs.astype(f32))
    features = pairs.shape[1]
    mean = both[count : count + 1] * (1.0 / features)
    square = (mm_nt(ones_op, upper) + mm_nt(ones_op, lower))[:1] * (1.0 / features)
    var = jnp.maximum(square - mean * mean, 0.0)
    return both[:count], mean, lax.rsqrt(var + norm_eps)


def pair_bias_kernel(pair_ref, weight_ref, bias_ref):
    weights = weight_ref[...]
    ones_op = jnp.ones((16, weights.shape[1]), bf16)
    weight_sum = jnp.sum(weights.astype(f32), -1, keepdims=True)
    for row in range(pair_ref.shape[0]):
        product, mean, inv_std = row_stats(pair_ref[row], ones_op, weights)
        bias_ref[:, row, :] = inv_std * (product - mean * weight_sum)


def pair_bias(pairs, weights):
    rows, keys, features = pairs.shape
    heads = weights.shape[0]
    return pl.pallas_call(
        pair_bias_kernel,
        out_shape=jax.ShapeDtypeStruct((heads, rows, keys), f32),
        grid=(rows // 8,),
        in_specs=[pl.BlockSpec((8, keys, features), lambda i: (i, 0, 0)), whole(weights.shape)],
        out_specs=pl.BlockSpec((heads, 8, keys), lambda i: (0, i, 0)),
        compiler_params=params(),
        name="pair_bias",
    )(pairs, weights)


def pair_grad_kernel(pair_ref, grad_ref, weight_ref, total_ref, mean_ref):
    @pl.when(pl.program_id(0) == 0)
    def _():
        total_ref[...] = jnp.zeros_like(total_ref)
        mean_ref[...] = jnp.zeros_like(mean_ref)

    heads = grad_ref.shape[0]
    ones_op = jnp.ones((16, pair_ref.shape[2]), bf16)
    total = jnp.zeros(total_ref.shape, f32)
    means = jnp.zeros(mean_ref.shape, f32)
    for row in range(pair_ref.shape[0]):
        pairs = pair_ref[row]
        _, mean, inv_std = row_stats(pairs, ones_op, weight_ref[...])
        scaled = grad_ref[:, row, :] * inv_std
        means += scaled * mean
        upper = scaled.astype(bf16)
        lower = (scaled - upper.astype(f32)).astype(bf16)
        both = mm(jnp.concatenate([upper, lower], 0), pairs)
        total += both[:heads] + both[heads:]
    total_ref[...] += total
    mean_ref[...] += means


def pair_grad(pairs, grads, weights):
    rows, keys, features = pairs.shape
    heads = grads.shape[0]
    total, means = pl.pallas_call(
        pair_grad_kernel,
        out_shape=[
            jax.ShapeDtypeStruct((heads, features), f32),
            jax.ShapeDtypeStruct((heads, keys), f32),
        ],
        grid=(rows // 8,),
        in_specs=[
            pl.BlockSpec((8, keys, features), lambda i: (i, 0, 0)),
            pl.BlockSpec((heads, 8, keys), lambda i: (0, i, 0)),
            whole(weights.shape),
        ],
        out_specs=[whole((heads, features)), whole((heads, keys))],
        compiler_params=params(),
        name="pair_grad",
    )(pairs, grads, weights)
    return total - jnp.sum(means, -1, keepdims=True)


def head_groups(width, heads):
    head_dim = width // heads
    groups = []
    for head in range(0, heads, 4):
        low = head * head_dim
        base = low // LANES * LANES
        groups.append((head, base, low - base))
    return head_dim, groups


def token_fwd_kernel(query_ref, keyval_ref, bias_ref, attend_ref, probs_ref, fold_s):
    tokens, width = query_ref.shape[1:]
    heads = bias_ref.shape[0]
    keys = bias_ref.shape[2]
    head_dim, groups = head_groups(width, heads)
    scale = float(head_dim) ** (-0.5)
    fold_s[...] = jnp.zeros_like(fold_s)
    for head, base, first in groups:
        span = slice(base, base + 256)
        key_rows = keyval_ref[:, 0, :, base : base + 256].reshape(keys, 256)
        value_rows = keyval_ref[:, 0, :, width + base : width + base + 256].reshape(keys, 256)
        stacked = head_stack(query_ref[0, :, span], 4, head_dim, first)
        bias = bias_ref[head : head + 4].reshape(4 * tokens, keys)
        scores = mm_nt(stacked, key_rows) * scale + bias
        exp_scores = jnp.exp(scores - jnp.max(scores, -1, keepdims=True))
        probs = exp_scores * (1.0 / jnp.sum(exp_scores, -1, keepdims=True))
        probs_low = probs.astype(bf16)
        probs_ref[0, head : head + 4] = probs_low.reshape(4, tokens, keys)
        fold_s[:, span] += head_fold(mm(probs_low, value_rows), 4, head_dim, first)
    attend_ref[0] = fold_s[...]


def token_attention(query, keyval, bias):
    samples, tokens, width = query.shape
    heads, _, keys = bias.shape
    devices = keyval.shape[0]
    return pl.pallas_call(
        token_fwd_kernel,
        out_shape=[
            jax.ShapeDtypeStruct(query.shape, f32),
            jax.ShapeDtypeStruct((samples, heads, tokens, keys), bf16),
        ],
        grid=(samples,),
        in_specs=[
            per_sample((tokens, width)),
            pl.BlockSpec((devices, 1, tokens, 2 * width), lambda b: (0, b, 0, 0)),
            whole(bias.shape),
        ],
        out_specs=[per_sample((tokens, width)), per_sample((heads, tokens, keys))],
        scratch_shapes=[pltpu.VMEM((tokens, width), f32)],
        compiler_params=params(),
        name="token_attention",
    )(query, keyval, bias)


def token_bwd_kernel(
    query_ref, keyval_ref, probs_ref, att_ref, dq_ref, dkv_ref, bias_ref, fold_s, grad_s
):
    tokens, width = query_ref.shape[1:]
    heads, _, keys = bias_ref.shape
    devices = keyval_ref.shape[0]
    head_dim, groups = head_groups(width, heads)
    scale = float(head_dim) ** (-0.5)

    @pl.when(pl.program_id(0) == 0)
    def _():
        bias_ref[...] = jnp.zeros_like(bias_ref)

    fold_s[...] = jnp.zeros_like(fold_s)
    grad_s[...] = jnp.zeros_like(grad_s)
    for head, base, first in groups:
        span = slice(base, base + 256)
        key_rows = keyval_ref[:, 0, :, base : base + 256].reshape(keys, 256)
        value_rows = keyval_ref[:, 0, :, width + base : width + base + 256].reshape(keys, 256)
        queries = head_stack(query_ref[0, :, span], 4, head_dim, first)
        att = head_stack(att_ref[0, :, span], 4, head_dim, first)
        probs_low = probs_ref[0, head : head + 4].reshape(4 * tokens, keys)
        probs = probs_low.astype(f32)
        prob_grad = mm_nt(att, value_rows)
        delta = jnp.sum(prob_grad * probs, -1, keepdims=True)
        score_low = (probs * (prob_grad - delta)).astype(bf16)
        bias_ref[head : head + 4] += score_low.astype(f32).reshape(4, tokens, keys)
        fold_s[:, span] += head_fold(mm(score_low, key_rows), 4, head_dim, first) * scale
        grad_s[:, span] += mm_tn(score_low, queries) * scale
        grad_s[:, width + base : width + base + 256] += mm_tn(probs_low, att)
    dq_ref[0] = fold_s[...]
    dkv_ref[:, 0] = grad_s[...].astype(bf16).reshape(devices, tokens, 2 * width)


def token_attention_back(query, keyval, probs, att):
    samples, tokens, width = query.shape
    heads, _, keys = probs.shape[1:]
    devices = keyval.shape[0]
    return pl.pallas_call(
        token_bwd_kernel,
        out_shape=[
            jax.ShapeDtypeStruct(query.shape, f32),
            jax.ShapeDtypeStruct(keyval.shape, bf16),
            jax.ShapeDtypeStruct((heads, tokens, keys), f32),
        ],
        grid=(samples,),
        in_specs=[
            per_sample((tokens, width)),
            pl.BlockSpec((devices, 1, tokens, 2 * width), lambda b: (0, b, 0, 0)),
            per_sample((heads, tokens, keys)),
            per_sample((tokens, width)),
        ],
        out_specs=[
            per_sample((tokens, width)),
            pl.BlockSpec((devices, 1, tokens, 2 * width), lambda b: (0, b, 0, 0)),
            whole((heads, tokens, keys)),
        ],
        scratch_shapes=[
            pltpu.VMEM((tokens, width), f32),
            pltpu.VMEM((keys, 2 * width), f32),
        ],
        compiler_params=params(),
        name="token_attention_back",
    )(query, keyval, probs, att)


def to_blocks(array, width):
    return [array[:, low : low + width] for low in range(0, array.shape[1], width)]


def pack_blocks(arrays, width):
    parts = []
    for array in arrays:
        parts += to_blocks(array, width)
    return jnp.concatenate(parts, 0)


def unpack_blocks(packed, shapes, width):
    arrays, low = [], 0
    for rows, columns in shapes:
        parts = []
        for _ in range(columns // width):
            parts.append(packed[low : low + rows])
            low += rows
        arrays.append(jnp.concatenate(parts, 1) if len(parts) > 1 else parts[0])
    return arrays


def sum_shares(grads, extra):
    samp, seq = lax.axis_size("samp"), lax.axis_size("seq")
    width = grads[2].shape[1]
    shapes = [(grad.shape[0] // samp, grad.shape[1]) for grad in grads]
    packed = jnp.concatenate(
        [
            block.astype(bf16).reshape(samp, -1, width)
            for grad in grads
            for block in to_blocks(grad, width)
        ]
        + [extra.astype(bf16).reshape(samp, -1, width)],
        1,
    )
    rows = packed.shape[1]
    packed = packed.reshape(samp, seq, rows // seq, width).transpose(1, 0, 2, 3)
    part = lax.psum_scatter(packed, "seq", scatter_dimension=0, tiled=False)
    part = lax.psum_scatter(part, "samp", scatter_dimension=0, tiled=False)
    packed = lax.all_gather(part, "seq", axis=0, tiled=True).astype(f32)
    shares = unpack_blocks(packed, shapes, width)
    return shares, packed[sum(r * (c // width) for r, c in shapes) :]


def local(
    atom_input,
    token_input,
    atom_counts,
    key_offsets,
    atom_pairs,
    pair_features,
    single_features,
    noise_levels,
    noise_direction,
    atom_proj,
    atom_qbias,
    atom_pairw,
    atom_outw,
    atom_upw,
    atom_downw,
    pool_weight,
    cond_weight,
    cond_bias,
    token_proj,
    token_qbias,
    token_pairw,
    token_outw,
    token_upw,
    token_downw,
    cotangent,
):
    samp, seq = lax.axis_size("samp"), lax.axis_size("seq")
    seq_pos = lax.axis_index("seq")
    samples, slots, atom_width = atom_input.shape
    tokens, width = token_input.shape[1:]
    features = atom_pairs.shape[-1]

    half = atom_downw.shape[0] // 2
    wide_own = jnp.concatenate(
        [atom_proj, atom_upw, pool_weight, atom_outw, atom_downw[:half], atom_downw[half:]], 1
    )
    tiny_own = jnp.concatenate(
        [
            atom_qbias,
            cond_bias,
            token_qbias,
            atom_pairw.reshape(-1),
            token_pairw.reshape(-1),
        ]
    )
    wide_all = lax.all_gather(wide_own, "samp", axis=0, tiled=True)
    tiny_all = lax.all_gather(tiny_own[None], "samp", axis=0, tiled=True)
    wide = wide_all[:, : -2 * atom_width]
    down = (
        wide_all[:, -2 * atom_width :]
        .reshape(samp, half, 2, atom_width)
        .transpose(0, 2, 1, 3)
        .reshape(-1, atom_width)
    )
    sizes = [atom_qbias.size, cond_bias.size, token_qbias.size, atom_pairw.size, token_pairw.size]
    cuts = [sum(sizes[:i]) for i in range(6)]
    tiny = [tiny_all[:, cuts[i] : cuts[i + 1]] for i in range(5)]
    atom_qb = tiny[0].reshape(1, -1).astype(f32)
    cond_b = tiny[1].reshape(-1)
    token_qb = tiny[2].reshape(-1)
    atom_pw = tiny[3].reshape(features, ATOM_HEADS)
    token_pw = tiny[4].reshape(-1, token_pairw.shape[1])

    cond_w = lax.all_gather(cond_weight, "samp", axis=0, tiled=True)
    proj_w = lax.all_gather(token_proj, "samp", axis=0, tiled=True)
    out_w = lax.all_gather(token_outw, "samp", axis=0, tiled=True)
    up_w = lax.all_gather(token_upw, "samp", axis=0, tiled=True)
    down_w = lax.all_gather(token_downw, "samp", axis=0, tiled=True)

    up_pairs = [(i, i + 1) for i in range(seq - 1)]
    down_pairs = [(i + 1, i) for i in range(seq - 1)]
    before = lax.ppermute(atom_input[:, slots - RIM :], "seq", up_pairs)
    after = lax.ppermute(atom_input[:, :RIM], "seq", down_pairs)
    ext = jnp.concatenate([before, atom_input, after], 1)
    rim_tokens = RIM // MAX_ATOMS
    counts = lax.dynamic_slice_in_dim(
        jnp.pad(atom_counts, (rim_tokens, rim_tokens)), seq_pos * tokens, tokens + 2 * rim_tokens
    )
    place = jnp.arange(MAX_ATOMS, dtype=jnp.int32)
    used = place[None, :] < counts[:, None]
    blocked = jnp.where(used, 0.0, masked_score).astype(f32).reshape(-1, 1)
    blocked = jnp.broadcast_to(blocked, (blocked.shape[0], LANES))
    own_counts = counts[rim_tokens : rim_tokens + tokens]
    share = used[rim_tokens : rim_tokens + tokens].astype(f32) / own_counts[:, None].astype(f32)
    share = jnp.broadcast_to(share.reshape(-1, 1), (slots, LANES))
    windows = slots // WIN_Q
    starts = jnp.arange(windows, dtype=jnp.int32) * WIN_Q + key_offsets + RIM
    pairs_t = atom_pairs.transpose(0, 1, 3, 2).reshape(windows, WIN_Q * features, WIN_K)
    eye = jnp.eye(WIN_Q, dtype=bool)
    spread = jnp.where(
        eye[None, :, :, None], atom_pw.T[:, None, None, :], jnp.zeros((), bf16)
    ).reshape(ATOM_HEADS * WIN_Q, WIN_Q * features)
    pooled, *stored = atom_forward(
        ext, starts, pairs_t, spread, blocked, share, wide, down, atom_qb
    )
    block_in = token_input.astype(f32) + pooled

    noise_feature = 0.25 * jnp.log(noise_levels / sigma_data)
    cond_rows = (
        single_features.astype(f32)[None]
        + noise_feature[:, None, None] * noise_direction[None, None, :]
    )
    cond_low = norm_stats(cond_rows)[0].astype(bf16)
    cond_all = dot_last(cond_low, cond_w) + cond_b.astype(f32)
    parts = [cond_all[..., i * width : (i + 1) * width] for i in range(6)]

    pair_w = token_pw.T
    bias = pair_bias(pair_features, pair_w)
    normed_in, inv_in = norm_stats(block_in)
    attn_in = (jax.nn.sigmoid(parts[0]) * normed_in + parts[1]).astype(bf16)
    mix = dot_last(attn_in, proj_w)
    queries = (mix[..., :width] + token_qb.astype(f32)).astype(bf16)
    keyval_own = mix[..., width : 3 * width].astype(bf16)
    gating = mix[..., 3 * width :]
    keyval = lax.all_gather(keyval_own, "seq", axis=0, tiled=False)
    attend, probs = token_attention(queries, keyval, bias)
    sig_gate = jax.nn.sigmoid(gating)
    gated_low = (attend * sig_gate).astype(bf16)
    branch = dot_last(gated_low, out_w)
    gate_one = jax.nn.sigmoid(parts[2])
    mid = block_in + gate_one * branch
    normed_mid, inv_mid = norm_stats(mid)
    scale_two = jax.nn.sigmoid(parts[3])
    ffn_in = (scale_two * normed_mid + parts[4]).astype(bf16)
    upper = dot_last(ffn_in, up_w)
    hidden_width = down_w.shape[0]
    first_half, second_half = upper[..., :hidden_width], upper[..., hidden_width:]
    sig_first = jax.nn.sigmoid(first_half)
    hidden = (first_half * sig_first * second_half).astype(bf16)
    branch_two = dot_last(hidden, down_w)
    gate_two = jax.nn.sigmoid(parts[5])
    block_out = (mid + gate_two * branch_two).astype(bf16)

    out_grad = cotangent.astype(f32)
    branch_two_low = (out_grad * gate_two).astype(bf16)
    gate_two_grad = out_grad * branch_two * gate_two * (1.0 - gate_two)
    hidden_grad = dot_back(branch_two_low, down_w)
    first_grad = hidden_grad * second_half * sig_first * (1.0 + first_half * (1.0 - sig_first))
    second_grad = hidden_grad * first_half * sig_first
    upper_grad = jnp.concatenate([first_grad, second_grad], -1).astype(bf16)
    ffn_grad = dot_back(upper_grad, up_w)
    scale_two_grad = ffn_grad * normed_mid * scale_two * (1.0 - scale_two)
    mid_grad = out_grad + norm_back(normed_mid, inv_mid, ffn_grad * scale_two)
    branch_low = (mid_grad * gate_one).astype(bf16)
    gate_one_grad = mid_grad * branch * gate_one * (1.0 - gate_one)
    gated_grad = dot_back(branch_low, out_w)
    attend_low = (gated_grad * sig_gate).astype(bf16)
    gating_grad = gated_grad * attend * sig_gate * (1.0 - sig_gate)
    query_grad, keyval_part, bias_grad = token_attention_back(queries, keyval, probs, attend_low)
    keyval_grad = lax.psum_scatter(keyval_part, "seq", scatter_dimension=0, tiled=False)
    pairw_grad = pair_grad(pair_features, bias_grad, pair_w).T
    mix_grad = jnp.concatenate(
        [query_grad.astype(bf16), keyval_grad, gating_grad.astype(bf16)], -1
    )
    token_qb_grad = jnp.sum(query_grad, (0, 1))
    attn_in_grad = dot_back(mix_grad, proj_w)
    scale_one = jax.nn.sigmoid(parts[0])
    scale_one_grad = attn_in_grad * normed_in * scale_one * (1.0 - scale_one)
    token_grad = mid_grad + norm_back(normed_in, inv_in, attn_in_grad * scale_one)
    cond_grad = jnp.concatenate(
        [scale_one_grad, attn_in_grad, gate_one_grad, scale_two_grad, ffn_grad, gate_two_grad], -1
    ).astype(bf16)
    cond_b_grad = jnp.sum(cond_grad.astype(f32), (0, 1))

    mix_part, own, left, right, atom_mid_grad, *atom_totals = atom_backward(
        token_grad, starts, stored, pairs_t, share, wide, down
    )
    from_right = lax.ppermute(left, "seq", down_pairs)
    from_left = lax.ppermute(right, "seq", up_pairs)
    atom_grad, atom_proj_grad = atom_input_backward(
        atom_input, mix_part, own, from_left, from_right, atom_mid_grad, wide
    )
    qb_grad, outw_grad, upw_grad, downw_grad, pool_grad, pairw_stack, pairw_mean = atom_totals
    diagonal = pairw_stack.reshape(ATOM_HEADS, WIN_Q, WIN_Q, features)
    atom_pw_grad = (
        jnp.sum(jnp.where(eye[None, :, :, None], diagonal, 0.0), (1, 2)).T
        - jnp.sum(pairw_mean.reshape(ATOM_HEADS, -1), 1)[None, :]
    )

    grads = [
        weight_grad(hidden, branch_two_low),
        weight_grad(attn_in, mix_grad),
        weight_grad(gated_low, branch_low),
        weight_grad(ffn_in, upper_grad),
        weight_grad(cond_low, cond_grad),
    ]
    small = [
        atom_proj_grad,
        qb_grad.reshape(-1),
        atom_pw_grad,
        outw_grad,
        upw_grad,
        downw_grad,
        pool_grad,
        cond_b_grad,
        token_qb_grad,
        pairw_grad,
    ]
    flat = jnp.concatenate([part.reshape(samp, -1) for part in small], 1)
    unit = 16 * seq * width
    flat = jnp.pad(flat, ((0, 0), (0, -flat.shape[1] % unit))).reshape(-1, width)
    shares, rest = sum_shares(grads, flat)
    rest = rest.reshape(-1)
    out, low = [], 0
    for part in small:
        size = part.size // samp
        out.append(rest[low : low + size].reshape((part.shape[0] // samp,) + part.shape[1:]))
        low += size
    return (
        block_out,
        atom_grad,
        token_grad,
        out[0],
        out[1],
        out[2],
        out[3],
        out[4],
        out[5],
        out[6],
        shares[4],
        out[7],
        shares[1],
        out[8],
        out[9],
        shares[2],
        shares[3],
        shares[0],
    )


def solution(mesh):
    in_specs = (
        P("samp", "seq", None),
        P("samp", "seq", None),
        P(),
        P("seq"),
        P("seq", None, None, None),
        P("seq", None, None),
        P("seq", None),
        P("samp"),
        P(),
        P("samp", None),
        P("samp"),
        P("samp", None),
        P("samp", None),
        P("samp", None),
        P("samp", None),
        P("samp", None),
        P("samp", None),
        P("samp"),
        P("samp", None),
        P("samp"),
        P("samp", None),
        P("samp", None),
        P("samp", None),
        P("samp", None),
        P("samp", "seq", None),
    )
    out_specs = (
        P("samp", "seq", None),
        P("samp", "seq", None),
        P("samp", "seq", None),
        P("samp", None),
        P("samp"),
        P("samp", None),
        P("samp", None),
        P("samp", None),
        P("samp", None),
        P("samp", None),
        P("samp", None),
        P("samp"),
        P("samp", None),
        P("samp"),
        P("samp", None),
        P("samp", None),
        P("samp", None),
        P("samp", None),
    )
    return jax.shard_map(local, mesh=mesh, in_specs=in_specs, out_specs=out_specs, check_vma=False)
```

profile of v0, /device:TPU:0, one launch (start us, length us, event | category | flops | bytes accessed | tf_op | source)
XLA Modules:
  0.0 1092.7 jit_solution(2121543622360988385)
XLA Ops:
  10.2 3.0 collective-permute-start
  13.4 24.2 %all_gather.31 = bf16[128,2176]{1,0:T(8,128)(2,1)S(1)} all-gather(bf16[32,2176]{1,0:T(8,128)(2,1)S(1)} %constant_dynamic-update-slice_fusion), channel_id=1, replica_groups=mesh['samp'=4,'seq'=8] {'samp'}, dimensions={0}, use_global_device_ids=true | all-gather | bytes 696320 | tf_op jit(solution)/shard_map/all_gather | solution.py:799
  40.4 19.8 %all-reduce.2 = bf16[7616]{0:T(1024)(128)(2,1)S(1)} all-reduce(bf16[7616]{0:T(1024)(128)(2,1)S(1)} %dynamic-update-slice), channel_id=2, replica_groups=mesh['samp'=4,'seq'=8] {'samp'}, use_global_device_ids=true, to_apply=%add.2 | all-reduce | flops 7616 | bytes 30464
  67.9 70.2 %atom_forward.1 = (f32[8,64,768]{2,1,0:T(8,128)}, bf16[8,512,128]{2,1,0:T(8,128)(2,1)}, bf16[8,704,256]{2,1,0:T(8,128)(2,1)}, f32[8,512,128]{2,1,0:T(8,128)}, bf...) custom-call(s32[16]{0:T(128)} %add_add_fusion.starts, ...), custom_call_target="tpu_custom_call" | custom-call | tf_op jit(solution)/shard_map/atom_forward/pallas_call | solution.py:244
  140.1 4.7 convolution_add_fusion
  144.8 3.5 copy-done.3
  148.9 29.7 %all-gather.13.cloned.1.call-done = bf16[768,3072]{1,0:T(8,128)(2,1)} async-done(((bf16[192,3072]{1,0:T(8,128)(2,1)}), bf16[768,3072]{1,0:T(8,128)(2,1)}) %all-gather.13.cloned.1.call-update) | async-done | bytes 4718608 | tf_op jit(solution)/shard_map/all_gather | solution.py:818
  178.6 4.5 fusion.7
  183.1 2.6 copy-done.2
  190.0 11.7 %pair_bias.1.bias_ref = f32[16,64,512]{2,1,0:T(8,128)} custom-call(bf16[64,512,128]{2,1,0:T(8,128)(2,1)} %pair_ref.3, bf16[16,128]{1,0:T(8,128)(2,1)} %bitcast.182), custom_call_target="tpu_custom_call" | custom-call | tf_op jit(solution)/shard_map/pair_bias/pallas_call | solution.py:532
  201.7 2.4 fusion.28.query_ref
  204.1 53.7 %all-gather.21.cloned.1.call-done = bf16[64,64,1536]{2,1,0:T(8,128)(2,1)} async-done(((bf16[8,64,1536]{2,1,0:T(8,128)(2,1)}), bf16[64,64,1536]{2,1,0:T(8,128)(2,1)}) %all-gather.21.cloned.1.call-update) | async-done | bytes 12582928 | tf_op jit(solution)/shard_map/all_gather | solution.py:868
  257.9 15.4 %token_attention.1 = (f32[8,64,768]{2,1,0:T(8,128)}, bf16[8,16,64,512]{3,2,1,0:T(8,128)(2,1)}) custom-call(bf16[8,64,768]{2,1,0:T(8,128)(2,1)} %fusion.28.query_ref, bf16[8,8,64,1536]{3,2,1,0:T(8,128)(2,1)} %bitcast.155, f32[16,64,512]{2,1,0:T(8,128)} %pair_bias.1.bias_ref), custom_call_target="tpu_custom_call" | custom-call | tf_op jit(solution)/shard_map/token_attention/pallas_call | solution.py:624
  273.3 3.2 multiply_convert_fusion.9
  276.4 13.3 %all-gather.15.cloned.1.call-done = bf16[768,768]{1,0:T(8,128)(2,1)} async-done(((bf16[192,768]{1,0:T(8,128)(2,1)}), bf16[768,768]{1,0:T(8,128)(2,1)}) %all-gather.15.cloned.1.call-update) | async-done | bytes 1179664 | tf_op jit(solution)/shard_map/all_gather | solution.py:819
  289.8 4.0 fusion.80
  294.0 3.3 fusion.18
  297.3 82.5 %all-gather.17.cloned.1.call-done = bf16[768,3072]{1,0:T(8,128)(2,1)} async-done(((bf16[192,3072]{1,0:T(8,128)(2,1)}), bf16[768,3072]{1,0:T(8,128)(2,1)}) %all-gather.17.cloned.1.call-update) | async-done | bytes 4718608 | tf_op jit(solution)/shard_map/all_gather | solution.py:820
  379.8 7.9 fusion.3
  387.7 42.5 %all-gather.19.cloned.1.call-done = bf16[1536,768]{1,0:T(8,128)(2,1)} async-done(((bf16[384,768]{1,0:T(8,128)(2,1)}), bf16[1536,768]{1,0:T(8,128)(2,1)}) %all-gather.19.cloned.1.call-update) | async-done | bytes 2359312 | tf_op jit(solution)/shard_map/all_gather | solution.py:821
  430.2 6.9 multiply_convert_fusion.1
  437.2 6.0 fusion.77
  443.3 5.5 multiply_convert_fusion.8
  448.8 3.9 multiply_convert_fusion.7
  452.7 23.0 %token_attention_back.1 = (f32[8,64,768]{2,1,0:T(8,128)}, bf16[8,8,64,1536]{3,2,1,0:T(8,128)(2,1)}, f32[16,64,512]{2,1,0:T(8,128)}) custom-call(bf16[8,64,768]{2,1,0:T(8,128)(2,1)} %fusion.28.query_ref, bf16[8,8,64,1536]{3,2,1,0:T(8,128)(2,1)} %bitcast.156, bf16[8,16,64,512]{3,2,1,0:T(8,128)(2,1)} %get-tuple-element.48.probs_ref, ...), custom_call_target="tpu_custom_call" | custom-call | tf_op jit(solution)/shard_map/token_attention_back/pallas_call | solution.py:681
  475.8 3.0 fusion.85
  478.9 19.6 %pair_grad.1 = (f32[16,128]{1,0:T(8,128)}, f32[16,512]{1,0:T(8,128)}) custom-call(bf16[64,512,128]{2,1,0:T(8,128)(2,1)} %pair_ref.3, f32[16,64,512]{2,1,0:T(8,128)} %get-tuple-element.71.grad_ref, bf16[16,128]{1,0:T(8,128)(2,1)} %bitcast.183), custom_call_target="tpu_custom_call" | custom-call | tf_op jit(solution)/shard_map/pair_grad/pallas_call | solution.py:569
  500.3 3.6 bitcast_convert_fusion.2
  508.7 3.0 bitcast_convert_fusion
  511.7 2.3 fusion.82
  514.0 53.2 %reduce-scatter.6.cloned.1.call-done = bf16[1,8,64,1536]{3,2,1,0:T(8,128)(2,1)} async-done(((bf16[8,8,64,1536]{3,2,1,0:T(8,128)(2,1)}), bf16[1,8,64,1536]{3,2,1,0:T(8,128)(2,1)}) %reduce-scatter.6.cloned.1.call-update) | async-done | bytes 1572880 | tf_op jit(solution)/shard_map/reduce_scatter | solution.py:903
  567.2 7.0 bitcast_convert_fusion.1
  574.2 5.9 fusion.76
  582.1 75.7 %atom_backward.1 = (bf16[8,512,256]{2,1,0:T(8,128)(2,1)}, f32[8,512,256]{2,1,0:T(8,128)}, bf16[8,96,256]{2,1,0:T(8,128)(2,1)}, bf16[8,96,256]{2,1,0:T(8,128)(2,1...) custom-call(s32[16]{0:T(128)} %add_add_fusion.starts, ...), custom_call_target="tpu_custom_call" | custom-call | tf_op jit(solution)/shard_map/atom_backward/pallas_call | solution.py:445
  657.8 2.5 collective-permute-start.2
  661.7 5.0 fusion.83
  666.6 2.6 fusion.44
  695.2 3.4 reduce.2
  702.3 10.3 atom_input_backward.1
  723.3 223.8 %all-reduce.6.cloned.1.call-done = bf16[8,4,352,768]{3,2,0,1:T(8,128)(2,1)} async-done(((bf16[8,4,352,768]{3,2,0,1:T(8,128)(2,1)}), bf16[8,4,352,768]{3,2,0,1:T(8,128)(2,1)}) %all-reduce.6.cloned.1.call-update) | async-done | bytes 17301520
  947.1 3.7 dynamic-slice_bitcast_fusion
  950.9 45.1 %reduce-scatter.8.cloned.1.call-done = bf16[1,352,768]{2,1,0:T(8,128)(2,1)} async-done(((bf16[4,352,768]{2,1,0:T(8,128)(2,1)}), bf16[1,352,768]{2,1,0:T(8,128)(2,1)}) %reduce-scatter.8.cloned.1.call-update) | async-done | bytes 540688 | tf_op jit(solution)/shard_map/reduce_scatter | solution.py:747
  996.1 38.5 %all-gather.23.cloned.1.call-done = bf16[1,2816,768]{2,1,0:T(8,128)(2,1)} async-done(((bf16[1,352,768]{2,1,0:T(8,128)(2,1)}), bf16[1,2816,768]{2,1,0:T(8,128)(2,1)}) %all-gather.23.cloned.1.call-update) | async-done | bytes 4325392 | tf_op jit(solution)/shard_map/all_gather | solution.py:748
  1036.5 14.8 %slice.261 = f32[24576,4]{1,0:T(8,128)} reshape(f32[1,128,768]{2,1,0:T(8,128)S(1)} %slice.337) | data formatting | bytes 786432 | tf_op jit(solution)/shard_map/slice | solution.py:960
  1055.2 2.9 convert_element_type.144
  1058.9 2.8 slice_bitcast_fusion.4
  1064.9 2.4 slice_bitcast_fusion
  1080.5 3.4 pad_maximum_fusion.2
  (334 shorter events, 94.5 us)
Async XLA Ops:
  7.2 6.0 copy-start.48
  7.2 6.1 copy-start.49
  7.2 6.1 copy-start.46
  7.2 6.1 copy-start.51
  7.2 6.1 copy-start.50
  7.3 132.9 %all-gather.11.cloned.1.call-start = ((), (), s32[]{:S(2)}) async-start(), calls=%async_computation.2 | async-start | bytes 4423680 | tf_op jit(solution)/shard_map/all_gather | solution.py:817
  8.0 170.6 %all-gather.13.cloned.1.call-start = ((), (), s32[]{:S(2)}) async-start(), calls=%async_computation.3 | async-start | bytes 5898240 | tf_op jit(solution)/shard_map/all_gather | solution.py:818
  8.7 29.7 %copy-start.61 = (bf16[4,4]{1,0:T(4,128)(2,1)S(1)}, bf16[4,4]{1,0:T(4,128)(2,1)}, u32[]{:S(2)}) copy-start(bf16[4,4]{1,0:T(4,128)(2,1)} %param.36) | copy-start | bytes 100
  8.7 29.8 %copy-start.52 = (bf16[32,16]{0,1:T(8,128)(2,1)S(1)}, bf16[32,16]{0,1:T(8,128)(2,1)}, u32[]{:S(2)}) copy-start(bf16[32,16]{0,1:T(8,128)(2,1)} %param.45) | copy-start | bytes 3076
  8.8 30.0 %copy-start.66 = (u32[32]{0:T(128)S(1)}, u32[32]{0:T(128)}, u32[]{:S(2)}) copy-start(u32[32]{0:T(128)} %constant.53) | copy-start | bytes 388
  8.8 31.2 %copy-start.53 = (bf16[1152]{0:T(1024)(128)(2,1)S(1)}, bf16[1152]{0:T(1024)(128)(2,1)}, u32[]{:S(2)}) copy-start(bf16[1152]{0:T(1024)(128)(2,1)} %param.42) | copy-start | bytes 6916
  8.8 31.2 %copy-start.56 = (bf16[32]{0:T(256)(128)(2,1)S(1)}, bf16[32]{0:T(256)(128)(2,1)}, u32[]{:S(2)}) copy-start(bf16[32]{0:T(256)(128)(2,1)} %param.35) | copy-start | bytes 196
  8.8 31.2 %copy-start.57 = (bf16[192]{0:T(256)(128)(2,1)S(1)}, bf16[192]{0:T(256)(128)(2,1)}, u32[]{:S(2)}) copy-start(bf16[192]{0:T(256)(128)(2,1)} %param.44) | copy-start | bytes 1156
  8.8 249.1 %all-gather.21.cloned.1.call-start = ((), (), s32[]{:S(2)}) async-start(), calls=%async_computation.9 | async-start | bytes 14155776 | tf_op jit(solution)/shard_map/all_gather | solution.py:868
  8.9 56.0 %collective-permute-start.1 = (bf16[8,96,128]{2,1,0:T(8,128)(2,1)S(1)}, bf16[8,96,128]{2,1,0:T(8,128)(2,1)S(1)}, u32[]{:S(2)}, u32[]{:S(2)}) collective-permute-start(bf16[8,96,128]{2,1,0:T(8,128)(2,1)S(1)} %get-tuple-element.153), channel_id=1, source_target_pairs={{1,0},{2,1},{3,2},{4,3},{5,4},{6,5},{7,6},{9,8},{10,9},{11,10},{12... | collective-permute-start | bytes 589832 | tf_op jit(solution)/shard_map/ppermute | solution.py:826
  10.2 54.7 %collective-permute-start = (bf16[8,96,128]{2,1,0:T(8,128)(2,1)S(1)}, bf16[8,96,128]{2,1,0:T(8,128)(2,1)S(1)}, u32[]{:S(2)}, u32[]{:S(2)}) collective-permute-start(bf16[8,96,128]{2,1,0:T(8,128)(2,1)S(1)} %get-tuple-element.152), channel_id=1, source_target_pairs={{0,1},{1,2},{2,3},{3,4},{4,5},{5,6},{6,7},{8,9},{9,10},{10,11},{11... | collective-permute-start | bytes 589832 | tf_op jit(solution)/shard_map/ppermute | solution.py:825
  13.4 48.5 %copy-start.54 = (s32[512]{0:T(512)S(1)}, s32[512]{0:T(512)}, u32[]{:S(2)}) copy-start(s32[512]{0:T(512)} %param.27) | copy-start | bytes 6148
  37.6 26.2 %copy-start.47 = (bf16[64,384]{1,0:T(8,128)(2,1)S(1)}, bf16[64,384]{1,0:T(8,128)(2,1)}, u32[]{:S(2)}) copy-start(bf16[64,384]{1,0:T(8,128)(2,1)} %param.31) | copy-start | bytes 147460
  37.6 26.2 %copy-start.62 = (f32[8]{0:T(128)S(1)}, f32[8]{0:T(128)}, u32[]{:S(2)}) copy-start(f32[8]{0:T(128)} %param.32) | copy-start | bytes 100
  37.6 26.3 %copy-start.55 = (f32[384]{0:T(512)S(1)}, f32[384]{0:T(512)}, u32[]{:S(2)}) copy-start(f32[384]{0:T(512)} %param.33) | copy-start | bytes 4612
  38.5 25.9 %copy-start.63 = (s32[16]{0:T(128)S(1)}, s32[16]{0:T(128)}, u32[]{:S(2)}) copy-start(s32[16]{0:T(128)} %param.28) | copy-start | bytes 196
  67.9 70.3 %copy-start.35 = (bf16[8,64,768]{2,1,0:T(8,128)(2,1)S(1)}, bf16[8,64,768]{2,1,0:T(8,128)(2,1)}, u32[]{:S(2)}) copy-start(bf16[8,64,768]{2,1,0:T(8,128)(2,1)} %param.26) | copy-start | bytes 2359300
  148.9 34.2 %copy-start.19 = (bf16[8,64,768]{2,1,0:T(8,128)(2,1)}, bf16[8,64,768]{2,1,0:T(8,128)(2,1)S(1)}, u32[]{:S(2)}) copy-start(bf16[8,64,768]{2,1,0:T(8,128)(2,1)S(1)} %fusion.29) | copy-start | bytes 2359300
  187.1 102.7 %all-gather.15.cloned.1.call-start = ((), (), s32[]{:S(2)}) async-start(), calls=%async_computation.4 | async-start | bytes 1474560 | tf_op jit(solution)/shard_map/all_gather | solution.py:819
  187.6 192.2 %all-gather.17.cloned.1.call-start = ((), (), s32[]{:S(2)}) async-start(), calls=%async_computation.5 | async-start | bytes 5898240 | tf_op jit(solution)/shard_map/all_gather | solution.py:820
  188.2 242.0 %all-gather.19.cloned.1.call-start = ((), (), s32[]{:S(2)}) async-start(), calls=%async_computation.6 | async-start | bytes 2949120 | tf_op jit(solution)/shard_map/all_gather | solution.py:821
  188.8 378.4 %reduce-scatter.6.cloned.1.call-start = ((), (), s32[]{:S(2)}) async-start(), calls=%async_computation.7 | async-start | bytes 14155776 | tf_op jit(solution)/shard_map/reduce_scatter | solution.py:903
  430.2 6.9 copy-start.18
  437.1 6.1 copy-start.67
  437.1 6.1 copy-start.69
  437.1 6.1 copy-start.74
  437.2 6.1 copy-start.4
  437.2 6.1 copy-start.58
  443.2 5.6 copy-start.7
  443.3 5.6 copy-start.32
  475.8 471.3 %all-reduce.6.cloned.1.call-start = ((), (), s32[]{:S(2)}) async-start(), calls=%async_computation.11 | async-start | bytes 34603008
  567.2 7.0 copy-start.36
  567.2 7.0 copy-start.59
  567.2 7.0 copy-start.71
  574.2 6.0 copy-start.5
  574.2 6.0 copy-start.8
  657.8 44.4 %collective-permute-start.2 = (bf16[8,96,256]{2,1,0:T(8,128)(2,1)}, bf16[8,96,256]{2,1,0:T(8,128)(2,1)}, u32[]{:S(2)}, u32[]{:S(2)}) collective-permute-start(bf16[8,96,256]{2,1,0:T(8,128)(2,1)} %get-tuple-element.59), channel_id=1, source_target_pairs={{0,1},{1,2},{2,3},{3,4},{4,5},{5,6},{6,7},{8,9},{9,10},{10,11},{11... | collective-permute-start | bytes 1179656 | tf_op jit(solution)/shard_map/ppermute | solution.py:922
  660.3 41.9 %collective-permute-start.3 = (bf16[8,96,256]{2,1,0:T(8,128)(2,1)}, bf16[8,96,256]{2,1,0:T(8,128)(2,1)}, u32[]{:S(2)}, u32[]{:S(2)}) collective-permute-start(bf16[8,96,256]{2,1,0:T(8,128)(2,1)} %get-tuple-element.60), channel_id=1, source_target_pairs={{1,0},{2,1},{3,2},{4,3},{5,4},{6,5},{7,6},{9,8},{10,9},{11,10},{12... | collective-permute-start | bytes 1179656 | tf_op jit(solution)/shard_map/ppermute | solution.py:921
  661.6 7.7 slice-start
  661.6 7.7 slice-start.1
  722.1 274.0 %reduce-scatter.8.cloned.1.call-start = ((), (), s32[]{:S(2)}) async-start(), calls=%async_computation.8 | async-start | bytes 2703360 | tf_op jit(solution)/shard_map/reduce_scatter | solution.py:747
  950.9 83.8 %all-gather.23.cloned.1.call-start = ((), (), s32[]{:S(2)}) async-start(), calls=%async_computation.10 | async-start | bytes 4866048 | tf_op jit(solution)/shard_map/all_gather | solution.py:748
  1064.9 5.8 copy-start.39
  (44 other events, 107.6 us)
Sparse Core Ops, SparseCore 0:
  9.7 78.4 all-gather.10
  89.7 88.8 all-gather.12
  187.2 70.6 all-gather.20
  259.3 30.4 all-gather.14
  291.2 88.5 all-gather.16
  381.2 48.9 all-gather.18
  475.9 91.2 reduce-scatter.5
  722.2 224.8 all-reduce.5
  951.0 45.0 reduce-scatter.7
  997.9 36.6 all-gather.22
where the time goes:
time: 1100 us; the launch traced here: 1090 us
  waiting for transfers between devices  585 us (53%)
  Pallas kernels  226 us (21%)
  local copies, waits for them, and re-layouts  106 us (10%)
  matrix products  66.9 us (6%)
  blocking collectives  44 us (4%)
  other arithmetic  39.3 us (4%)
  between operations  16.3 us (1%)
    unnamed x11, waiting for transfers between devices  227 us
    all_gather x1, waiting for transfers between devices, local(): up_w = lax.all_gather(token_upw, 'samp', axis=0, tiled=True)  82.5 us
    pallas_call x1, Pallas kernels, atom_backward(): pl.pallas_call(atom_bwd_kernel, out_shape=[jax.ShapeDtypeStruct((samples,...  75.7 us
    pallas_call x1, Pallas kernels, atom_forward(): pl.pallas_call(atom_fwd_kernel, out_shape=[jax.ShapeDtypeStruct((samples,...  70.2 us
    all_gather x1, waiting for transfers between devices, local(): keyval = lax.all_gather(keyval_own, 'seq', axis=0, tiled=False)  53.7 us
    reduce_scatter x1, waiting for transfers between devices, local(): lax.psum_scatter(keyval_part, 'seq', scatter_dimension=0, tiled=False)  53.2 us
    unnamed x197, local copies, waits for them, and re-layouts  49.1 us
    reduce_scatter x1, waiting for transfers between devices, sum_shares(): part = lax.psum_scatter(part, 'samp', scatter_dimension=0, tiled=False)  45.1 us
  transfers between devices with their start and end apart: 14, of which 9 were waited for; matrix products, arithmetic and copies ran while one was open for 8% of the time, Pallas kernels for 11%

commit v1 on v0

--- a/solution.py
+++ b/solution.py
@@ -104,6 +104,650 @@
     return total
 
 
+MESH = pl.DeviceIdType.MESH
+
+
+def places():
+    samp_pos, seq_pos = lax.axis_index("samp"), lax.axis_index("seq")
+    core, across, along = seq_pos % 2, seq_pos // 2 % 2, seq_pos // 4
+
+    def index(along, across, core):
+        return (along * 2 + across) * 2 + core
+
+    return (
+        samp_pos,
+        seq_pos,
+        index(along, across, 1 - core),
+        index(along, 1 - across, core),
+        index(1 - along, across, core),
+        index(1 - along, 1 - across, core),
+    )
+
+
+def remote(source, target, send_sem, recv_sem, device):
+    return pltpu.make_async_remote_copy(
+        src_ref=source,
+        dst_ref=target,
+        send_sem=send_sem,
+        recv_sem=recv_sem,
+        device_id=device,
+        device_id_type=MESH,
+    )
+
+
+def greet(devices):
+    barrier = pltpu.get_barrier_semaphore()
+    for device in devices:
+        pl.semaphore_signal(barrier, inc=1, device_id=device, device_id_type=MESH)
+    pl.semaphore_wait(barrier, len(devices))
+
+
+def pick(position, values):
+    chosen = values[0]
+    for index, value in enumerate(values[1:], 1):
+        chosen = jnp.where(position == index, value, chosen)
+    return chosen
+
+
+class WeightGather:
+    def __init__(self, shapes, samp, seq):
+        self.shapes, self.samp, self.seq = shapes, samp, seq
+        self.splits = [self.split(shape, seq) for shape in shapes]
+
+    @staticmethod
+    def split(shape, parts):
+        rows, columns = shape
+        for down in (1, 2, 4, 8):
+            across = parts // down
+            if rows % (16 * down) == 0 and columns % (LANES * across) == 0:
+                return (down, across)
+        return None
+
+    @staticmethod
+    def fits(shapes, samp, seq):
+        return (
+            samp == 4
+            and seq == 8
+            and len(shapes) == 5
+            and all(WeightGather.split(shape, seq) for shape in shapes)
+        )
+
+    def full_shapes(self):
+        return [(rows * self.samp, columns) for rows, columns in self.shapes]
+
+    def scratch(self):
+        count = len(self.shapes)
+        return [
+            pltpu.SemaphoreType.DMA((9, self.samp, count)),
+            pltpu.SemaphoreType.DMA((8, self.samp, count)),
+            pltpu.SemaphoreType.DMA((2, count)),
+        ] + [pltpu.VMEM(shape, bf16) for shape in self.shapes]
+
+    def params(self):
+        return pltpu.CompilerParams(
+            vmem_limit_bytes=vmem_bytes, collective_id=1, has_side_effects=True
+        )
+
+    def cell(self, ref, weight, origin, part):
+        rows, columns = self.shapes[weight]
+        down, across = self.splits[weight]
+        height, width = rows // down, columns // across
+        low = origin * rows + part // across * height
+        left = part % across * width
+        return ref.at[
+            pl.ds(pl.multiple_of(low, 16), height), pl.ds(pl.multiple_of(left, LANES), width)
+        ]
+
+    def origin(self, position, turn):
+        order = [sorted(range(self.samp), key=lambda o: (abs(o - z), o)) for z in range(self.samp)]
+        if isinstance(turn, int):
+            return pick(position, [order[z][turn] for z in range(self.samp)])
+        return pick(
+            position, [pick(turn, [order[z][t] for t in range(self.samp)]) for z in range(self.samp)]
+        )
+
+    def own_copies(self, shards, fulls, own, held, stage):
+        z = places()[0]
+        copies = []
+        for w, shard in enumerate(shards):
+            rows = self.shapes[w][0]
+            target = fulls[w].at[pl.ds(pl.multiple_of(z * rows, 16), rows), :]
+            ends = (shard, held[w]) if stage == 0 else (held[w], target)
+            copies.append(pltpu.make_async_copy(*ends, own.at[stage, w]))
+        return copies
+
+    def start(self, shards, fulls, send, recv, own, held):
+        z, me, sib, xn, yn, dg = places()
+        above, below = lax.rem(z + 1, self.samp), lax.rem(z + self.samp - 1, self.samp)
+        greet([(z, sib), (z, xn), (z, yn), (above, me), (below, me)])
+        for w, shard in enumerate(shards):
+            source = self.cell(shard, w, 0, me)
+            target = self.cell(fulls[w], w, z, me)
+
+            @pl.when(z < self.samp - 1)
+            def _():
+                remote(source, target, send.at[0, 0, w], recv.at[0, z, w], (z + 1, me)).start()
+
+            @pl.when(z > 0)
+            def _():
+                remote(source, target, send.at[1, 0, w], recv.at[0, z, w], (z - 1, me)).start()
+
+        for copy in self.own_copies(shards, fulls, own, held, 0):
+            copy.start()
+
+    def place_own(self, shards, fulls, own, held):
+        for copy in self.own_copies(shards, fulls, own, held, 0):
+            copy.wait()
+        for copy in self.own_copies(shards, fulls, own, held, 1):
+            copy.start()
+
+    def share_own(self, turn, origin, sources, fulls, send, recv):
+        z, me, sib, xn, yn, dg = places()
+        for kind, part in ((2, xn), (3, yn), (5, sib)):
+            for w, source in enumerate(sources):
+                target = self.cell(fulls[w], w, origin, me)
+                arrival = {2: 1, 3: 2, 5: 4}[kind]
+                remote(
+                    source, target, send.at[kind, turn, w], recv.at[arrival, origin, w], (z, part)
+                ).start()
+
+    def wait_cell(self, fulls, recv, kind, w, origin, part, device):
+        target = self.cell(fulls[w], w, origin, part)
+        remote(target, target, recv.at[kind, origin, w], recv.at[kind, origin, w], device).wait_recv()
+
+    def issue(self, turn, fulls, send, recv):
+        z, me, sib, xn, yn, dg = places()
+        origin = self.origin(z, turn)
+        count = len(self.shapes)
+        for w in range(count):
+            self.wait_cell(fulls, recv, 0, w, origin, me, (z, sib))
+        for w in range(count):
+            cell = self.cell(fulls[w], w, origin, me)
+
+            @pl.when((origin < z) & (z < self.samp - 1))
+            def _():
+                remote(cell, cell, send.at[0, turn, w], recv.at[0, origin, w], (z + 1, me)).start()
+
+            @pl.when((origin > z) & (z > 0))
+            def _():
+                remote(cell, cell, send.at[1, turn, w], recv.at[0, origin, w], (z - 1, me)).start()
+
+        cells = [self.cell(fulls[w], w, origin, me) for w in range(count)]
+        self.share_own(turn, origin, cells, fulls, send, recv)
+
+    def passed_on(self, w):
+        return w in (0, 3)
+
+    def finish(self, turn, fulls, send, recv):
+        z, me, sib, xn, yn, dg = places()
+        origin = self.origin(z, turn)
+        count = len(self.shapes)
+        for kind, part, other, by in ((1, xn, yn, True), (2, yn, xn, False)):
+            for w in range(count):
+                self.wait_cell(fulls, recv, kind, w, origin, part, (z, part))
+                cell = self.cell(fulls[w], w, origin, part)
+                if self.passed_on(w) == by:
+                    remote(
+                        cell, cell, send.at[4, turn, w], recv.at[3, origin, w], (z, other)
+                    ).start()
+                remote(
+                    cell, cell, send.at[5 + kind, turn, w], recv.at[4 + kind, origin, w], (z, sib)
+                ).start()
+
+    def diagonal(self, turn, fulls, send, recv):
+        z, me, sib, xn, yn, dg = places()
+        origin = self.origin(z, turn)
+        for w in range(len(self.shapes)):
+            self.wait_cell(fulls, recv, 3, w, origin, dg, (z, yn))
+            cell = self.cell(fulls[w], w, origin, dg)
+            remote(cell, cell, send.at[8, turn, w], recv.at[7, origin, w], (z, sib)).start()
+
+    def drain(self, shards, fulls, send, recv, own, held):
+        z, me, sib, xn, yn, dg = places()
+        count = len(self.shapes)
+
+        def sent(kind, turn, w):
+            cell = self.cell(fulls[w], w, 0, me)
+            remote(cell, cell, send.at[kind, turn, w], recv.at[0, 0, w], (z, sib)).wait_send()
+
+        def one(turn, carry):
+            origin = self.origin(z, turn)
+            for w in range(count):
+                for kind in range(2, 9):
+                    sent(kind, turn, w)
+
+                @pl.when((z < self.samp - 1) & (origin < z))
+                def _():
+                    sent(0, turn, w)
+
+                @pl.when((z > 0) & (origin > z))
+                def _():
+                    sent(1, turn, w)
+
+                for kind in range(4, 8):
+                    self.wait_cell(fulls, recv, kind, w, origin, sib, (z, sib))
+            return carry
+
+        lax.fori_loop(1, self.samp, one, 0)
+        for w in range(count):
+
+            @pl.when(z < self.samp - 1)
+            def _():
+                sent(0, 0, w)
+
+            @pl.when(z > 0)
+            def _():
+                sent(1, 0, w)
+
+        for copy in self.own_copies(shards, fulls, own, held, 1):
+            copy.wait()
+
+    def step(self, sample, shards, fulls, send, recv, own, *held):
+        @pl.when(sample == 0)
+        def _():
+            self.start(shards, fulls, send, recv, own, held)
+
+        @pl.when(sample == 1)
+        def _():
+            self.place_own(shards, fulls, own, held)
+
+        for at, turn in ((2, 1), (3, 2), (5, 3)):
+
+            @pl.when(sample == at)
+            def _():
+                self.issue(turn, fulls, send, recv)
+
+        for at, turn in ((4, 1), (5, 2), (7, 3)):
+
+            @pl.when(sample == at)
+            def _():
+                self.finish(turn, fulls, send, recv)
+
+        for at, turn in ((5, 1), (7, 2)):
+
+            @pl.when(sample == at)
+            def _():
+                self.diagonal(turn, fulls, send, recv)
+
+    def last(self, sample, shards, fulls, send, recv, own, *held):
+        @pl.when(sample == pl.num_programs(0) - 1)
+        def _():
+            self.diagonal(3, fulls, send, recv)
+            self.drain(shards, fulls, send, recv, own, held)
+
+
+def edge_kernel(samp, seq, wide_ref, tiny_ref, rows_ref, wide_out, tiny_out, ext_out, send, recv):
+    z, me = lax.axis_index("samp"), lax.axis_index("seq")
+    samples, slots, width = rows_ref.shape
+    right, left = lax.rem(me + 1, seq), lax.rem(me + seq - 1, seq)
+    others = [(lax.rem(z + hop, samp), me) for hop in range(1, samp)]
+    greet(others + [(z, right), (z, left)])
+    copies = []
+    for hop, device in enumerate(others):
+        for kind, (ref, out) in enumerate(((wide_ref, wide_out), (tiny_ref, tiny_out))):
+            rows = ref.shape[0]
+            target = out.at[pl.ds(pl.multiple_of(z * rows, 16), rows), :]
+            copy = remote(ref, target, send.at[kind, hop], recv.at[kind, hop], device)
+            copy.start()
+            copies.append(copy)
+    before, after = ext_out.at[:, :RIM, :], ext_out.at[:, RIM + slots :, :]
+    to_right = remote(rows_ref.at[:, slots - RIM :, :], before, send.at[2, 0], recv.at[2, 0], (z, right))
+    to_left = remote(rows_ref.at[:, :RIM, :], after, send.at[2, 1], recv.at[2, 1], (z, left))
+    first, last = me == 0, me == seq - 1
+
+    @pl.when(~last)
+    def _():
+        to_right.start()
+
+    @pl.when(~first)
+    def _():
+        to_left.start()
+
+    @pl.when(first)
+    def _():
+        ext_out[:, :RIM, :] = jnp.zeros((samples, RIM, width), bf16)
+
+    @pl.when(last)
+    def _():
+        ext_out[:, RIM + slots :, :] = jnp.zeros((samples, RIM, width), bf16)
+
+    def move(sample, carry):
+        ext_out[sample, RIM : RIM + slots, :] = rows_ref[sample]
+        return carry
+
+    lax.fori_loop(0, samples, move, 0)
+    for ref, out in ((wide_ref, wide_out), (tiny_ref, tiny_out)):
+        rows = ref.shape[0]
+        out[pl.ds(pl.multiple_of(z * rows, 16), rows), :] = ref[...]
+    for copy in copies:
+        copy.wait()
+
+    @pl.when(~last)
+    def _():
+        to_right.wait_send()
+        to_left.wait_recv()
+
+    @pl.when(~first)
+    def _():
+        to_left.wait_send()
+        to_right.wait_recv()
+
+
+def edges(wide_own, tiny_own, rows):
+    samp, seq = lax.axis_size("samp"), lax.axis_size("seq")
+    samples, slots, width = rows.shape
+    place = pl.BlockSpec(memory_space=pltpu.VMEM)
+    return pl.pallas_call(
+        functools.partial(edge_kernel, samp, seq),
+        out_shape=[
+            jax.ShapeDtypeStruct((samp * wide_own.shape[0], wide_own.shape[1]), bf16),
+            jax.ShapeDtypeStruct((samp * tiny_own.shape[0], tiny_own.shape[1]), bf16),
+            jax.ShapeDtypeStruct((samples, slots + 2 * RIM, width), bf16),
+        ],
+        in_specs=[place] * 3,
+        out_specs=[place] * 3,
+        scratch_shapes=[
+            pltpu.SemaphoreType.DMA((3, samp)),
+            pltpu.SemaphoreType.DMA((3, samp)),
+        ],
+        compiler_params=pltpu.CompilerParams(
+            vmem_limit_bytes=vmem_bytes, collective_id=0, has_side_effects=True
+        ),
+        name="edges",
+    )(wide_own, tiny_own, rows)
+
+
+UNIT = 352
+
+
+def weight_grad_kernel(
+    attn_ref,
+    mix_ref,
+    ffn_ref,
+    upper_ref,
+    hidden_ref,
+    two_ref,
+    cond_ref,
+    condgrad_ref,
+    gated_ref,
+    branch_ref,
+    small_ref,
+    out_ref,
+    down_s,
+    cond_s,
+    outw_s,
+):
+    part = pl.program_id(0)
+    samp = out_ref.shape[1]
+
+    @pl.when(part == 0)
+    def _():
+        down_s[...] = mm_tn(hidden_ref[...], two_ref[...]).astype(bf16)
+        outw_s[...] = mm_tn(gated_ref[...], branch_ref[...]).astype(bf16)
+        for low in range(0, cond_s.shape[1], 768):
+            cond_s[:, low : low + 768] = mm_tn(
+                cond_ref[...], condgrad_ref[:, low : low + 768]
+            ).astype(bf16)
+
+    proj = mm_tn(attn_ref[...], mix_ref[...]).astype(bf16)
+    upw = mm_tn(ffn_ref[...], upper_ref[...]).astype(bf16)
+    rows = proj.shape[0] // samp
+    for z in range(samp):
+        out_ref[0, z, :rows, :384] = proj[z * rows : (z + 1) * rows]
+        out_ref[0, z, :rows, 384:] = upw[z * rows : (z + 1) * rows]
+        out_ref[0, z, 192:240, :] = down_s[pl.ds(pl.multiple_of(z * 384 + part * 48, 16), 48), :]
+        low = pl.multiple_of(z * 96 + part // 4 * 48, 16)
+        left = pl.multiple_of(part % 4 * 1152, LANES)
+        out_ref[0, z, 240:288, :] = cond_s[pl.ds(low, 48), pl.ds(left, 768)]
+        left = pl.multiple_of(part % 4 * 1152 + 768, LANES)
+        out_ref[0, z, 288:336, :384] = cond_s[pl.ds(low, 48), pl.ds(left, 384)]
+        low = pl.multiple_of(z * 192 + part // 2 * 48, 16)
+        left = pl.multiple_of(part % 2 * 384, LANES)
+        out_ref[0, z, 288:336, 384:] = outw_s[pl.ds(low, 48), pl.ds(left, 384)]
+        out_ref[0, z, 336:, :] = small_ref[0, z]
+
+
+def weight_grads(pairs, small, samp, seq):
+    flat = [array.reshape(-1, array.shape[-1]) for pair in pairs for array in pair]
+    rows = flat[0].shape[0]
+    columns = pl.BlockSpec((rows, 384), lambda s: (0, s))
+    specs = [whole(array.shape) for array in flat]
+    specs[1] = columns
+    specs[3] = columns
+    return pl.pallas_call(
+        weight_grad_kernel,
+        out_shape=jax.ShapeDtypeStruct((seq, samp, UNIT, 768), bf16),
+        grid=(seq,),
+        in_specs=specs + [pl.BlockSpec((1, samp, 16, 768), lambda s: (s, 0, 0, 0))],
+        out_specs=pl.BlockSpec((1, samp, UNIT, 768), lambda s: (s, 0, 0, 0)),
+        scratch_shapes=[
+            pltpu.VMEM((1536, 768), bf16),
+            pltpu.VMEM((384, 4608), bf16),
+            pltpu.VMEM((768, 768), bf16),
+        ],
+        compiler_params=params(),
+        name="weight_grads",
+    )(*flat, small)
+
+
+def add_into(target, source, lanes=slice(None)):
+    def one(step, carry):
+        rows = pl.ds(pl.multiple_of(step * 32, 32), 32)
+        both = target[rows, lanes].astype(f32) + source[rows, :].astype(f32)
+        target[rows, lanes] = both.astype(bf16)
+        return carry
+
+    lax.fori_loop(0, UNIT // 32, one, 0)
+
+
+def grad_sum_kernel(
+    grads,
+    proj_ref,
+    up_ref,
+    down_ref,
+    cond_ref,
+    outw_ref,
+    small_ref,
+    mine,
+    theirs,
+    from_x,
+    from_y,
+    last_x,
+    last_y,
+    planes,
+    shares,
+    s_sib,
+    r_sib,
+    s_own,
+    s_one,
+    r_one,
+    s_two,
+    r_two,
+    s_z,
+    r_z,
+    s_share,
+    r_share,
+):
+    z, me, sib, xn, yn, dg = places()
+    core, chip = me % 2, me // 2
+    chip_x, chip_y, chip_d = xn // 2, yn // 2, dg // 2
+    order = [[p ^ hop for hop in (2, 3, 1, 0)] for p in range(4)]
+    planes_of = [pick(z, [order[p][r] for p in range(4)]) for r in range(4)]
+    greet([(z, sib), (z, xn), (z, yn)] + [(planes_of[r], me) for r in range(3)])
+    head, tail = slice(0, 384), slice(384, 768)
+
+    def pair_copies(r, j):
+        return (
+            remote(
+                grads.at[2 * j + 1 - core, planes_of[r]],
+                theirs.at[r, j],
+                s_sib.at[r, j],
+                r_sib.at[r, j],
+                (z, sib),
+            ),
+            pltpu.make_async_copy(grads.at[2 * j + core, planes_of[r]], mine.at[r, j], s_own.at[r, j]),
+        )
+
+    def begin(r):
+        for j in range(4):
+            for copy in pair_copies(r, j):
+                copy.start()
+
+    def ones(r):
+        return (
+            remote(mine.at[r, chip_x, :, head], from_x.at[r, 0], s_one.at[r, 0], r_one.at[r, 0], (z, xn)),
+            remote(mine.at[r, chip_d, :, head], from_x.at[r, 1], s_one.at[r, 1], r_one.at[r, 1], (z, xn)),
+            remote(mine.at[r, chip_y, :, tail], from_y.at[r, 0], s_one.at[r, 2], r_one.at[r, 2], (z, yn)),
+            remote(mine.at[r, chip_d, :, tail], from_y.at[r, 1], s_one.at[r, 3], r_one.at[r, 3], (z, yn)),
+        )
+
+    def twos(r):
+        return (
+            remote(mine.at[r, chip_y, :, head], last_y.at[r], s_two.at[r, 0], r_two.at[r, 0], (z, yn)),
+            remote(mine.at[r, chip_x, :, tail], last_x.at[r], s_two.at[r, 1], r_two.at[r, 1], (z, xn)),
+        )
+
+    def across(r):
+        return remote(mine.at[r, chip], planes.at[r], s_z.at[r], r_z.at[r], (planes_of[r], me))
+
+    def pairs(r):
+        for j in range(4):
+            there, here = pair_copies(r, j)
+            there.wait_recv()
+            here.wait()
+        for j in range(4):
+            add_into(mine.at[r, j], theirs.at[r, j])
+        for copy in ones(r):
+            copy.start()
+
+    def middle(r):
+        one = ones(r)
+        two = twos(r)
+        one[1].wait_recv()
+        add_into(mine.at[r, chip_y], from_x.at[r, 1], head)
+        two[0].start()
+        one[3].wait_recv()
+        add_into(mine.at[r, chip_x], from_y.at[r, 1], tail)
+        two[1].start()
+        one[0].wait_recv()
+        add_into(mine.at[r, chip], from_x.at[r, 0], head)
+        one[2].wait_recv()
+        add_into(mine.at[r, chip], from_y.at[r, 0], tail)
+
+    def finish(r):
+        two = twos(r)
+        two[0].wait_recv()
+        add_into(mine.at[r, chip], last_y.at[r], head)
+        two[1].wait_recv()
+        add_into(mine.at[r, chip], last_x.at[r], tail)
+        if r < 3:
+            across(r).start()
+
+    begin(0)
+    for r in range(6):
+        if r < 4:
+            if r < 3:
+                begin(r + 1)
+            pairs(r)
+        if 1 <= r < 5:
+            middle(r - 1)
+        if r >= 2:
+            finish(r - 2)
+    for r in range(3):
+        across(r).wait_recv()
+
+    def total(step, carry):
+        rows = pl.ds(pl.multiple_of(step * 32, 32), 32)
+        both = mine[3, chip, rows, :].astype(f32)
+        for r in range(3):
+            both += planes[r, rows, :].astype(f32)
+        shares[me, rows, :] = both.astype(bf16)
+        return carry
+
+    lax.fori_loop(0, UNIT // 32, total, 0)
+
+    def share(part, lanes, kind, device):
+        ref = shares.at[part, :, lanes]
+        return remote(ref, ref, s_share.at[kind], r_share.at[kind], (z, device))
+
+    full = slice(0, 768)
+    sends = [share(me, full, 0, xn), share(me, full, 1, yn), share(me, full, 4, sib)]
+    for copy in sends:
+        copy.start()
+    share(xn, full, 0, xn).wait_recv()
+    more = [share(xn, head, 2, yn), share(xn, full, 5, sib)]
+    for copy in more:
+        copy.start()
+    share(yn, full, 1, yn).wait_recv()
+    more += [share(yn, tail, 3, xn), share(yn, full, 6, sib)]
+    for copy in more[2:]:
+        copy.start()
+    share(dg, head, 2, yn).wait_recv()
+    share(dg, tail, 3, xn).wait_recv()
+    more.append(share(dg, full, 7, sib))
+    more[-1].start()
+    for kind in range(4, 8):
+        share(sib, full, kind, sib).wait_recv()
+    for copy in sends + more:
+        copy.wait_send()
+    for r in range(4):
+        for j in range(4):
+            pair_copies(r, j)[0].wait_send()
+        for copy in ones(r) + twos(r):
+            copy.wait_send()
+        if r < 3:
+            across(r).wait_send()
+
+    for part in range(8):
+        proj_ref[:, part * 384 : (part + 1) * 384] = shares[part, :192, head].astype(f32)
+        up_ref[:, part * 384 : (part + 1) * 384] = shares[part, :192, tail].astype(f32)
+        down_ref[part * 48 : (part + 1) * 48, :] = shares[part, 192:240, :].astype(f32)
+        low, left = part // 4 * 48, part % 4 * 1152
+        cond_ref[low : low + 48, left : left + 768] = shares[part, 240:288, :].astype(f32)
+        cond_ref[low : low + 48, left + 768 : left + 1152] = shares[part, 288:336, head].astype(f32)
+        low, left = part // 2 * 48, part % 2 * 384
+        outw_ref[low : low + 48, left : left + 384] = shares[part, 288:336, tail].astype(f32)
+        small_ref[part] = shares[part, 336:, :].astype(f32)
+
+
+def grad_sums(grads, shapes):
+    seq = grads.shape[0]
+    outs = list(shapes) + [(seq, 16, 768)]
+    half = (UNIT, 384)
+    dma = pltpu.SemaphoreType.DMA
+    return pl.pallas_call(
+        grad_sum_kernel,
+        out_shape=[jax.ShapeDtypeStruct(shape, f32) for shape in outs],
+        in_specs=[pl.BlockSpec(memory_space=pl.ANY)],
+        out_specs=[pl.BlockSpec(memory_space=pltpu.VMEM)] * 6,
+        scratch_shapes=[
+            pltpu.VMEM((4, 4, UNIT, 768), bf16),
+            pltpu.VMEM((4, 4, UNIT, 768), bf16),
+            pltpu.VMEM((4, 2) + half, bf16),
+            pltpu.VMEM((4, 2) + half, bf16),
+            pltpu.VMEM((4,) + half, bf16),
+            pltpu.VMEM((4,) + half, bf16),
+            pltpu.VMEM((3, UNIT, 768), bf16),
+            pltpu.VMEM((8, UNIT, 768), bf16),
+            dma((4, 4)),
+            dma((4, 4)),
+            dma((4, 4)),
+            dma((4, 4)),
+            dma((4, 4)),
+            dma((4, 2)),
+            dma((4, 2)),
+            dma((3,)),
+            dma((3,)),
+            dma((8,)),
+            dma((8,)),
+        ],
+        compiler_params=pltpu.CompilerParams(
+            vmem_limit_bytes=vmem_bytes, collective_id=2, has_side_effects=True
+        ),
+        name="grad_sums",
+    )(grads)
+
+
 def pair_stats(pairs, fold):
     upper, lower = square_sums(fold, pairs.astype(f32) * pairs.astype(f32))
     features = pairs.shape[0] // WIN_Q
@@ -122,6 +766,7 @@
 
 
 def atom_fwd_kernel(
+    gather,
     starts,
     ext_ref,
     pairs_ref,
@@ -131,17 +776,21 @@
     wide_ref,
     down_ref,
     qbias_ref,
-    pooled_ref,
-    query_ref,
-    keyval_ref,
-    gate_ref,
-    probs_ref,
-    attend_ref,
-    mid_ref,
-    bias_s,
-    keys_s,
-    values_s,
+    *refs,
 ):
+    count = len(gather.shapes) if gather is not None else 0
+    shards, refs = refs[:count], refs[count:]
+    (
+        pooled_ref,
+        query_ref,
+        keyval_ref,
+        gate_ref,
+        probs_ref,
+        attend_ref,
+        mid_ref,
+    ), refs = refs[:7], refs[7:]
+    fulls, refs = refs[:count], refs[count:]
+    (bias_s, keys_s, values_s), sems = refs[:3], refs[3:]
     width = ext_ref.shape[-1]
     head_dim = width // ATOM_HEADS
     scale = float(head_dim) ** (-0.5)
@@ -150,8 +799,11 @@
     hidden_width = down_ref.shape[0]
     model_width = pooled_ref.shape[-1]
     features = pairs_ref.shape[1] // WIN_Q
-
-    @pl.when(pl.program_id(0) == 0)
+    sample = pl.program_id(0)
+    if gather is not None:
+        gather.step(sample, shards, fulls, *sems)
+
+    @pl.when(sample == 0)
     def _():
         fold = pair_fold(features)
         spread = spread_ref[...]
@@ -223,9 +875,11 @@
         pooled_ref[0, :, lane : lane + LANES] = jnp.sum(
             part.reshape(slots // MAX_ATOMS, MAX_ATOMS, LANES), 1
         )
-
-
-def atom_forward(ext, starts, pairs, spread, blocked, share, wide, down, qbias):
+    if gather is not None:
+        gather.last(sample, shards, fulls, *sems)
+
+
+def atom_forward(ext, starts, pairs, spread, blocked, share, wide, down, qbias, gather, shards):
     samples, ext_slots, width = ext.shape
     slots = ext_slots - 2 * RIM
     tokens = slots // MAX_ATOMS
@@ -241,32 +895,35 @@
         ((slots, width), f32),
         ((slots, width), f32),
     )
-    return pl.pallas_call(
-        atom_fwd_kernel,
-        out_shape=[jax.ShapeDtypeStruct((samples,) + shape, kind) for shape, kind in outs],
-        grid_spec=pltpu.PrefetchScalarGridSpec(
-            num_scalar_prefetch=1,
-            grid=(samples,),
-            in_specs=[
-                per_sample((ext_slots, width)),
-                whole(pairs.shape),
-                whole(spread.shape),
-                whole(blocked.shape),
-                whole(share.shape),
-                whole(wide.shape),
-                whole(down.shape),
-                whole(qbias.shape),
-            ],
-            out_specs=[per_sample(shape) for shape, _ in outs],
-            scratch_shapes=[
-                pltpu.VMEM((windows, stack, WIN_K), f32),
-                pltpu.VMEM((ext_slots, width), f32),
-                pltpu.VMEM((ext_slots, width), f32),
-            ],
-        ),
-        compiler_params=params(),
+    place = pl.BlockSpec(memory_space=pl.ANY)
+    results = pl.pallas_call(
+        functools.partial(atom_fwd_kernel, gather),
+        out_shape=[jax.ShapeDtypeStruct((samples,) + shape, kind) for shape, kind in outs]
+        + [jax.ShapeDtypeStruct(shape, bf16) for shape in (gather.full_shapes() if gather else [])],
+        grid=(samples,),
+        in_specs=[
+            pl.BlockSpec(memory_space=pltpu.SMEM),
+            per_sample((ext_slots, width)),
+            whole(pairs.shape),
+            whole(spread.shape),
+            whole(blocked.shape),
+            whole(share.shape),
+            whole(wide.shape),
+            whole(down.shape),
+            whole(qbias.shape),
+        ]
+        + [place] * len(shards),
+        out_specs=[per_sample(shape) for shape, _ in outs] + [place] * len(shards),
+        scratch_shapes=[
+            pltpu.VMEM((windows, stack, WIN_K), f32),
+            pltpu.VMEM((ext_slots, width), f32),
+            pltpu.VMEM((ext_slots, width), f32),
+        ]
+        + (gather.scratch() if gather else []),
+        compiler_params=gather.params() if gather else params(),
         name="atom_forward",
-    )(starts, ext, pairs, spread, blocked, share, wide, down, qbias)
+    )(starts, ext, pairs, spread, blocked, share, wide, down, qbias, *shards)
+    return results[0], results[1:7], results[7:]
 
 
 def atom_bwd_kernel(
@@ -796,8 +1453,20 @@
             token_pairw.reshape(-1),
         ]
     )
-    wide_all = lax.all_gather(wide_own, "samp", axis=0, tiled=True)
-    tiny_all = lax.all_gather(tiny_own[None], "samp", axis=0, tiled=True)
+    tiny_own = jnp.pad(tiny_own, (0, -tiny_own.size % (16 * LANES))).reshape(-1, LANES)
+    large = (token_proj, token_upw, token_downw, cond_weight, token_outw)
+    kernels = samples == 8 and WeightGather.fits([part.shape for part in large], samp, seq)
+    up_pairs = [(i, i + 1) for i in range(seq - 1)]
+    down_pairs = [(i + 1, i) for i in range(seq - 1)]
+    if kernels:
+        wide_all, tiny_all, ext = edges(wide_own, tiny_own, atom_input)
+    else:
+        wide_all = lax.all_gather(wide_own, "samp", axis=0, tiled=True)
+        tiny_all = lax.all_gather(tiny_own, "samp", axis=0, tiled=True)
+        before = lax.ppermute(atom_input[:, slots - RIM :], "seq", up_pairs)
+        after = lax.ppermute(atom_input[:, :RIM], "seq", down_pairs)
+        ext = jnp.concatenate([before, atom_input, after], 1)
+    tiny_all = tiny_all.reshape(samp, -1)
     wide = wide_all[:, : -2 * atom_width]
     down = (
         wide_all[:, -2 * atom_width :]
@@ -814,17 +1483,6 @@
     atom_pw = tiny[3].reshape(features, ATOM_HEADS)
     token_pw = tiny[4].reshape(-1, token_pairw.shape[1])
 
-    cond_w = lax.all_gather(cond_weight, "samp", axis=0, tiled=True)
-    proj_w = lax.all_gather(token_proj, "samp", axis=0, tiled=True)
-    out_w = lax.all_gather(token_outw, "samp", axis=0, tiled=True)
-    up_w = lax.all_gather(token_upw, "samp", axis=0, tiled=True)
-    down_w = lax.all_gather(token_downw, "samp", axis=0, tiled=True)
-
-    up_pairs = [(i, i + 1) for i in range(seq - 1)]
-    down_pairs = [(i + 1, i) for i in range(seq - 1)]
-    before = lax.ppermute(atom_input[:, slots - RIM :], "seq", up_pairs)
-    after = lax.ppermute(atom_input[:, :RIM], "seq", down_pairs)
-    ext = jnp.concatenate([before, atom_input, after], 1)
     rim_tokens = RIM // MAX_ATOMS
     counts = lax.dynamic_slice_in_dim(
         jnp.pad(atom_counts, (rim_tokens, rim_tokens)), seq_pos * tokens, tokens + 2 * rim_tokens
@@ -843,9 +1501,23 @@
     spread = jnp.where(
         eye[None, :, :, None], atom_pw.T[:, None, None, :], jnp.zeros((), bf16)
     ).reshape(ATOM_HEADS * WIN_Q, WIN_Q * features)
-    pooled, *stored = atom_forward(
-        ext, starts, pairs_t, spread, blocked, share, wide, down, atom_qb
-    )
+    gather = WeightGather([part.shape for part in large], samp, seq) if kernels else None
+    pooled, stored, fulls = atom_forward(
+        ext,
+        starts,
+        pairs_t,
+        spread,
+        blocked,
+        share,
+        wide,
+        down,
+        atom_qb,
+        gather,
+        large if kernels else (),
+    )
+    if not kernels:
+        fulls = [lax.all_gather(part, "samp", axis=0, tiled=True) for part in large]
+    proj_w, up_w, down_w, cond_w, out_w = fulls
     block_in = token_input.astype(f32) + pooled
 
     noise_feature = 0.25 * jnp.log(noise_levels / sigma_data)
@@ -930,54 +1602,73 @@
         - jnp.sum(pairw_mean.reshape(ATOM_HEADS, -1), 1)[None, :]
     )
 
-    grads = [
-        weight_grad(hidden, branch_two_low),
-        weight_grad(attn_in, mix_grad),
-        weight_grad(gated_low, branch_low),
-        weight_grad(ffn_in, upper_grad),
-        weight_grad(cond_low, cond_grad),
+    factors = [
+        (attn_in, mix_grad),
+        (ffn_in, upper_grad),
+        (hidden, branch_two_low),
+        (cond_low, cond_grad),
+        (gated_low, branch_low),
     ]
-    small = [
-        atom_proj_grad,
-        qb_grad.reshape(-1),
-        atom_pw_grad,
-        outw_grad,
-        upw_grad,
-        downw_grad,
-        pool_grad,
-        cond_b_grad,
-        token_qb_grad,
-        pairw_grad,
-    ]
-    flat = jnp.concatenate([part.reshape(samp, -1) for part in small], 1)
-    unit = 16 * seq * width
-    flat = jnp.pad(flat, ((0, 0), (0, -flat.shape[1] % unit))).reshape(-1, width)
-    shares, rest = sum_shares(grads, flat)
-    rest = rest.reshape(-1)
-    out, low = [], 0
-    for part in small:
+    rows = atom_width // samp
+    tiny_parts = [qb_grad.reshape(-1), atom_pw_grad, cond_b_grad, token_qb_grad, pairw_grad]
+    tiny_flat = jnp.concatenate([part.astype(bf16).reshape(samp, -1) for part in tiny_parts], 1)
+    spare = width - upw_grad.shape[1] - atom_width
+    tiny_flat = jnp.pad(tiny_flat, ((0, 0), (0, rows * spare - tiny_flat.shape[1])))
+    lanes = lambda part: part.astype(bf16).reshape(samp, rows, -1)
+    downw_two = downw_grad.astype(bf16).reshape(samp, 2, rows, atom_width)
+    small = jnp.stack(
+        [
+            lanes(pool_grad),
+            jnp.concatenate([lanes(atom_proj_grad), downw_two[:, 0], downw_two[:, 1]], -1),
+            jnp.concatenate(
+                [lanes(upw_grad), lanes(outw_grad), tiny_flat.reshape(samp, rows, spare)], -1
+            ),
+            jnp.zeros((samp, rows, width), bf16),
+        ],
+        1,
+    ).reshape(samp, -1, width)
+    if kernels:
+        small = small.reshape(samp, seq, 16, width).transpose(1, 0, 2, 3)
+        *shares, rest = grad_sums(
+            weight_grads(factors, small, samp, seq), [part.shape for part in large]
+        )
+    else:
+        shares, rest = sum_shares(
+            [weight_grad(*pair) for pair in factors], small.reshape(-1, width)
+        )
+    rest = rest.reshape(-1, width)
+    pool_out, second, third = rest[:rows], rest[rows : 2 * rows], rest[2 * rows : 3 * rows]
+    low = atom_proj_grad.shape[1]
+    downw_out = jnp.concatenate(
+        [second[:, low : low + atom_width], second[:, low + atom_width :]], 0
+    )
+    high = upw_grad.shape[1]
+    tiny_out = third[:, high + atom_width :].reshape(-1)
+    tiny_shares, cut = [], 0
+    for part in tiny_parts:
         size = part.size // samp
-        out.append(rest[low : low + size].reshape((part.shape[0] // samp,) + part.shape[1:]))
-        low += size
+        shape = (part.shape[0] // samp,) + part.shape[1:]
+        tiny_shares.append(tiny_out[cut : cut + size].reshape(shape))
+        cut += size
     return (
         block_out,
         atom_grad,
         token_grad,
-        out[0],
-        out[1],
-        out[2],
-        out[3],
-        out[4],
-        out[5],
-        out[6],
+        second[:, :low],
+        tiny_shares[0],
+        tiny_shares[1],
+        third[:, high : high + atom_width],
+        third[:, :high],
+        downw_out,
+        pool_out,
+        shares[3],
+        tiny_shares[2],
+        shares[0],
+        tiny_shares[3],
+        tiny_shares[4],
         shares[4],
-        out[7],
         shares[1],
-        out[8],
-        out[9],
         shares[2],
-        shares[3],
-        shares[0],
     )
 
 

time: 1100 us -> 699 us (0.64)
  waiting for transfers between devices: 585 us -> 116 us
  Pallas kernels: 226 us -> 409 us
  local copies, waits for them, and re-layouts: 106 us -> 53 us
  blocking collectives: 44 us -> 0 us
  matrix products: 66.9 us -> 36.6 us
  other arithmetic: 39.3 us -> 55.1 us
    unnamed x11 -> x2, waiting for transfers between devices: 227 us -> 0.03 us
    all_gather x6 -> x0, waiting for transfers between devices: 207 us -> none  [the longest x1 82.5 us: local(): up_w = lax.all_gather(token_upw, 'samp', axis=0, tiled=True)]
    pallas_call x1 -> x4, Pallas kernels: 70.2 us -> 253 us  [the longest x1 118 us: grad_sums(): pl.pallas_call(grad_sum_kernel, out_shape=[jax.ShapeDtypeStruct(shape, f3...]
    reduce_scatter x1 -> x0, waiting for transfers between devices: 45.1 us -> none  [sum_shares(): part = lax.psum_scatter(part, 'samp', scatter_dimension=0, tiled=False)]
    slice x18 -> x12, local copies, waits for them, and re-layouts: 37.9 us -> 6.67 us  [the longest x7 3.02 us: local(): tiny_shares.append(tiny_out[cut:cut + size].reshape(shape))]
    all_gather x1 -> x0, blocking collectives: 24.2 us -> none  [local(): wide_all = lax.all_gather(wide_own, 'samp', axis=0, tiled=True)]
    unnamed x197 -> x117, local copies, waits for them, and re-layouts: 49.1 us -> 28.7 us
    unnamed x1 -> x0, blocking collectives: 19.8 us -> none
  transfers between devices with their start and end apart: 14 -> 4, of which waited for: 9 -> 2; matrix products, arithmetic and copies ran while one was open for 8% -> 3% of each run, Pallas kernels for 11% -> 5%
where the time goes in v1:
time: 699 us; the launch traced here: 689 us
  Pallas kernels  409 us (59%)
  waiting for transfers between devices  116 us (17%)
  other arithmetic  55.1 us (8%)
  local copies, waits for them, and re-layouts  53 us (8%)
  matrix products  36.6 us (5%)
  between operations  15.3 us (2%)
    pallas_call x1, Pallas kernels, grad_sums(): pl.pallas_call(grad_sum_kernel, out_shape=[jax.ShapeDtypeStruct(shape, f3...  118 us
    pallas_call x1, Pallas kernels, atom_forward(): pl.pallas_call(functools.partial(atom_fwd_kernel, gather), out_shape=[jax...  95.1 us
    pallas_call x1, Pallas kernels, atom_backward(): pl.pallas_call(atom_bwd_kernel, out_shape=[jax.ShapeDtypeStruct((samples,...  75.8 us
    reduce_scatter x1, waiting for transfers between devices, local(): lax.psum_scatter(keyval_part, 'seq', scatter_dimension=0, tiled=False)  62 us
    all_gather x1, waiting for transfers between devices, local(): keyval = lax.all_gather(keyval_own, 'seq', axis=0, tiled=False)  54.3 us
    unnamed x117, local copies, waits for them, and re-layouts  28.7 us
    pallas_call x1, Pallas kernels, token_attention_back(): pl.pallas_call(token_bwd_kernel, out_shape=[jax.ShapeDtypeStruct(query.sh...  23.2 us
    pallas_call x1, Pallas kernels, weight_grads(): pl.pallas_call(weight_grad_kernel, out_shape=jax.ShapeDtypeStruct((seq, s...  20.5 us
  transfers between devices with their start and end apart: 4, of which 2 were waited for; matrix products, arithmetic and copies ran while one was open for 3% of the time, Pallas kernels for 5%

profile of v1, /device:TPU:0, one launch (start us, length us, event | category | flops | bytes accessed | tf_op | source)
XLA Modules:
  0.0 688.5 jit_solution(3926739982435324086)
XLA Ops:
  9.9 2.1 concatenate.63
  17.7 19.6 %edges.1 = (bf16[128,2176]{1,0:T(8,128)(2,1)}, bf16[64,128]{1,0:T(8,128)(2,1)}, bf16[8,704,128]{2,1,0:T(8,128)(2,1)}) custom-call(bf16[32,2176]{1,0:T(8,128)(2,1)} %copy-done.37, bf16[16,128]{1,0:T(8,128)(2,1)} %pad_bitcast_fusion.1.tiny_ref, bf16[8,512,128]{2,1,0:T(8,128)(2,1)} %rows_ref.3), custom_call_target="tpu_custom_call" | custom-call | tf_op jit(solution)/shard_map/edges/pallas_call | solution.py:440
  39.1 1.8 slice.135.wide_ref
  47.4 95.1 %atom_forward.1 = (f32[8,64,768]{2,1,0:T(8,128)}, bf16[8,512,128]{2,1,0:T(8,128)(2,1)}, bf16[8,704,256]{2,1,0:T(8,128)(2,1)}, f32[8,512,128]{2,1,0:T(8,128)}, bf...) custom-call(s32[16]{0:T(128)} %add_add_fusion.starts, ...), custom_call_target="tpu_custom_call" | custom-call | tf_op jit(solution)/shard_map/atom_forward/pallas_call | solution.py:899
  142.5 1.8 fusion.65
  145.0 2.7 convolution_add_fusion
  148.3 2.6 fusion.6
  151.5 2.6 copy-done.1
  154.1 1.4 slice.293
  156.7 11.8 %pair_bias.1.bias_ref = f32[16,64,512]{2,1,0:T(8,128)} custom-call(bf16[64,512,128]{2,1,0:T(8,128)(2,1)} %pair_ref.3, bf16[16,128]{1,0:T(8,128)(2,1)} %bitcast.159), custom_call_target="tpu_custom_call" | custom-call | tf_op jit(solution)/shard_map/pair_bias/pallas_call | solution.py:1189
  168.4 2.4 fusion.35.query_ref
  170.8 54.3 %all-gather.3.cloned.1.call-done = bf16[64,64,1536]{2,1,0:T(8,128)(2,1)} async-done(((bf16[8,64,1536]{2,1,0:T(8,128)(2,1)}), bf16[64,64,1536]{2,1,0:T(8,128)(2,1)}) %all-gather.3.cloned.1.call-update) | async-done | bytes 12582928 | tf_op jit(solution)/shard_map/all_gather | solution.py:1540
  225.1 15.3 %token_attention.1 = (f32[8,64,768]{2,1,0:T(8,128)}, bf16[8,16,64,512]{3,2,1,0:T(8,128)(2,1)}) custom-call(bf16[8,64,768]{2,1,0:T(8,128)(2,1)} %fusion.35.query_ref, bf16[8,8,64,1536]{3,2,1,0:T(8,128)(2,1)} %bitcast.118, f32[16,64,512]{2,1,0:T(8,128)} %pair_bias.1.bias_ref), custom_call_target="tpu_custom_call" | custom-call | tf_op jit(solution)/shard_map/token_attention/pallas_call | solution.py:1281
  240.4 2.4 multiply_convert_fusion.9
  242.9 3.7 fusion.64
  247.7 3.6 fusion.21
  251.4 2.6 fusion.2
  254.1 2.7 multiply_convert_fusion.1
  256.8 5.8 fusion.60
  262.7 5.1 multiply_convert_fusion.8
  267.8 3.9 multiply_convert_fusion.7
  271.7 23.2 %token_attention_back.1 = (f32[8,64,768]{2,1,0:T(8,128)}, bf16[8,8,64,1536]{3,2,1,0:T(8,128)(2,1)}, f32[16,64,512]{2,1,0:T(8,128)}) custom-call(bf16[8,64,768]{2,1,0:T(8,128)(2,1)} %fusion.35.query_ref, bf16[8,8,64,1536]{3,2,1,0:T(8,128)(2,1)} %bitcast.119, bf16[8,16,64,512]{3,2,1,0:T(8,128)(2,1)} %get-tuple-element.70.probs_ref, ...), custom_call_target="tpu_custom_call" | custom-call | tf_op jit(solution)/shard_map/token_attention_back/pallas_call | solution.py:1338
  295.2 2.1 fusion.48.cond_ref
  297.3 3.0 fusion.66
  300.3 19.4 %pair_grad.1 = (f32[16,128]{1,0:T(8,128)}, f32[16,512]{1,0:T(8,128)}) custom-call(bf16[64,512,128]{2,1,0:T(8,128)(2,1)} %pair_ref.3, f32[16,64,512]{2,1,0:T(8,128)} %get-tuple-element.93.grad_ref, bf16[16,128]{1,0:T(8,128)(2,1)} %bitcast.160), custom_call_target="tpu_custom_call" | custom-call | tf_op jit(solution)/shard_map/pair_grad/pallas_call | solution.py:1226
  321.6 3.9 pad_maximum_fusion.1.upper_ref
  325.5 62.0 %reduce-scatter.2.cloned.1.call-done = bf16[1,8,64,1536]{3,2,1,0:T(8,128)(2,1)} async-done(((bf16[8,8,64,1536]{3,2,1,0:T(8,128)(2,1)}), bf16[1,8,64,1536]{3,2,1,0:T(8,128)(2,1)}) %reduce-scatter.2.cloned.1.call-update) | async-done | bytes 1572880 | tf_op jit(solution)/shard_map/reduce_scatter | solution.py:1575
  387.5 7.4 %constant_dynamic-update-slice_fusion.17 = (bf16[8,64,4608]{2,1,0:T(8,128)(2,1)S(1)}, bf16[8,64,768]{2,1,0:T(8,128)(2,1)}, f32[8,64,768]{2,1,0:T(8,128)S(1)}) fusion(f32[8,64,4608]{2,1,0:T(8,128)} %copy-done, f32[8,64]{1,0:T(8,128)S(1)} %add_rsqrt_fusion.1, f32[8,64,768]{2,1,0:T(8,128)S(1)} %get-tuple-element.159, ...), kind=kOutput, calls=%fused_computation.118 | convolution fusion | flops 2429288448 | bytes 14159872 | tf_op jit(solution)/shard_map/...n,kn->...k/dot_general | solution.py:30
  394.9 3.2 fusion.59
  400.1 3.1 constant_dynamic-update-slice_fusion.15
  403.1 2.9 constant_dynamic-update-slice_fusion.14
  407.7 2.9 constant_dynamic-update-slice_fusion.12
  410.6 2.1 copy-done.10
  412.8 3.3 reduce_sum.159
  416.1 3.5 multiply_add_fusion.grad_ref
  419.5 75.8 %atom_backward.1 = (bf16[8,512,256]{2,1,0:T(8,128)(2,1)}, f32[8,512,256]{2,1,0:T(8,128)}, bf16[8,96,256]{2,1,0:T(8,128)(2,1)}, bf16[8,96,256]{2,1,0:T(8,128)(2,1...) custom-call(s32[16]{0:T(128)} %add_add_fusion.starts, ...), custom_call_target="tpu_custom_call" | custom-call | tf_op jit(solution)/shard_map/atom_backward/pallas_call | solution.py:1102
  501.2 1.9 collective-permute-start
  503.1 1.3 collective-permute-start.1
  509.3 1.4 copy-done.23
  511.5 1.9 pad_maximum_fusion.mix_ref
  514.1 10.0 %atom_input_backward.1 = (f32[8,512,128]{2,1,0:T(8,128)}, f32[128,512]{1,0:T(8,128)}) custom-call(bf16[8,512,128]{2,1,0:T(8,128)(2,1)} %rows_ref.3, bf16[8,512,256]{2,1,0:T(8,128)(2,1)} %get-tuple-element.79.mix_ref, f32[8,512,256]{2,1,0:T(8,128)} %get-tuple-element.80.own_ref, bf16[8,96,256]{2,1,0:T(8,128)(2,1)} %copy-done.35, ...), custom_call_target="tpu_custom_call" | custom-call | tf_op jit(solution)/shard_map/atom_input_backward/pallas_call | solution.py:1151
  526.2 20.5 %weight_grads.1.grads = bf16[8,4,352,768]{3,2,1,0:T(8,128)(2,1)} custom-call(bf16[512,768]{1,0:T(8,128)(2,1)} %bitcast.123, bf16[512,3072]{1,0:T(8,128)(2,1)} %pad_maximum_fusion.mix_ref, bf16[512,768]{1,0:T(8,128)(2,1)} %bitcast.122, bf16[512,3072]{1,0:T(8,128)(2,1)} %pad_maximum_fusion.1.upper_ref, bf16[512,1536]{1,0:T(8,128)(2,1)} %bitcast.138, ...), custom_call_target="tpu_custom_call" | custom-call | tf_op jit(solution)/shard_map/weight_grads/pallas_call | solution.py:517
  546.7 118.1 %grad_sums.1 = (f32[192,3072]{1,0:T(8,128)}, f32[192,3072]{1,0:T(8,128)}, f32[384,768]{1,0:T(8,128)}, f32[96,4608]{1,0:T(8,128)}, f32[192,768]{1,0:T(8,128)}, /*index=5*/f32[8,16,768]{2,1,0:T(8,128)}) custom-call(bf16[8,4,352,768]{3,2,1,0:T(8,128)(2,1)} %weight_grads.1.grads), custom_call_target="tpu_custom_call" | custom-call | tf_op jit(solution)/shard_map/grad_sums/pallas_call | solution.py:718
  664.9 1.8 fusion.67
  672.9 1.2 copy.96
  674.1 1.1 copy-done.20
  675.2 1.4 copy.97
  678.1 1.4 copy.99
  (213 shorter events, 50.2 us)
Async XLA Ops:
  7.2 33.7 %copy-start.43 = (s32[16]{0:T(128)S(1)}, s32[16]{0:T(128)}, u32[]{:S(2)}) copy-start(s32[16]{0:T(128)} %param.28) | copy-start | bytes 196
  7.2 34.2 %copy-start.44 = (f32[8]{0:T(128)S(1)}, f32[8]{0:T(128)}, u32[]{:S(2)}) copy-start(f32[8]{0:T(128)} %param.32) | copy-start | bytes 100
  7.2 34.5 %copy-start.38 = (bf16[64,384]{1,0:T(8,128)(2,1)S(1)}, bf16[64,384]{1,0:T(8,128)(2,1)}, u32[]{:S(2)}) copy-start(bf16[64,384]{1,0:T(8,128)(2,1)} %param.31) | copy-start | bytes 147460
  7.2 34.5 %copy-start.39 = (f32[384]{0:T(512)S(1)}, f32[384]{0:T(512)}, u32[]{:S(2)}) copy-start(f32[384]{0:T(512)} %param.33) | copy-start | bytes 4612
  7.2 217.9 %all-gather.3.cloned.1.call-start = ((), (), s32[]{:S(2)}) async-start(), calls=%async_computation.2 | async-start | bytes 14155776 | tf_op jit(solution)/shard_map/all_gather | solution.py:1540
  47.4 95.1 %copy-start.32 = (bf16[8,64,768]{2,1,0:T(8,128)(2,1)S(1)}, bf16[8,64,768]{2,1,0:T(8,128)(2,1)}, u32[]{:S(2)}) copy-start(bf16[8,64,768]{2,1,0:T(8,128)(2,1)} %param.26) | copy-start | bytes 2359300
  142.5 2.5 copy-start.40
  144.3 3.9 slice-start
  145.0 3.3 slice-start.1
  147.7 3.6 copy-start
  148.2 3.2 copy-start.5
  151.5 2.6 copy-start.1
  155.5 232.1 %reduce-scatter.2.cloned.1.call-start = ((), (), s32[]{:S(2)}) async-start(), calls=%async_computation.1 | async-start | bytes 14155776 | tf_op jit(solution)/shard_map/reduce_scatter | solution.py:1575
  240.4 2.4 copy-start.42
  242.8 3.7 copy-start.18
  246.5 4.8 slice-start.2
  247.7 3.7 slice-start.3
  251.3 2.7 copy-start.4
  251.3 2.7 copy-start.17
  251.4 2.7 copy-start.41
  256.8 5.9 copy-start.25
  256.8 5.9 copy-start.26
  256.8 5.9 copy-start.22
  262.6 5.2 copy-start.8
  262.7 5.1 copy-start.27
  267.8 3.9 copy-start.33
  394.9 4.2 copy-start.28
  398.1 1.3 copy-start.3
  398.1 1.9 copy-start.9
  400.0 3.1 copy-start.7
  406.0 1.7 copy-start.24
  410.6 2.1 copy-start.10
  495.3 5.8 copy-start.36
  501.1 4.6 copy-start.31
  501.2 12.1 %collective-permute-start = (bf16[8,96,256]{2,1,0:T(8,128)(2,1)}, bf16[8,96,256]{2,1,0:T(8,128)(2,1)S(1)}, u32[]{:S(2)}, u32[]{:S(2)}) collective-permute-start(bf16[8,96,256]{2,1,0:T(8,128)(2,1)} %get-tuple-element.81), channel_id=1, source_target_pairs={{0,1},{1,2},{2,3},{3,4},{4,5},{5,6},{6,7},{8,9},{9,10},{10,11},{11... | collective-permute-start | bytes 1179656 | tf_op jit(solution)/shard_map/ppermute | solution.py:1594
  503.1 10.3 %collective-permute-start.1 = (bf16[8,96,256]{2,1,0:T(8,128)(2,1)}, bf16[8,96,256]{2,1,0:T(8,128)(2,1)}, u32[]{:S(2)}, u32[]{:S(2)}) collective-permute-start(bf16[8,96,256]{2,1,0:T(8,128)(2,1)} %get-tuple-element.82), channel_id=1, source_target_pairs={{1,0},{2,1},{3,2},{4,3},{5,4},{6,5},{7,6},{9,8},{10,9},{11,10},{12... | collective-permute-start | bytes 1179656 | tf_op jit(solution)/shard_map/ppermute | solution.py:1593
  505.7 1.2 copy-start.11
  506.0 1.2 copy-start.12
  506.9 1.2 copy-start.15
  508.1 1.2 copy-start.13
  508.1 2.6 copy-start.23
  508.1 3.4 copy-start.30
  508.4 4.9 copy-start.6
  664.9 8.0 %copy-start.21 = (f32[96,4608]{1,0:T(8,128)S(1)}, f32[96,4608]{1,0:T(8,128)}, u32[]{:S(2)}) copy-start(f32[96,4608]{1,0:T(8,128)} %get-tuple-element.217) | copy-start | bytes 5308420
  672.9 2.3 copy-start.20
  675.2 1.4 copy-start.34
  675.2 2.9 copy-start.19
  678.1 2.1 copy-start.29
  (5 other events, 4.9 us)
Sparse Core Ops, SparseCore 0:
  155.6 69.4 all-gather.2
  295.1 92.3 reduce-scatter.1

commit v2 on v1

--- a/solution.py
+++ b/solution.py
@@ -457,7 +457,7 @@
     )(wide_own, tiny_own, rows)
 
 
-UNIT = 352
+UNIT = 336
 
 
 def weight_grad_kernel(
@@ -471,7 +471,6 @@
     condgrad_ref,
     gated_ref,
     branch_ref,
-    small_ref,
     out_ref,
     down_s,
     cond_s,
@@ -504,10 +503,9 @@
         low = pl.multiple_of(z * 192 + part // 2 * 48, 16)
         left = pl.multiple_of(part % 2 * 384, LANES)
         out_ref[0, z, 288:336, 384:] = outw_s[pl.ds(low, 48), pl.ds(left, 384)]
-        out_ref[0, z, 336:, :] = small_ref[0, z]
-
-
-def weight_grads(pairs, small, samp, seq):
+
+
+def weight_grads(pairs, samp, seq):
     flat = [array.reshape(-1, array.shape[-1]) for pair in pairs for array in pair]
     rows = flat[0].shape[0]
     columns = pl.BlockSpec((rows, 384), lambda s: (0, s))
@@ -518,7 +516,7 @@
         weight_grad_kernel,
         out_shape=jax.ShapeDtypeStruct((seq, samp, UNIT, 768), bf16),
         grid=(seq,),
-        in_specs=specs + [pl.BlockSpec((1, samp, 16, 768), lambda s: (s, 0, 0, 0))],
+        in_specs=specs,
         out_specs=pl.BlockSpec((1, samp, UNIT, 768), lambda s: (s, 0, 0, 0)),
         scratch_shapes=[
             pltpu.VMEM((1536, 768), bf16),
@@ -527,200 +525,29 @@
         ],
         compiler_params=params(),
         name="weight_grads",
-    )(*flat, small)
-
-
-def add_into(target, source, lanes=slice(None)):
+    )(*flat)
+
+
+def add_into(target, source, lanes=slice(None), rows=48):
     def one(step, carry):
-        rows = pl.ds(pl.multiple_of(step * 32, 32), 32)
-        both = target[rows, lanes].astype(f32) + source[rows, :].astype(f32)
-        target[rows, lanes] = both.astype(bf16)
+        part = pl.ds(pl.multiple_of(step * rows, 16), rows)
+        both = target[part, lanes].astype(f32) + source[part, :].astype(f32)
+        target[part, lanes] = both.astype(bf16)
         return carry
 
-    lax.fori_loop(0, UNIT // 32, one, 0)
-
-
-def grad_sum_kernel(
-    grads,
-    proj_ref,
-    up_ref,
-    down_ref,
-    cond_ref,
-    outw_ref,
-    small_ref,
-    mine,
-    theirs,
-    from_x,
-    from_y,
-    last_x,
-    last_y,
-    planes,
-    shares,
-    s_sib,
-    r_sib,
-    s_own,
-    s_one,
-    r_one,
-    s_two,
-    r_two,
-    s_z,
-    r_z,
-    s_share,
-    r_share,
-):
-    z, me, sib, xn, yn, dg = places()
-    core, chip = me % 2, me // 2
-    chip_x, chip_y, chip_d = xn // 2, yn // 2, dg // 2
-    order = [[p ^ hop for hop in (2, 3, 1, 0)] for p in range(4)]
-    planes_of = [pick(z, [order[p][r] for p in range(4)]) for r in range(4)]
-    greet([(z, sib), (z, xn), (z, yn)] + [(planes_of[r], me) for r in range(3)])
-    head, tail = slice(0, 384), slice(384, 768)
-
-    def pair_copies(r, j):
-        return (
-            remote(
-                grads.at[2 * j + 1 - core, planes_of[r]],
-                theirs.at[r, j],
-                s_sib.at[r, j],
-                r_sib.at[r, j],
-                (z, sib),
-            ),
-            pltpu.make_async_copy(grads.at[2 * j + core, planes_of[r]], mine.at[r, j], s_own.at[r, j]),
-        )
-
-    def begin(r):
-        for j in range(4):
-            for copy in pair_copies(r, j):
-                copy.start()
-
-    def ones(r):
-        return (
-            remote(mine.at[r, chip_x, :, head], from_x.at[r, 0], s_one.at[r, 0], r_one.at[r, 0], (z, xn)),
-            remote(mine.at[r, chip_d, :, head], from_x.at[r, 1], s_one.at[r, 1], r_one.at[r, 1], (z, xn)),
-            remote(mine.at[r, chip_y, :, tail], from_y.at[r, 0], s_one.at[r, 2], r_one.at[r, 2], (z, yn)),
-            remote(mine.at[r, chip_d, :, tail], from_y.at[r, 1], s_one.at[r, 3], r_one.at[r, 3], (z, yn)),
-        )
-
-    def twos(r):
-        return (
-            remote(mine.at[r, chip_y, :, head], last_y.at[r], s_two.at[r, 0], r_two.at[r, 0], (z, yn)),
-            remote(mine.at[r, chip_x, :, tail], last_x.at[r], s_two.at[r, 1], r_two.at[r, 1], (z, xn)),
-        )
-
-    def across(r):
-        return remote(mine.at[r, chip], planes.at[r], s_z.at[r], r_z.at[r], (planes_of[r], me))
-
-    def pairs(r):
-        for j in range(4):
-            there, here = pair_copies(r, j)
-            there.wait_recv()
-            here.wait()
-        for j in range(4):
-            add_into(mine.at[r, j], theirs.at[r, j])
-        for copy in ones(r):
-            copy.start()
-
-    def middle(r):
-        one = ones(r)
-        two = twos(r)
-        one[1].wait_recv()
-        add_into(mine.at[r, chip_y], from_x.at[r, 1], head)
-        two[0].start()
-        one[3].wait_recv()
-        add_into(mine.at[r, chip_x], from_y.at[r, 1], tail)
-        two[1].start()
-        one[0].wait_recv()
-        add_into(mine.at[r, chip], from_x.at[r, 0], head)
-        one[2].wait_recv()
-        add_into(mine.at[r, chip], from_y.at[r, 0], tail)
-
-    def finish(r):
-        two = twos(r)
-        two[0].wait_recv()
-        add_into(mine.at[r, chip], last_y.at[r], head)
-        two[1].wait_recv()
-        add_into(mine.at[r, chip], last_x.at[r], tail)
-        if r < 3:
-            across(r).start()
-
-    begin(0)
-    for r in range(6):
-        if r < 4:
-            if r < 3:
-                begin(r + 1)
-            pairs(r)
-        if 1 <= r < 5:
-            middle(r - 1)
-        if r >= 2:
-            finish(r - 2)
-    for r in range(3):
-        across(r).wait_recv()
-
-    def total(step, carry):
-        rows = pl.ds(pl.multiple_of(step * 32, 32), 32)
-        both = mine[3, chip, rows, :].astype(f32)
-        for r in range(3):
-            both += planes[r, rows, :].astype(f32)
-        shares[me, rows, :] = both.astype(bf16)
-        return carry
-
-    lax.fori_loop(0, UNIT // 32, total, 0)
-
-    def share(part, lanes, kind, device):
-        ref = shares.at[part, :, lanes]
-        return remote(ref, ref, s_share.at[kind], r_share.at[kind], (z, device))
-
-    full = slice(0, 768)
-    sends = [share(me, full, 0, xn), share(me, full, 1, yn), share(me, full, 4, sib)]
-    for copy in sends:
-        copy.start()
-    share(xn, full, 0, xn).wait_recv()
-    more = [share(xn, head, 2, yn), share(xn, full, 5, sib)]
-    for copy in more:
-        copy.start()
-    share(yn, full, 1, yn).wait_recv()
-    more += [share(yn, tail, 3, xn), share(yn, full, 6, sib)]
-    for copy in more[2:]:
-        copy.start()
-    share(dg, head, 2, yn).wait_recv()
-    share(dg, tail, 3, xn).wait_recv()
-    more.append(share(dg, full, 7, sib))
-    more[-1].start()
-    for kind in range(4, 8):
-        share(sib, full, kind, sib).wait_recv()
-    for copy in sends + more:
-        copy.wait_send()
-    for r in range(4):
-        for j in range(4):
-            pair_copies(r, j)[0].wait_send()
-        for copy in ones(r) + twos(r):
-            copy.wait_send()
-        if r < 3:
-            across(r).wait_send()
-
-    for part in range(8):
-        proj_ref[:, part * 384 : (part + 1) * 384] = shares[part, :192, head].astype(f32)
-        up_ref[:, part * 384 : (part + 1) * 384] = shares[part, :192, tail].astype(f32)
-        down_ref[part * 48 : (part + 1) * 48, :] = shares[part, 192:240, :].astype(f32)
-        low, left = part // 4 * 48, part % 4 * 1152
-        cond_ref[low : low + 48, left : left + 768] = shares[part, 240:288, :].astype(f32)
-        cond_ref[low : low + 48, left + 768 : left + 1152] = shares[part, 288:336, head].astype(f32)
-        low, left = part // 2 * 48, part % 2 * 384
-        outw_ref[low : low + 48, left : left + 384] = shares[part, 288:336, tail].astype(f32)
-        small_ref[part] = shares[part, 336:, :].astype(f32)
-
-
-def grad_sums(grads, shapes):
-    seq = grads.shape[0]
-    outs = list(shapes) + [(seq, 16, 768)]
-    half = (UNIT, 384)
-    dma = pltpu.SemaphoreType.DMA
-    return pl.pallas_call(
-        grad_sum_kernel,
-        out_shape=[jax.ShapeDtypeStruct(shape, f32) for shape in outs],
-        in_specs=[pl.BlockSpec(memory_space=pl.ANY)],
-        out_specs=[pl.BlockSpec(memory_space=pltpu.VMEM)] * 6,
-        scratch_shapes=[
+    lax.fori_loop(0, target.shape[0] // rows, one, 0)
+
+
+class GradSum:
+    head, tail, full = slice(0, 384), slice(384, 768), slice(0, 768)
+
+    def __init__(self, shapes):
+        self.shapes = list(shapes)
+
+    def scratch(self):
+        half = (UNIT, 384)
+        dma = pltpu.SemaphoreType.DMA
+        return [
             pltpu.VMEM((4, 4, UNIT, 768), bf16),
             pltpu.VMEM((4, 4, UNIT, 768), bf16),
             pltpu.VMEM((4, 2) + half, bf16),
@@ -729,6 +556,7 @@
             pltpu.VMEM((4,) + half, bf16),
             pltpu.VMEM((3, UNIT, 768), bf16),
             pltpu.VMEM((8, UNIT, 768), bf16),
+            pltpu.VMEM((2, UNIT, 768), f32),
             dma((4, 4)),
             dma((4, 4)),
             dma((4, 4)),
@@ -740,11 +568,333 @@
             dma((3,)),
             dma((8,)),
             dma((8,)),
+            dma((2, 6)),
+        ]
+
+    def params(self):
+        return pltpu.CompilerParams(
+            vmem_limit_bytes=vmem_bytes, collective_id=2, has_side_effects=True
+        )
+
+    def bind(self, grads, totals, mine, theirs, from_x, from_y, last_x, last_y, planes, shares, stage, *sems):
+        self.grads, self.totals = grads, totals
+        self.mine, self.theirs, self.from_x, self.from_y = mine, theirs, from_x, from_y
+        self.last_x, self.last_y, self.planes, self.shares = last_x, last_y, planes, shares
+        self.stage = stage
+        (
+            self.s_sib,
+            self.r_sib,
+            self.s_own,
+            self.s_one,
+            self.r_one,
+            self.s_two,
+            self.r_two,
+            self.s_z,
+            self.r_z,
+            self.s_share,
+            self.r_share,
+            self.s_out,
+        ) = sems
+        self.z, self.me, self.sib, self.xn, self.yn, self.dg = places()
+        self.core, self.chip = self.me % 2, self.me // 2
+        self.chip_x, self.chip_y, self.chip_d = self.xn // 2, self.yn // 2, self.dg // 2
+        order = [[p ^ hop for hop in (2, 3, 1, 0)] for p in range(4)]
+        self.plane = [pick(self.z, [order[p][r] for p in range(4)]) for r in range(4)]
+
+    def there(self, r, j):
+        return remote(
+            self.grads.at[2 * j + 1 - self.core, self.plane[r]],
+            self.theirs.at[r, j],
+            self.s_sib.at[r, j],
+            self.r_sib.at[r, j],
+            (self.z, self.sib),
+        )
+
+    def here(self, r, j):
+        return pltpu.make_async_copy(
+            self.grads.at[2 * j + self.core, self.plane[r]], self.mine.at[r, j], self.s_own.at[r, j]
+        )
+
+    def one(self, r, k):
+        chip = (self.chip_x, self.chip_d, self.chip_y, self.chip_d)[k]
+        lanes = self.head if k < 2 else self.tail
+        target = (self.from_x if k < 2 else self.from_y).at[r, k % 2]
+        device = (self.z, self.xn if k < 2 else self.yn)
+        return remote(
+            self.mine.at[r, chip, :, lanes], target, self.s_one.at[r, k], self.r_one.at[r, k], device
+        )
+
+    def two(self, r, k):
+        chip, lanes, target, device = (
+            (self.chip_y, self.head, self.last_y, self.yn),
+            (self.chip_x, self.tail, self.last_x, self.xn),
+        )[k]
+        return remote(
+            self.mine.at[r, chip, :, lanes],
+            target.at[r],
+            self.s_two.at[r, k],
+            self.r_two.at[r, k],
+            (self.z, device),
+        )
+
+    def across(self, r):
+        return remote(
+            self.mine.at[r, self.chip],
+            self.planes.at[r],
+            self.s_z.at[r],
+            self.r_z.at[r],
+            (self.plane[r], self.me),
+        )
+
+    def share(self, part, lanes, kind, device):
+        ref = self.shares.at[part, :, lanes]
+        return remote(ref, ref, self.s_share.at[kind], self.r_share.at[kind], (self.z, device))
+
+    def begin(self, r):
+        for j in range(4):
+            self.there(r, j).start()
+            self.here(r, j).start()
+
+    def pairs(self, r):
+        for j in range(4):
+            self.there(r, j).wait_recv()
+            self.here(r, j).wait()
+        for j in range(4):
+            add_into(self.mine.at[r, j], self.theirs.at[r, j])
+        for k in range(4):
+            self.one(r, k).start()
+
+    def middle(self, r):
+        self.one(r, 1).wait_recv()
+        add_into(self.mine.at[r, self.chip_y], self.from_x.at[r, 1], self.head)
+        self.two(r, 0).start()
+        self.one(r, 3).wait_recv()
+        add_into(self.mine.at[r, self.chip_x], self.from_y.at[r, 1], self.tail)
+        self.two(r, 1).start()
+        self.one(r, 0).wait_recv()
+        add_into(self.mine.at[r, self.chip], self.from_x.at[r, 0], self.head)
+        self.one(r, 2).wait_recv()
+        add_into(self.mine.at[r, self.chip], self.from_y.at[r, 0], self.tail)
+
+    def finish(self, r):
+        self.two(r, 0).wait_recv()
+        add_into(self.mine.at[r, self.chip], self.last_y.at[r], self.head)
+        self.two(r, 1).wait_recv()
+        add_into(self.mine.at[r, self.chip], self.last_x.at[r], self.tail)
+        if r < 3:
+            self.across(r).start()
+
+    def total(self):
+        for r in range(3):
+            self.across(r).wait_recv()
+
+        def one(step, carry):
+            rows = pl.ds(pl.multiple_of(step * 48, 16), 48)
+            both = self.mine[3, self.chip, rows, :].astype(f32)
+            for r in range(3):
+                both += self.planes[r, rows, :].astype(f32)
+            self.shares[self.me, rows, :] = both.astype(bf16)
+            return carry
+
+        lax.fori_loop(0, UNIT // 48, one, 0)
+        self.share(self.me, self.full, 0, self.xn).start()
+        self.share(self.me, self.full, 1, self.yn).start()
+        self.share(self.me, self.full, 4, self.sib).start()
+
+    def pieces(self, part):
+        proj, upw, down, cond, outw = self.totals
+        stage = self.stage.at[part % 2]
+        low, left = part // 4 * 48, part % 4 * 1152
+        high, right = part // 2 * 48, part % 2 * 384
+        return (
+            (stage.at[:192, self.head], proj.at[:, part * 384 : (part + 1) * 384]),
+            (stage.at[:192, self.tail], upw.at[:, part * 384 : (part + 1) * 384]),
+            (stage.at[192:240, :], down.at[part * 48 : (part + 1) * 48, :]),
+            (stage.at[240:288, :], cond.at[low : low + 48, left : left + 768]),
+            (stage.at[288:336, self.head], cond.at[low : low + 48, left + 768 : left + 1152]),
+            (stage.at[288:336, self.tail], outw.at[high : high + 48, right : right + 384]),
+        )
+
+    def write(self, part):
+        return [
+            pltpu.make_async_copy(source, target, self.s_out.at[part % 2, k])
+            for k, (source, target) in enumerate(self.pieces(part))
+        ]
+
+    def collect(self):
+        me, sib, xn, yn, dg = self.me, self.sib, self.xn, self.yn, self.dg
+        self.share(xn, self.full, 0, xn).wait_recv()
+        self.share(xn, self.head, 2, yn).start()
+        self.share(xn, self.full, 5, sib).start()
+        self.share(yn, self.full, 1, yn).wait_recv()
+        self.share(yn, self.tail, 3, xn).start()
+        self.share(yn, self.full, 6, sib).start()
+        self.share(dg, self.head, 2, yn).wait_recv()
+        self.share(dg, self.tail, 3, xn).wait_recv()
+        self.share(dg, self.full, 7, sib).start()
+        for kind in range(4, 8):
+            self.share(sib, self.full, kind, sib).wait_recv()
+        for part in range(8):
+            if part >= 2:
+                for copy in self.write(part - 2):
+                    copy.wait()
+
+            def one(step, carry):
+                rows = pl.ds(pl.multiple_of(step * 48, 16), 48)
+                self.stage[part % 2, rows, :] = self.shares[part, rows, :].astype(f32)
+                return carry
+
+            lax.fori_loop(0, UNIT // 48, one, 0)
+            for copy in self.write(part):
+                copy.start()
+        for part in (6, 7):
+            for copy in self.write(part):
+                copy.wait()
+        for kind, part, lanes, device in (
+            (0, me, self.full, xn),
+            (1, me, self.full, yn),
+            (2, xn, self.head, yn),
+            (3, yn, self.tail, xn),
+            (4, me, self.full, sib),
+            (5, xn, self.full, sib),
+            (6, yn, self.full, sib),
+            (7, dg, self.full, sib),
+        ):
+            self.share(part, lanes, kind, device).wait_send()
+        for r in range(4):
+            for j in range(4):
+                self.there(r, j).wait_send()
+                self.one(r, j).wait_send()
+            for k in range(2):
+                self.two(r, k).wait_send()
+            if r < 3:
+                self.across(r).wait_send()
+
+    def hello(self):
+        greet(
+            [(self.z, self.sib), (self.z, self.xn), (self.z, self.yn)]
+            + [(self.plane[r], self.me) for r in range(3)]
+        )
+        self.begin(0)
+        self.begin(1)
+
+    def slot(self, index, grads, totals, *refs):
+        self.bind(grads, totals, *refs)
+        plan = {
+            0: [self.hello],
+            1: [lambda: self.pairs(0), lambda: self.begin(2)],
+            2: [lambda: self.pairs(1), lambda: self.begin(3)],
+            4: [lambda: self.middle(0)],
+            5: [lambda: self.pairs(2)],
+            6: [lambda: self.middle(1)],
+            7: [lambda: self.finish(0)],
+            8: [lambda: self.pairs(3)],
+            9: [lambda: self.middle(2), lambda: self.finish(1)],
+            11: [lambda: self.finish(2)],
+            13: [lambda: self.middle(3)],
+            15: [lambda: self.finish(3), self.total],
+        }
+        for at, actions in plan.items():
+
+            @pl.when(index == at)
+            def _():
+                for action in actions:
+                    action()
+
+    def last(self, grads, totals, *refs):
+        self.bind(grads, totals, *refs)
+        self.collect()
+
+
+def small_sum_kernel(
+    grads, out_ref, cores, chips, planes, share, total, s_one, r_one, s_two, r_two, s_z, r_z, s_all, r_all
+):
+    z, me, sib, xn, yn, dg = places()
+    core, chip = me % 2, me // 2
+    near = (xn, yn, dg)
+    others = [lax.rem(z + hop, 4) for hop in (1, 2, 3)]
+    greet(
+        [(z, sib)]
+        + [(z, part) for part in near]
+        + [(z, part + 1 - 2 * core) for part in near]
+        + [(other, me) for other in others]
+    )
+
+    def one(j):
+        return remote(
+            grads.at[2 * j + 1 - core], cores.at[j], s_one.at[j], r_one.at[j], (z, sib)
+        )
+
+    for j in range(4):
+        one(j).start()
+    for j in range(4):
+        one(j).wait()
+        both = cores[j].astype(f32) + grads[2 * j + core].astype(f32)
+        cores[j] = both.astype(bf16)
+
+    def two(k):
+        return remote(cores.at[near[k] // 2], chips.at[k], s_two.at[k], r_two.at[k], (z, near[k]))
+
+    for k in range(3):
+        two(k).start()
+    both = cores[chip].astype(f32)
+    for k in range(3):
+        two(k).wait()
+        both += chips[k].astype(f32)
+    share[...] = both.astype(bf16)
+
+    def three(k):
+        return remote(share.at[others[k]], planes.at[k], s_z.at[k], r_z.at[k], (others[k], me))
+
+    for k in range(3):
+        three(k).start()
+    both = share[z].astype(f32)
+    for k in range(3):
+        three(k).wait()
+        both += planes[k].astype(f32)
+    total[me] = both.astype(bf16)
+
+    receivers = [sib] + list(near) + [part + 1 - 2 * core for part in near]
+
+    def four(k, part, device):
+        return remote(total.at[part], total.at[part], s_all.at[k], r_all.at[k], (z, device))
+
+    for k, device in enumerate(receivers):
+        four(k, me, device).start()
+    for k, device in enumerate(receivers):
+        four(k, device, device).wait_recv()
+    for k, device in enumerate(receivers):
+        four(k, me, device).wait_send()
+    out_ref[...] = total[...].astype(f32)
+
+
+def small_sums(grads):
+    seq, samp, rows, width = grads.shape
+    dma = pltpu.SemaphoreType.DMA
+    return pl.pallas_call(
+        small_sum_kernel,
+        out_shape=jax.ShapeDtypeStruct((seq, rows, width), f32),
+        in_specs=[pl.BlockSpec(memory_space=pltpu.VMEM)],
+        out_specs=pl.BlockSpec(memory_space=pltpu.VMEM),
+        scratch_shapes=[
+            pltpu.VMEM((4, samp, rows, width), bf16),
+            pltpu.VMEM((3, samp, rows, width), bf16),
+            pltpu.VMEM((3, rows, width), bf16),
+            pltpu.VMEM((samp, rows, width), bf16),
+            pltpu.VMEM((seq, rows, width), bf16),
+            dma((4,)),
+            dma((4,)),
+            dma((3,)),
+            dma((3,)),
+            dma((3,)),
+            dma((3,)),
+            dma((7,)),
+            dma((7,)),
         ],
         compiler_params=pltpu.CompilerParams(
-            vmem_limit_bytes=vmem_bytes, collective_id=2, has_side_effects=True
+            vmem_limit_bytes=vmem_bytes, collective_id=3, has_side_effects=True
         ),
-        name="grad_sums",
+        name="small_sums",
     )(grads)
 
 
@@ -927,6 +1077,7 @@
 
 
 def atom_bwd_kernel(
+    summing,
     starts,
     grad_ref,
     query_ref,
@@ -939,26 +1090,26 @@
     share_ref,
     wide_ref,
     down_ref,
-    mix_ref,
-    own_ref,
-    left_ref,
-    right_ref,
-    midgrad_ref,
-    qbias_ref,
-    outw_ref,
-    upw_ref,
-    downw_ref,
-    pool_ref,
-    pairw_ref,
-    pairm_ref,
-    keys_s,
-    values_s,
-    acck_s,
-    accv_s,
-    bias_s,
-    attlow_s,
-    dq_s,
+    *refs,
 ):
+    count = len(summing.shapes) if summing is not None else 0
+    grads, refs = refs[: min(count, 1)], refs[min(count, 1) :]
+    (
+        mix_ref,
+        own_ref,
+        left_ref,
+        right_ref,
+        midgrad_ref,
+        qbias_ref,
+        outw_ref,
+        upw_ref,
+        downw_ref,
+        pool_ref,
+        pairw_ref,
+        pairm_ref,
+    ), refs = refs[:12], refs[12:]
+    totals, refs = refs[:count], refs[count:]
+    (keys_s, values_s, acck_s, accv_s, bias_s, attlow_s, dq_s), sums = refs[:7], refs[7:]
     width = query_ref.shape[-1]
     head_dim = width // ATOM_HEADS
     scale = float(head_dim) ** (-0.5)
@@ -968,6 +1119,8 @@
     model_width = grad_ref.shape[-1]
     tokens = grad_ref.shape[1]
     sample = pl.program_id(0)
+    if summing is not None:
+        summing.slot(2 * sample, *grads, totals, *sums)
 
     @pl.when(sample == 0)
     def _():
@@ -1024,6 +1177,8 @@
     values_s[...] = keyval_ref[0, :, width:].astype(f32)
     acck_s[...] = jnp.zeros_like(acck_s)
     accv_s[...] = jnp.zeros_like(accv_s)
+    if summing is not None:
+        summing.slot(2 * sample + 1, *grads, totals, *sums)
 
     def one_window(win):
         first = pl.multiple_of(win * WIN_Q, WIN_Q)
@@ -1041,8 +1196,19 @@
         dq_s[pl.ds(first, WIN_Q), :] = (
             head_fold(mm(score_low, keys), ATOM_HEADS, head_dim, 0) * scale
         )
-        acck_s[pl.ds(start, WIN_K), :] += mm_tn(score_low, queries) * scale
-        accv_s[pl.ds(start, WIN_K), :] += mm_tn(probs_low, att)
+        shift = start - first
+        lane = lax.broadcasted_iota(jnp.int32, probs.shape, 1)
+
+        def placed(values):
+            moved = pltpu.roll(values, shift, 1)
+            inside = lane >= shift
+            return jnp.concatenate(
+                [jnp.where(inside, moved, 0.0), jnp.where(inside, 0.0, moved)], 1
+            ).astype(bf16)
+
+        rows = pl.ds(first, 2 * WIN_K)
+        acck_s[rows, :] += mm_tn(placed(score_low.astype(f32)), queries) * scale
+        accv_s[rows, :] += mm_tn(placed(probs), att)
 
     def some_windows(step, carry):
         for part in range(4):
@@ -1073,9 +1239,11 @@
             return carry
 
         lax.fori_loop(0, windows, one, 0)
-
-
-def atom_backward(grad, starts, stored, pairs, share, wide, down):
+        if summing is not None:
+            summing.last(*grads, totals, *sums)
+
+
+def atom_backward(grad, starts, stored, pairs, share, wide, down, summing, weight_grad_units):
     query, keyval, gate, probs, attend, mid = stored
     samples, slots, width = query.shape
     ext_slots = slots + 2 * RIM
@@ -1099,30 +1267,34 @@
         (stack, pairs.shape[1]),
         (stack, WIN_K),
     )
-    return pl.pallas_call(
-        atom_bwd_kernel,
+    place = pl.BlockSpec(memory_space=pl.ANY)
+    sums = summing.shapes if summing else []
+    results = pl.pallas_call(
+        functools.partial(atom_bwd_kernel, summing),
         out_shape=[jax.ShapeDtypeStruct((samples,) + shape, kind) for shape, kind in outs]
-        + [jax.ShapeDtypeStruct(shape, f32) for shape in totals],
-        grid_spec=pltpu.PrefetchScalarGridSpec(
-            num_scalar_prefetch=1,
-            grid=(samples,),
-            in_specs=[per_sample(grad.shape[1:])]
-            + [per_sample(part.shape[1:]) for part in stored]
-            + [whole(part.shape) for part in (pairs, share, wide, down)],
-            out_specs=[per_sample(shape) for shape, _ in outs] + [whole(shape) for shape in totals],
-            scratch_shapes=[
-                pltpu.VMEM((ext_slots, width), f32),
-                pltpu.VMEM((ext_slots, width), f32),
-                pltpu.VMEM((ext_slots, width), f32),
-                pltpu.VMEM((ext_slots, width), f32),
-                pltpu.VMEM((windows, stack, WIN_K), f32),
-                pltpu.VMEM((slots, width), bf16),
-                pltpu.VMEM((slots, width), f32),
-            ],
-        ),
-        compiler_params=params(),
+        + [jax.ShapeDtypeStruct(shape, f32) for shape in list(totals) + list(sums)],
+        grid=(samples,),
+        in_specs=[pl.BlockSpec(memory_space=pltpu.SMEM), per_sample(grad.shape[1:])]
+        + [per_sample(part.shape[1:]) for part in stored]
+        + [whole(part.shape) for part in (pairs, share, wide, down)]
+        + [place] * len(weight_grad_units),
+        out_specs=[per_sample(shape) for shape, _ in outs]
+        + [whole(shape) for shape in totals]
+        + [place] * len(sums),
+        scratch_shapes=[
+            pltpu.VMEM((ext_slots, width), f32),
+            pltpu.VMEM((ext_slots, width), f32),
+            pltpu.VMEM((slots + 2 * WIN_K, width), f32),
+            pltpu.VMEM((slots + 2 * WIN_K, width), f32),
+            pltpu.VMEM((windows, stack, WIN_K), f32),
+            pltpu.VMEM((slots, width), bf16),
+            pltpu.VMEM((slots, width), f32),
+        ]
+        + (summing.scratch() if summing else []),
+        compiler_params=summing.params() if summing else params(),
         name="atom_backward",
-    )(starts, grad, *stored, pairs, share, wide, down)
+    )(starts, grad, *stored, pairs, share, wide, down, *weight_grad_units)
+    return results[:12], results[12:]
 
 
 def atom_input_kernel(
@@ -1587,21 +1759,6 @@
     ).astype(bf16)
     cond_b_grad = jnp.sum(cond_grad.astype(f32), (0, 1))
 
-    mix_part, own, left, right, atom_mid_grad, *atom_totals = atom_backward(
-        token_grad, starts, stored, pairs_t, share, wide, down
-    )
-    from_right = lax.ppermute(left, "seq", down_pairs)
-    from_left = lax.ppermute(right, "seq", up_pairs)
-    atom_grad, atom_proj_grad = atom_input_backward(
-        atom_input, mix_part, own, from_left, from_right, atom_mid_grad, wide
-    )
-    qb_grad, outw_grad, upw_grad, downw_grad, pool_grad, pairw_stack, pairw_mean = atom_totals
-    diagonal = pairw_stack.reshape(ATOM_HEADS, WIN_Q, WIN_Q, features)
-    atom_pw_grad = (
-        jnp.sum(jnp.where(eye[None, :, :, None], diagonal, 0.0), (1, 2)).T
-        - jnp.sum(pairw_mean.reshape(ATOM_HEADS, -1), 1)[None, :]
-    )
-
     factors = [
         (attn_in, mix_grad),
         (ffn_in, upper_grad),
@@ -1609,6 +1766,27 @@
         (cond_low, cond_grad),
         (gated_low, branch_low),
     ]
+    if kernels:
+        summing = GradSum([part.shape for part in large])
+        units = (weight_grads(factors, samp, seq),)
+    else:
+        summing, units = None, ()
+    atom_results, shares = atom_backward(
+        token_grad, starts, stored, pairs_t, share, wide, down, summing, units
+    )
+    mix_part, own, left, right, atom_mid_grad, *atom_totals = atom_results
+    from_right = lax.ppermute(left, "seq", down_pairs)
+    from_left = lax.ppermute(right, "seq", up_pairs)
+    atom_grad, atom_proj_grad = atom_input_backward(
+        atom_input, mix_part, own, from_left, from_right, atom_mid_grad, wide
+    )
+    qb_grad, outw_grad, upw_grad, downw_grad, pool_grad, pairw_stack, pairw_mean = atom_totals
+    diagonal = pairw_stack.reshape(ATOM_HEADS, WIN_Q, WIN_Q, features)
+    atom_pw_grad = (
+        jnp.sum(jnp.where(eye[None, :, :, None], diagonal, 0.0), (1, 2)).T
+        - jnp.sum(pairw_mean.reshape(ATOM_HEADS, -1), 1)[None, :]
+    )
+
     rows = atom_width // samp
     tiny_parts = [qb_grad.reshape(-1), atom_pw_grad, cond_b_grad, token_qb_grad, pairw_grad]
     tiny_flat = jnp.concatenate([part.astype(bf16).reshape(samp, -1) for part in tiny_parts], 1)
@@ -1628,10 +1806,7 @@
         1,
     ).reshape(samp, -1, width)
     if kernels:
-        small = small.reshape(samp, seq, 16, width).transpose(1, 0, 2, 3)
-        *shares, rest = grad_sums(
-            weight_grads(factors, small, samp, seq), [part.shape for part in large]
-        )
+        rest = small_sums(small.reshape(samp, seq, 16, width).transpose(1, 0, 2, 3))
     else:
         shares, rest = sum_shares(
             [weight_grad(*pair) for pair in factors], small.reshape(-1, width)

time: 699 us -> 653 us (0.934)
  Pallas kernels: 409 us -> 364 us
    pallas_call x2, Pallas kernels: 194 us -> 149 us  [the longest x1 123 us: atom_backward(): pl.pallas_call(functools.partial(atom_bwd_kernel, summing), out_shape=[ja...]
    unnamed x117 -> x129, local copies, waits for them, and re-layouts: 28.7 us -> 29 us
  transfers between devices with their start and end apart: 4 -> 4, of which waited for: 2 -> 3; matrix products, arithmetic and copies ran while one was open for 3% -> 2% of each run, Pallas kernels for 5% -> 5%
where the time goes in v2:
time: 653 us; the launch traced here: 642 us
  Pallas kernels  364 us (56%)
  waiting for transfers between devices  118 us (18%)
  local copies, waits for them, and re-layouts  54.2 us (8%)
  other arithmetic  49.5 us (8%)
  matrix products  36.9 us (6%)
  between operations  15.1 us (2%)
    pallas_call x1, Pallas kernels, atom_backward(): pl.pallas_call(functools.partial(atom_bwd_kernel, summing), out_shape=[ja...  123 us
    pallas_call x1, Pallas kernels, atom_forward(): pl.pallas_call(functools.partial(atom_fwd_kernel, gather), out_shape=[jax...  95 us
    reduce_scatter x1, waiting for transfers between devices, local(): lax.psum_scatter(keyval_part, 'seq', scatter_dimension=0, tiled=False)  62.1 us
    all_gather x1, waiting for transfers between devices, local(): keyval = lax.all_gather(keyval_own, 'seq', axis=0, tiled=False)  54.3 us
    unnamed x129, local copies, waits for them, and re-layouts  29 us
    pallas_call x1, Pallas kernels, small_sums(): pl.pallas_call(small_sum_kernel, out_shape=jax.ShapeDtypeStruct((seq, row...  26.5 us
    pallas_call x1, Pallas kernels, token_attention_back(): pl.pallas_call(token_bwd_kernel, out_shape=[jax.ShapeDtypeStruct(query.sh...  23.4 us
    pallas_call x1, Pallas kernels, weight_grads(): pl.pallas_call(weight_grad_kernel, out_shape=jax.ShapeDtypeStruct((seq, s...  20.2 us
  transfers between devices with their start and end apart: 4, of which 3 were waited for; matrix products, arithmetic and copies ran while one was open for 2% of the time, Pallas kernels for 5%

profile of v2, /device:TPU:0, one launch (start us, length us, event | category | flops | bytes accessed | tf_op | source)
XLA Modules:
  0.0 642.0 jit_solution(5996542683888785907)
XLA Ops:
  9.9 2.1 concatenate.63
  17.7 19.6 %edges.1 = (bf16[128,2176]{1,0:T(8,128)(2,1)}, bf16[64,128]{1,0:T(8,128)(2,1)}, bf16[8,704,128]{2,1,0:T(8,128)(2,1)}) custom-call(bf16[32,2176]{1,0:T(8,128)(2,1)} %copy-done.41, bf16[16,128]{1,0:T(8,128)(2,1)} %pad_bitcast_fusion.1.tiny_ref, bf16[8,512,128]{2,1,0:T(8,128)(2,1)} %rows_ref.3), custom_call_target="tpu_custom_call" | custom-call | tf_op jit(solution)/shard_map/edges/pallas_call | solution.py:440
  39.1 1.8 slice.135.wide_ref
  47.4 95.0 %atom_forward.1 = (f32[8,64,768]{2,1,0:T(8,128)}, bf16[8,512,128]{2,1,0:T(8,128)(2,1)}, bf16[8,704,256]{2,1,0:T(8,128)(2,1)}, f32[8,512,128]{2,1,0:T(8,128)}, bf...) custom-call(s32[16]{0:T(128)} %add_add_fusion.starts, ...), custom_call_target="tpu_custom_call" | custom-call | tf_op jit(solution)/shard_map/atom_forward/pallas_call | solution.py:1049
  142.4 1.8 fusion.65
  144.9 2.7 convolution_add_fusion
  148.2 2.6 fusion.6
  151.4 2.6 copy-done.1
  154.0 1.4 slice.293
  156.6 11.8 %pair_bias.1.bias_ref = f32[16,64,512]{2,1,0:T(8,128)} custom-call(bf16[64,512,128]{2,1,0:T(8,128)(2,1)} %pair_ref.3, bf16[16,128]{1,0:T(8,128)(2,1)} %bitcast.159), custom_call_target="tpu_custom_call" | custom-call | tf_op jit(solution)/shard_map/pair_bias/pallas_call | solution.py:1361
  168.3 2.4 fusion.35.query_ref
  170.7 54.3 %all-gather.3.cloned.1.call-done = bf16[64,64,1536]{2,1,0:T(8,128)(2,1)} async-done(((bf16[8,64,1536]{2,1,0:T(8,128)(2,1)}), bf16[64,64,1536]{2,1,0:T(8,128)(2,1)}) %all-gather.3.cloned.1.call-update) | async-done | bytes 12582928 | tf_op jit(solution)/shard_map/all_gather | solution.py:1712
  225.1 15.3 %token_attention.1 = (f32[8,64,768]{2,1,0:T(8,128)}, bf16[8,16,64,512]{3,2,1,0:T(8,128)(2,1)}) custom-call(bf16[8,64,768]{2,1,0:T(8,128)(2,1)} %fusion.35.query_ref, bf16[8,8,64,1536]{3,2,1,0:T(8,128)(2,1)} %bitcast.118, f32[16,64,512]{2,1,0:T(8,128)} %pair_bias.1.bias_ref), custom_call_target="tpu_custom_call" | custom-call | tf_op jit(solution)/shard_map/token_attention/pallas_call | solution.py:1453
  240.4 2.4 multiply_convert_fusion.9
  242.8 3.7 fusion.64
  247.6 3.6 fusion.21
  251.4 2.6 fusion.2
  254.0 2.7 multiply_convert_fusion.1
  256.8 5.8 fusion.60
  262.7 5.1 multiply_convert_fusion.8
  267.8 3.9 multiply_convert_fusion.7
  271.7 23.4 %token_attention_back.1 = (f32[8,64,768]{2,1,0:T(8,128)}, bf16[8,8,64,1536]{3,2,1,0:T(8,128)(2,1)}, f32[16,64,512]{2,1,0:T(8,128)}) custom-call(bf16[8,64,768]{2,1,0:T(8,128)(2,1)} %fusion.35.query_ref, bf16[8,8,64,1536]{3,2,1,0:T(8,128)(2,1)} %bitcast.119, bf16[8,16,64,512]{3,2,1,0:T(8,128)(2,1)} %get-tuple-element.69.probs_ref, ...), custom_call_target="tpu_custom_call" | custom-call | tf_op jit(solution)/shard_map/token_attention_back/pallas_call | solution.py:1510
  295.4 2.1 fusion.48.cond_ref
  297.4 3.0 fusion.66
  300.5 19.4 %pair_grad.1 = (f32[16,128]{1,0:T(8,128)}, f32[16,512]{1,0:T(8,128)}) custom-call(bf16[64,512,128]{2,1,0:T(8,128)(2,1)} %pair_ref.3, f32[16,64,512]{2,1,0:T(8,128)} %get-tuple-element.92.grad_ref, bf16[16,128]{1,0:T(8,128)(2,1)} %bitcast.160), custom_call_target="tpu_custom_call" | custom-call | tf_op jit(solution)/shard_map/pair_grad/pallas_call | solution.py:1398
  321.8 3.9 pad_maximum_fusion.1.upper_ref
  325.7 62.1 %reduce-scatter.2.cloned.1.call-done = bf16[1,8,64,1536]{3,2,1,0:T(8,128)(2,1)} async-done(((bf16[8,8,64,1536]{3,2,1,0:T(8,128)(2,1)}), bf16[1,8,64,1536]{3,2,1,0:T(8,128)(2,1)}) %reduce-scatter.2.cloned.1.call-update) | async-done | bytes 1572880 | tf_op jit(solution)/shard_map/reduce_scatter | solution.py:1747
  387.7 7.7 %fusion.59 = (f32[8,64]{1,0:T(8,128)S(1)}, f32[8,64]{1,0:T(8,128)S(1)}, f32[8,64,768]{2,1,0:T(8,128)}, f32[8,64,768]{2,1,0:T(8,128)S(1)}) fusion(f32[8,64]{1,0:T(8,128)S(1)} %add_rsqrt_fusion.1, f32[8,64,768]{2,1,0:T(8,128)S(1)} %get-tuple-element.157, f32[8,64]{1,0:T(8,128)S(1)} %broadcast_multiply_fusion.6, f32[8,64,4608]{2,1,0:T(8,128)} %copy-done, ...), kind=kOutput, calls=%fused_computation.156 | convolution fusion | flops 2428894208 | bytes 14163968 | tf_op jit(solution)/shard_map/...n,kn->...k/dot_general | solution.py:30
  395.4 3.0 constant_dynamic-update-slice_fusion.17
  400.4 3.1 constant_dynamic-update-slice_fusion.15
  403.4 2.9 constant_dynamic-update-slice_fusion.14
  408.1 2.9 constant_dynamic-update-slice_fusion.12
  410.9 2.1 copy-done.7
  413.1 3.3 reduce_sum.159
  416.4 1.3 constant_dynamic-update-slice_fusion.11
  421.7 1.9 multiply_add_fusion.grad_ref
  424.3 1.8 pad_maximum_fusion.mix_ref
  426.1 20.2 %weight_grads.1.refs_0_ = bf16[8,4,336,768]{3,2,1,0:T(8,128)(2,1)} custom-call(bf16[512,768]{1,0:T(8,128)(2,1)} %bitcast.123, bf16[512,3072]{1,0:T(8,128)(2,1)} %pad_maximum_fusion.mix_ref, bf16[512,768]{1,0:T(8,128)(2,1)} %bitcast.122, bf16[512,3072]{1,0:T(8,128)(2,1)} %pad_maximum_fusion.1.upper_ref, bf16[512,1536]{1,0:T(8,128)(2,1)} %bitcast.139, ...), custom_call_target="tpu_custom_call" | custom-call | tf_op jit(solution)/shard_map/weight_grads/pallas_call | solution.py:515
  446.4 122.8 %atom_backward.1 = (bf16[8,512,256]{2,1,0:T(8,128)(2,1)}, f32[8,512,256]{2,1,0:T(8,128)}, bf16[8,96,256]{2,1,0:T(8,128)(2,1)}, bf16[8,96,256]{2,1,0:T(8,128)(2,1...) custom-call(s32[16]{0:T(128)} %add_add_fusion.starts, ...), custom_call_target="tpu_custom_call" | custom-call | tf_op jit(solution)/shard_map/atom_backward/pallas_call | solution.py:1272
  572.3 2.9 collective-permute-start
  575.2 1.4 collective-permute-start.1
  578.1 1.2 collective-permute-done.1.right_ref
  580.1 10.0 %atom_input_backward.1 = (f32[8,512,128]{2,1,0:T(8,128)}, f32[128,512]{1,0:T(8,128)}) custom-call(bf16[8,512,128]{2,1,0:T(8,128)(2,1)} %rows_ref.3, bf16[8,512,256]{2,1,0:T(8,128)(2,1)} %get-tuple-element.78.mix_ref, f32[8,512,256]{2,1,0:T(8,128)} %get-tuple-element.79.own_ref, bf16[8,96,256]{2,1,0:T(8,128)(2,1)} %copy-done.38, ...), custom_call_target="tpu_custom_call" | custom-call | tf_op jit(solution)/shard_map/atom_input_backward/pallas_call | solution.py:1323
  592.2 26.5 %small_sums.1 = f32[8,16,768]{2,1,0:T(8,128)} custom-call(bf16[8,4,16,768]{3,2,1,0:T(8,128)(2,1)} %bitcast.133), custom_call_target="tpu_custom_call" | custom-call | tf_op jit(solution)/shard_map/small_sums/pallas_call | solution.py:874
  618.7 1.6 fusion.67
  626.6 1.2 copy.96
  628.9 1.4 copy.97
  631.8 1.4 copy.99
  (225 shorter events, 48.9 us)
Async XLA Ops:
  7.2 33.7 %copy-start.49 = (s32[16]{0:T(128)S(1)}, s32[16]{0:T(128)}, u32[]{:S(2)}) copy-start(s32[16]{0:T(128)} %param.28) | copy-start | bytes 196
  7.2 34.2 %copy-start.50 = (f32[8]{0:T(128)S(1)}, f32[8]{0:T(128)}, u32[]{:S(2)}) copy-start(f32[8]{0:T(128)} %param.32) | copy-start | bytes 100
  7.2 34.5 %copy-start.44 = (bf16[64,384]{1,0:T(8,128)(2,1)S(1)}, bf16[64,384]{1,0:T(8,128)(2,1)}, u32[]{:S(2)}) copy-start(bf16[64,384]{1,0:T(8,128)(2,1)} %param.31) | copy-start | bytes 147460
  7.2 34.5 %copy-start.45 = (f32[384]{0:T(512)S(1)}, f32[384]{0:T(512)}, u32[]{:S(2)}) copy-start(f32[384]{0:T(512)} %param.33) | copy-start | bytes 4612
  7.2 217.8 %all-gather.3.cloned.1.call-start = ((), (), s32[]{:S(2)}) async-start(), calls=%async_computation.2 | async-start | bytes 14155776 | tf_op jit(solution)/shard_map/all_gather | solution.py:1712
  47.4 95.0 %copy-start.34 = (bf16[8,64,768]{2,1,0:T(8,128)(2,1)S(1)}, bf16[8,64,768]{2,1,0:T(8,128)(2,1)}, u32[]{:S(2)}) copy-start(bf16[8,64,768]{2,1,0:T(8,128)(2,1)} %param.26) | copy-start | bytes 2359300
  142.4 2.5 copy-start.46
  144.2 3.9 slice-start
  144.9 3.3 slice-start.1
  147.6 3.6 copy-start
  148.1 3.2 copy-start.6
  151.4 2.6 copy-start.1
  155.3 232.4 %reduce-scatter.2.cloned.1.call-start = ((), (), s32[]{:S(2)}) async-start(), calls=%async_computation.1 | async-start | bytes 14155776 | tf_op jit(solution)/shard_map/reduce_scatter | solution.py:1747
  240.4 2.4 copy-start.48
  242.8 3.7 copy-start.20
  246.5 4.8 slice-start.2
  247.6 3.7 slice-start.3
  251.3 2.7 copy-start.5
  251.3 2.7 copy-start.19
  251.3 2.7 copy-start.47
  256.7 5.9 copy-start.27
  256.7 5.9 copy-start.28
  256.7 5.9 copy-start.24
  262.6 5.2 copy-start.10
  262.6 5.1 copy-start.29
  267.8 3.9 copy-start.35
  395.4 4.0 copy-start.30
  398.4 1.9 copy-start.11
  400.4 3.1 copy-start.9
  406.4 1.7 copy-start.26
  410.9 2.1 copy-start.7
  418.9 1.7 copy-start.31
  419.2 1.7 copy-start.4
  419.2 2.6 copy-start.12
  420.2 3.5 copy-start.8
  421.7 1.9 copy-start.15
  421.7 2.4 copy-start.25
  421.7 2.6 copy-start.33
  569.2 8.7 %copy-start.43 = (f32[128,128]{1,0:T(8,128)S(1)}, f32[128,128]{1,0:T(8,128)}, u32[]{:S(2)}) copy-start(f32[128,128]{1,0:T(8,128)} %get-tuple-element.88) | copy-start | bytes 196612
  570.0 8.0 %copy-start.42 = (f32[256,128]{1,0:T(8,128)S(1)}, f32[256,128]{1,0:T(8,128)}, u32[]{:S(2)}) copy-start(f32[256,128]{1,0:T(8,128)} %get-tuple-element.86) | copy-start | bytes 393220
  571.2 6.8 %copy-start.40 = (f32[128,512]{1,0:T(8,128)S(1)}, f32[128,512]{1,0:T(8,128)}, u32[]{:S(2)}) copy-start(f32[128,512]{1,0:T(8,128)} %get-tuple-element.87) | copy-start | bytes 786436
  572.3 5.8 collective-permute-start
  575.2 2.8 copy-start.37
  575.2 4.1 collective-permute-start.1
  592.2 34.3 %copy-start.23 = (f32[96,4608]{1,0:T(8,128)S(1)}, f32[96,4608]{1,0:T(8,128)}, u32[]{:S(2)}) copy-start(f32[96,4608]{1,0:T(8,128)} %get-tuple-element.215) | copy-start | bytes 5308420
  626.6 2.3 copy-start.22
  628.9 2.9 copy-start.21
  631.8 2.1 copy-start.32
  (11 other events, 13.1 us)
Sparse Core Ops, SparseCore 0:
  155.5 69.5 all-gather.2
  295.2 92.4 reduce-scatter.1

commit v3 on v2

--- a/solution.py
+++ b/solution.py
@@ -461,40 +461,24 @@
 
 
 def weight_grad_kernel(
-    attn_ref,
-    mix_ref,
-    ffn_ref,
-    upper_ref,
-    hidden_ref,
-    two_ref,
-    cond_ref,
-    condgrad_ref,
-    gated_ref,
-    branch_ref,
-    out_ref,
-    down_s,
-    cond_s,
-    outw_s,
+    attn_ref, mix_ref, cond_ref, condgrad_ref, upw_ref, downw_ref, outw_ref, out_ref, cond_s
 ):
     part = pl.program_id(0)
     samp = out_ref.shape[1]
 
     @pl.when(part == 0)
     def _():
-        down_s[...] = mm_tn(hidden_ref[...], two_ref[...]).astype(bf16)
-        outw_s[...] = mm_tn(gated_ref[...], branch_ref[...]).astype(bf16)
         for low in range(0, cond_s.shape[1], 768):
             cond_s[:, low : low + 768] = mm_tn(
                 cond_ref[...], condgrad_ref[:, low : low + 768]
             ).astype(bf16)
 
     proj = mm_tn(attn_ref[...], mix_ref[...]).astype(bf16)
-    upw = mm_tn(ffn_ref[...], upper_ref[...]).astype(bf16)
     rows = proj.shape[0] // samp
     for z in range(samp):
         out_ref[0, z, :rows, :384] = proj[z * rows : (z + 1) * rows]
-        out_ref[0, z, :rows, 384:] = upw[z * rows : (z + 1) * rows]
-        out_ref[0, z, 192:240, :] = down_s[pl.ds(pl.multiple_of(z * 384 + part * 48, 16), 48), :]
+        out_ref[0, z, :rows, 384:] = upw_ref[z * rows : (z + 1) * rows, :]
+        out_ref[0, z, 192:240, :] = downw_ref[pl.ds(pl.multiple_of(z * 384 + part * 48, 16), 48), :]
         low = pl.multiple_of(z * 96 + part // 4 * 48, 16)
         left = pl.multiple_of(part % 4 * 1152, LANES)
         out_ref[0, z, 240:288, :] = cond_s[pl.ds(low, 48), pl.ds(left, 768)]
@@ -502,27 +486,22 @@
         out_ref[0, z, 288:336, :384] = cond_s[pl.ds(low, 48), pl.ds(left, 384)]
         low = pl.multiple_of(z * 192 + part // 2 * 48, 16)
         left = pl.multiple_of(part % 2 * 384, LANES)
-        out_ref[0, z, 288:336, 384:] = outw_s[pl.ds(low, 48), pl.ds(left, 384)]
-
-
-def weight_grads(pairs, samp, seq):
-    flat = [array.reshape(-1, array.shape[-1]) for pair in pairs for array in pair]
-    rows = flat[0].shape[0]
-    columns = pl.BlockSpec((rows, 384), lambda s: (0, s))
+        out_ref[0, z, 288:336, 384:] = outw_ref[pl.ds(low, 48), pl.ds(left, 384)]
+
+
+def weight_grads(attn_in, mix_grad, cond_low, cond_grad, ready, samp, seq):
+    flat = [part.reshape(-1, part.shape[-1]) for part in (attn_in, mix_grad, cond_low, cond_grad)]
+    flat += ready
     specs = [whole(array.shape) for array in flat]
-    specs[1] = columns
-    specs[3] = columns
+    for index in (1, 4):
+        specs[index] = pl.BlockSpec((flat[index].shape[0], 384), lambda s: (0, s))
     return pl.pallas_call(
         weight_grad_kernel,
         out_shape=jax.ShapeDtypeStruct((seq, samp, UNIT, 768), bf16),
         grid=(seq,),
         in_specs=specs,
         out_specs=pl.BlockSpec((1, samp, UNIT, 768), lambda s: (s, 0, 0, 0)),
-        scratch_shapes=[
-            pltpu.VMEM((1536, 768), bf16),
-            pltpu.VMEM((384, 4608), bf16),
-            pltpu.VMEM((768, 768), bf16),
-        ],
+        scratch_shapes=[pltpu.VMEM((384, 4608), bf16)],
         compiler_params=params(),
         name="weight_grads",
     )(*flat)
@@ -1535,6 +1514,437 @@
     )(query, keyval, probs, att)
 
 
+def attend_groups(heads, width, tokens, query, keyval, bias, probs_ref, fold_s):
+    head_dim, groups = head_groups(width, heads)
+    scale = float(head_dim) ** (-0.5)
+    fold_s[...] = jnp.zeros_like(fold_s)
+    for head, base, first in groups:
+        span = slice(base, base + 256)
+        stacked = head_stack(query[:, span], 4, head_dim, first)
+        scores = mm_nt(stacked, keyval(base)) * scale + bias(head)
+        exp_scores = jnp.exp(scores - jnp.max(scores, -1, keepdims=True))
+        probs = exp_scores * (1.0 / jnp.sum(exp_scores, -1, keepdims=True))
+        probs_low = probs.astype(bf16)
+        probs_ref[0, head : head + 4] = probs_low.reshape(4, tokens, -1)
+        fold_s[:, span] += head_fold(mm(probs_low, keyval(width + base)), 4, head_dim, first)
+
+
+def gather_attend_kernel(
+    query_ref,
+    own_ref,
+    pair_ref,
+    weight_ref,
+    attend_ref,
+    probs_ref,
+    keyval_ref,
+    stats_ref,
+    all_s,
+    bias_s,
+    fold_s,
+    send,
+    recv,
+    load,
+):
+    z, me, sib, xn, yn, dg = places()
+    step = pl.program_id(0)
+    tokens, width = query_ref.shape[1:]
+    heads = weight_ref.shape[0]
+    devices, samples = all_s.shape[:2]
+    keys = devices * tokens
+    head, tail, full = slice(0, width), slice(width, 2 * width), slice(0, 2 * width)
+
+    def unit(part, sample, lanes, kind, device):
+        ref = all_s.at[part, sample, :, lanes]
+        return remote(ref, ref, send.at[kind, sample], recv.at[kind, sample], (z, device))
+
+    def issue(sample):
+        unit(me, sample, full, 0, xn).start()
+        unit(me, sample, full, 1, yn).start()
+        unit(me, sample, full, 4, sib).start()
+
+    def relay(sample):
+        unit(xn, sample, full, 0, xn).wait_recv()
+        unit(xn, sample, head, 2, yn).start()
+        unit(xn, sample, full, 5, sib).start()
+        unit(yn, sample, full, 1, yn).wait_recv()
+        unit(yn, sample, tail, 3, xn).start()
+        unit(yn, sample, full, 6, sib).start()
+
+    def collect(sample):
+        unit(dg, sample, head, 2, yn).wait_recv()
+        unit(dg, sample, tail, 3, xn).wait_recv()
+        unit(dg, sample, full, 7, sib).start()
+
+    @pl.when(step == 0)
+    def _():
+        copy = pltpu.make_async_copy(own_ref, all_s.at[me], load)
+        copy.start()
+        greet([(z, sib), (z, xn), (z, yn)])
+        copy.wait()
+        issue(0)
+        issue(1)
+
+    @pl.when((step >= 1) & (step + 1 < samples))
+    def _():
+        issue(step + 1)
+
+    @pl.when((step >= 1) & (step - 1 < samples))
+    def _():
+        relay(step - 1)
+
+    @pl.when(step < 2)
+    def _():
+        weights = weight_ref[...]
+        ones_op = jnp.ones((16, weights.shape[1]), bf16)
+        weight_sum = jnp.sum(weights.astype(f32), -1, keepdims=True)
+        groups = pair_ref.shape[0] // 8
+
+        def one(group, carry):
+            for row in range(8):
+                product, mean, inv_std = row_stats(pair_ref[group * 8 + row], ones_op, weights)
+                place = step * groups + group
+                bias_s[:, place, row, :] = inv_std * (product - mean * weight_sum)
+                stats_ref[0, place, row : row + 1, :] = mean
+                stats_ref[1, place, row : row + 1, :] = inv_std
+            return carry
+
+        lax.fori_loop(0, groups, one, 0)
+
+    @pl.when(step >= 2)
+    def _():
+        sample = step - 2
+        collect(sample)
+        for kind, part in ((4, sib), (5, sib), (6, sib), (7, sib)):
+            unit(part, sample, full, kind, sib).wait_recv()
+        for part in range(devices):
+            keyval_ref[part, 0] = all_s[part, sample]
+        attend_groups(
+            heads,
+            width,
+            tokens,
+            query_ref[0],
+            lambda base: keyval_ref[:, 0, :, base : base + 256].reshape(keys, 256),
+            lambda head: bias_s[head : head + 4].reshape(4 * tokens, keys),
+            probs_ref,
+            fold_s,
+        )
+        attend_ref[0] = fold_s[...]
+
+    @pl.when(step == pl.num_programs(0) - 1)
+    def _():
+        def sent(sample, carry):
+            for kind in (0, 1, 4, 5, 6, 7):
+                unit(me, sample, full, kind, sib).wait_send()
+            unit(me, sample, head, 2, sib).wait_send()
+            unit(me, sample, tail, 3, sib).wait_send()
+            return carry
+
+        lax.fori_loop(0, samples, sent, 0)
+
+
+def gather_attend(query, own, pairs, weights, seq):
+    samples, tokens, width = query.shape
+    heads, features = weights.shape
+    keys = seq * tokens
+    late = lambda g: jnp.maximum(g - 2, 0)
+    sample_block = lambda shape: pl.BlockSpec((1,) + shape, lambda g: (late(g),) + (0,) * len(shape))
+    dma = pltpu.SemaphoreType.DMA
+    return pl.pallas_call(
+        gather_attend_kernel,
+        out_shape=[
+            jax.ShapeDtypeStruct(query.shape, f32),
+            jax.ShapeDtypeStruct((samples, heads, tokens, keys), bf16),
+            jax.ShapeDtypeStruct((seq, samples, tokens, 2 * width), bf16),
+            jax.ShapeDtypeStruct((2, tokens // 8, 8, keys), f32),
+        ],
+        grid=(samples + 2,),
+        in_specs=[
+            sample_block((tokens, width)),
+            pl.BlockSpec(memory_space=pl.ANY),
+            pl.BlockSpec((tokens // 2, keys, features), lambda g: (jnp.minimum(g, 1), 0, 0)),
+            whole(weights.shape),
+        ],
+        out_specs=[
+            sample_block((tokens, width)),
+            sample_block((heads, tokens, keys)),
+            pl.BlockSpec((seq, 1, tokens, 2 * width), lambda g: (0, late(g), 0, 0)),
+            whole((2, tokens // 8, 8, keys)),
+        ],
+        scratch_shapes=[
+            pltpu.VMEM((seq, samples, tokens, 2 * width), bf16),
+            pltpu.VMEM((heads, tokens // 8, 8, keys), f32),
+            pltpu.VMEM((tokens, width), f32),
+            dma((8, samples)),
+            dma((8, samples)),
+            dma,
+        ],
+        compiler_params=pltpu.CompilerParams(
+            vmem_limit_bytes=vmem_bytes, collective_id=4, has_side_effects=True
+        ),
+        name="gather_attend",
+    )(query, own, pairs, weights)
+
+
+def attend_back_scatter_kernel(
+    query_ref,
+    keyval_ref,
+    probs_ref,
+    att_ref,
+    pair_ref,
+    stats_ref,
+    ffn_ref,
+    upper_ref,
+    hidden_ref,
+    two_ref,
+    gated_ref,
+    branch_ref,
+    dq_ref,
+    dkv_ref,
+    pairw_ref,
+    pairm_ref,
+    upw_ref,
+    downw_ref,
+    outw_ref,
+    fold_s,
+    grad_s,
+    bias_s,
+    mine,
+    theirs,
+    from_x,
+    from_y,
+    last_x,
+    last_y,
+    s_sib,
+    r_sib,
+    s_one,
+    r_one,
+    s_two,
+    r_two,
+):
+    z, me, sib, xn, yn, dg = places()
+    core, chip = me % 2, me // 2
+    chip_x, chip_y, chip_d = xn // 2, yn // 2, dg // 2
+    step = pl.program_id(0)
+    tokens, width = query_ref.shape[1:]
+    samples = mine.shape[0]
+    heads, keys = probs_ref.shape[1], probs_ref.shape[3]
+    head_dim, groups = head_groups(width, heads)
+    scale = float(head_dim) ** (-0.5)
+    head, tail = slice(0, width), slice(width, 2 * width)
+
+    def there(b):
+        return remote(
+            mine.at[b, :, 1 - core], theirs.at[b], s_sib.at[b], r_sib.at[b], (z, sib)
+        )
+
+    def one(b, k):
+        part = (chip_x, chip_d, chip_y, chip_d)[k]
+        lanes = head if k < 2 else tail
+        target = (from_x if k < 2 else from_y).at[b, k % 2]
+        device = xn if k < 2 else yn
+        source = mine.at[b, part, core, :, lanes]
+        return remote(source, target, s_one.at[b, k], r_one.at[b, k], (z, device))
+
+    def two(b, k):
+        part, lanes, target, device = ((chip_y, head, last_y, yn), (chip_x, tail, last_x, xn))[k]
+        source = mine.at[b, part, core, :, lanes]
+        return remote(source, target.at[b], s_two.at[b, k], r_two.at[b, k], (z, device))
+
+    def add(b, part, lanes, source):
+        both = mine[b, part, core, :, lanes].astype(f32) + source.astype(f32)
+        mine[b, part, core, :, lanes] = both.astype(bf16)
+
+    @pl.when(step == 0)
+    def _():
+        greet([(z, sib), (z, xn), (z, yn)])
+        bias_s[...] = jnp.zeros_like(bias_s)
+        pairw_ref[...] = jnp.zeros_like(pairw_ref)
+        pairm_ref[...] = jnp.zeros_like(pairm_ref)
+
+    @pl.when((step >= 1) & (step - 1 < samples))
+    def _():
+        b = step - 1
+        there(b).wait_recv()
+
+        def chips(j, carry):
+            add(b, j, slice(0, 2 * width), theirs[b, j])
+            return carry
+
+        lax.fori_loop(0, 4, chips, 0)
+        for k in range(4):
+            one(b, k).start()
+
+    @pl.when((step >= 2) & (step - 2 < samples))
+    def _():
+        b = step - 2
+        one(b, 1).wait_recv()
+        add(b, chip_y, head, from_x[b, 1])
+        two(b, 0).start()
+        one(b, 3).wait_recv()
+        add(b, chip_x, tail, from_y[b, 1])
+        two(b, 1).start()
+        one(b, 0).wait_recv()
+        add(b, chip, head, from_x[b, 0])
+        one(b, 2).wait_recv()
+        add(b, chip, tail, from_y[b, 0])
+
+    @pl.when((step >= 3) & (step - 3 < samples))
+    def _():
+        b = step - 3
+        two(b, 0).wait_recv()
+        add(b, chip, head, last_y[b])
+        two(b, 1).wait_recv()
+        add(b, chip, tail, last_x[b])
+        dkv_ref[0] = mine[b, chip, core]
+
+    @pl.when(step < samples)
+    def _():
+        fold_s[...] = jnp.zeros_like(fold_s)
+        grad_s[...] = jnp.zeros_like(grad_s)
+        for first_head, base, first in groups:
+            span = slice(base, base + 256)
+            key_rows = keyval_ref[:, 0, :, base : base + 256].reshape(keys, 256)
+            value_rows = keyval_ref[:, 0, :, width + base : width + base + 256].reshape(keys, 256)
+            queries = head_stack(query_ref[0, :, span], 4, head_dim, first)
+            att = head_stack(att_ref[0, :, span], 4, head_dim, first)
+            probs_low = probs_ref[0, first_head : first_head + 4].reshape(4 * tokens, keys)
+            probs = probs_low.astype(f32)
+            prob_grad = mm_nt(att, value_rows)
+            delta = jnp.sum(prob_grad * probs, -1, keepdims=True)
+            score_low = (probs * (prob_grad - delta)).astype(bf16)
+            bias_s[first_head : first_head + 4] += score_low.astype(f32).reshape(
+                4, tokens // 8, 8, keys
+            )
+            fold_s[:, span] += head_fold(mm(score_low, key_rows), 4, head_dim, first) * scale
+            grad_s[:, span] += mm_tn(score_low, queries) * scale
+            grad_s[:, width + base : width + base + 256] += mm_tn(probs_low, att)
+        dq_ref[0] = fold_s[...]
+        mine[step] = grad_s[...].astype(bf16).reshape(mine.shape[1:])
+        there(step).start()
+        upw_ref[...] = mm_tn(ffn_ref[...], upper_ref[...]).astype(bf16)
+
+    @pl.when(step < 6)
+    def _():
+        downw_ref[...] = mm_tn(hidden_ref[...], two_ref[...]).astype(bf16)
+
+    @pl.when((step >= 6) & (step < 8))
+    def _():
+        outw_ref[...] = mm_tn(gated_ref[...], branch_ref[...]).astype(bf16)
+
+    @pl.when((step >= samples) & (step < samples + 2))
+    def _():
+        rows = pair_ref.shape[0] // 8
+
+        def some(group, carry):
+            total, means = carry
+            place = (step - samples) * rows + group
+            for row in range(8):
+                inv_std = stats_ref[1, place, row : row + 1, :]
+                scaled = bias_s[:, place, row, :] * inv_std
+                means += scaled * stats_ref[0, place, row : row + 1, :]
+                upper = scaled.astype(bf16)
+                lower = (scaled - upper.astype(f32)).astype(bf16)
+                both = mm(jnp.concatenate([upper, lower], 0), pair_ref[group * 8 + row])
+                total += both[:heads] + both[heads:]
+            return total, means
+
+        zeros = (jnp.zeros(pairw_ref.shape, f32), jnp.zeros(pairm_ref.shape, f32))
+        total, means = lax.fori_loop(0, rows, some, zeros)
+        pairw_ref[...] += total
+        pairm_ref[...] += means
+
+    @pl.when(step == pl.num_programs(0) - 1)
+    def _():
+        def sent(b, carry):
+            there(b).wait_send()
+            for k in range(4):
+                one(b, k).wait_send()
+            for k in range(2):
+                two(b, k).wait_send()
+            return carry
+
+        lax.fori_loop(0, samples, sent, 0)
+
+
+def attend_back_scatter(query, keyval, probs, att, pairs, stats, ffn, upper, hidden, two, gated, branch):
+    samples, tokens, width = query.shape
+    heads, _, keys = probs.shape[1:]
+    seq = keyval.shape[0]
+    features = pairs.shape[-1]
+    flat = [part.reshape(-1, part.shape[-1]) for part in (ffn, upper, hidden, two, gated, branch)]
+    rows = flat[0].shape[0]
+    held = lambda g: jnp.minimum(g, samples - 1)
+    late = lambda g: jnp.clip(g - 3, 0, samples - 1)
+    pair_step = lambda g: jnp.clip(g - samples, 0, 1)
+    up_step = lambda g: jnp.minimum(g, seq - 1)
+    down_step = lambda g: jnp.minimum(g, 5)
+    out_step = lambda g: jnp.clip(g - 6, 0, 1)
+    sample_block = lambda shape, at: pl.BlockSpec((1,) + shape, lambda g: (at(g),) + (0,) * len(shape))
+    keyval_block = pl.BlockSpec((seq, 1, tokens, 2 * width), lambda g: (0, held(g), 0, 0))
+    up_width = flat[1].shape[1] // seq
+    hidden_width = flat[2].shape[1]
+    dma = pltpu.SemaphoreType.DMA
+    results = pl.pallas_call(
+        attend_back_scatter_kernel,
+        out_shape=[
+            jax.ShapeDtypeStruct(query.shape, f32),
+            jax.ShapeDtypeStruct((samples, tokens, 2 * width), bf16),
+            jax.ShapeDtypeStruct((heads, features), f32),
+            jax.ShapeDtypeStruct((heads, keys), f32),
+            jax.ShapeDtypeStruct((width, flat[1].shape[1]), bf16),
+            jax.ShapeDtypeStruct((hidden_width, width), bf16),
+            jax.ShapeDtypeStruct((width, width), bf16),
+        ],
+        grid=(samples + 3,),
+        in_specs=[
+            sample_block((tokens, width), held),
+            keyval_block,
+            sample_block((heads, tokens, keys), held),
+            sample_block((tokens, width), held),
+            pl.BlockSpec((tokens // 2, keys, features), lambda g: (pair_step(g), 0, 0)),
+            whole(stats.shape),
+            whole(flat[0].shape),
+            pl.BlockSpec((rows, up_width), lambda g: (0, up_step(g))),
+            pl.BlockSpec((rows, 256), lambda g: (0, down_step(g))),
+            whole(flat[3].shape),
+            pl.BlockSpec((rows, width // 2), lambda g: (0, out_step(g))),
+            whole(flat[5].shape),
+        ],
+        out_specs=[
+            sample_block((tokens, width), held),
+            sample_block((tokens, 2 * width), late),
+            whole((heads, features)),
+            whole((heads, keys)),
+            pl.BlockSpec((width, up_width), lambda g: (0, up_step(g))),
+            pl.BlockSpec((256, width), lambda g: (down_step(g), 0)),
+            pl.BlockSpec((width // 2, width), lambda g: (out_step(g), 0)),
+        ],
+        scratch_shapes=[
+            pltpu.VMEM((tokens, width), f32),
+            pltpu.VMEM((keys, 2 * width), f32),
+            pltpu.VMEM((heads, tokens // 8, 8, keys), f32),
+            pltpu.VMEM((samples, seq // 2, 2, tokens, 2 * width), bf16),
+            pltpu.VMEM((samples, seq // 2, tokens, 2 * width), bf16),
+            pltpu.VMEM((samples, 2, tokens, width), bf16),
+            pltpu.VMEM((samples, 2, tokens, width), bf16),
+            pltpu.VMEM((samples, tokens, width), bf16),
+            pltpu.VMEM((samples, tokens, width), bf16),
+            dma((samples,)),
+            dma((samples,)),
+            dma((samples, 4)),
+            dma((samples, 4)),
+            dma((samples, 2)),
+            dma((samples, 2)),
+        ],
+        compiler_params=pltpu.CompilerParams(
+            vmem_limit_bytes=60 << 20, collective_id=5, has_side_effects=True
+        ),
+        name="attend_back_scatter",
+    )(query, keyval, probs, att, pairs, stats, *flat)
+    dq, dkv, total, means, upw, downw, outw = results
+    return dq, dkv, total - jnp.sum(means, -1, keepdims=True), (upw, downw, outw)
+
+
 def to_blocks(array, width):
     return [array[:, low : low + width] for low in range(0, array.shape[1], width)]
 
@@ -1702,15 +2112,20 @@
     parts = [cond_all[..., i * width : (i + 1) * width] for i in range(6)]
 
     pair_w = token_pw.T
-    bias = pair_bias(pair_features, pair_w)
     normed_in, inv_in = norm_stats(block_in)
     attn_in = (jax.nn.sigmoid(parts[0]) * normed_in + parts[1]).astype(bf16)
     mix = dot_last(attn_in, proj_w)
     queries = (mix[..., :width] + token_qb.astype(f32)).astype(bf16)
     keyval_own = mix[..., width : 3 * width].astype(bf16)
     gating = mix[..., 3 * width :]
-    keyval = lax.all_gather(keyval_own, "seq", axis=0, tiled=False)
-    attend, probs = token_attention(queries, keyval, bias)
+    if kernels:
+        attend, probs, keyval, stats = gather_attend(
+            queries, keyval_own, pair_features, pair_w, seq
+        )
+    else:
+        bias = pair_bias(pair_features, pair_w)
+        keyval = lax.all_gather(keyval_own, "seq", axis=0, tiled=False)
+        attend, probs = token_attention(queries, keyval, bias)
     sig_gate = jax.nn.sigmoid(gating)
     gated_low = (attend * sig_gate).astype(bf16)
     branch = dot_last(gated_low, out_w)
@@ -1743,9 +2158,28 @@
     gated_grad = dot_back(branch_low, out_w)
     attend_low = (gated_grad * sig_gate).astype(bf16)
     gating_grad = gated_grad * attend * sig_gate * (1.0 - sig_gate)
-    query_grad, keyval_part, bias_grad = token_attention_back(queries, keyval, probs, attend_low)
-    keyval_grad = lax.psum_scatter(keyval_part, "seq", scatter_dimension=0, tiled=False)
-    pairw_grad = pair_grad(pair_features, bias_grad, pair_w).T
+    if kernels:
+        query_grad, keyval_grad, pairw_grad, ready = attend_back_scatter(
+            queries,
+            keyval,
+            probs,
+            attend_low,
+            pair_features,
+            stats,
+            ffn_in,
+            upper_grad,
+            hidden,
+            branch_two_low,
+            gated_low,
+            branch_low,
+        )
+    else:
+        query_grad, keyval_part, bias_grad = token_attention_back(
+            queries, keyval, probs, attend_low
+        )
+        keyval_grad = lax.psum_scatter(keyval_part, "seq", scatter_dimension=0, tiled=False)
+        pairw_grad = pair_grad(pair_features, bias_grad, pair_w)
+    pairw_grad = pairw_grad.T
     mix_grad = jnp.concatenate(
         [query_grad.astype(bf16), keyval_grad, gating_grad.astype(bf16)], -1
     )
@@ -1759,16 +2193,9 @@
     ).astype(bf16)
     cond_b_grad = jnp.sum(cond_grad.astype(f32), (0, 1))
 
-    factors = [
-        (attn_in, mix_grad),
-        (ffn_in, upper_grad),
-        (hidden, branch_two_low),
-        (cond_low, cond_grad),
-        (gated_low, branch_low),
-    ]
     if kernels:
         summing = GradSum([part.shape for part in large])
-        units = (weight_grads(factors, samp, seq),)
+        units = (weight_grads(attn_in, mix_grad, cond_low, cond_grad, ready, samp, seq),)
     else:
         summing, units = None, ()
     atom_results, shares = atom_backward(
@@ -1808,6 +2235,13 @@
     if kernels:
         rest = small_sums(small.reshape(samp, seq, 16, width).transpose(1, 0, 2, 3))
     else:
+        factors = [
+            (attn_in, mix_grad),
+            (ffn_in, upper_grad),
+            (hidden, branch_two_low),
+            (cond_low, cond_grad),
+            (gated_low, branch_low),
+        ]
         shares, rest = sum_shares(
             [weight_grad(*pair) for pair in factors], small.reshape(-1, width)
         )

time: 653 us -> 550 us (0.84)
  waiting for transfers between devices: 118 us -> 0.01 us
  Pallas kernels: 364 us -> 418 us
  other arithmetic: 49.5 us -> 33 us
  between operations: 15.1 us -> 1.76 us
    pallas_call x4 -> x2, Pallas kernels: 69.9 us -> 132 us  [the longest x1 67.2 us: attend_back_scatter(): pl.pallas_call(attend_back_scatter_kernel, out_shape=[jax.ShapeDtypeStruc...]
    reduce_scatter x1 -> x0, waiting for transfers between devices: 62.1 us -> none  [local(): lax.psum_scatter(keyval_part, 'seq', scatter_dimension=0, tiled=False)]
    all_gather x1 -> x0, waiting for transfers between devices: 54.3 us -> none  [local(): keyval = lax.all_gather(keyval_own, 'seq', axis=0, tiled=False)]
    unnamed x7 -> x8, other arithmetic: 11 us -> 2.53 us
    unnamed x129 -> x119, local copies, waits for them, and re-layouts: 29 us -> 24.1 us
  transfers between devices with their start and end apart: 4 -> 2, of which waited for: 3 -> 0; matrix products, arithmetic and copies ran while one was open for 2% -> 1% of each run, Pallas kernels for 5% -> 0%
where the time goes in v3:
time: 550 us; the launch traced here: 539 us
  Pallas kernels  418 us (76%)
  local copies, waits for them, and re-layouts  47.7 us (9%)
  matrix products  35.2 us (6%)
  other arithmetic  33 us (6%)
    pallas_call x1, Pallas kernels, atom_backward(): pl.pallas_call(functools.partial(atom_bwd_kernel, summing), out_shape=[ja...  121 us
    pallas_call x1, Pallas kernels, atom_forward(): pl.pallas_call(functools.partial(atom_fwd_kernel, gather), out_shape=[jax...  95 us
    pallas_call x1, Pallas kernels, attend_back_scatter(): pl.pallas_call(attend_back_scatter_kernel, out_shape=[jax.ShapeDtypeStruc...  67.2 us
    pallas_call x1, Pallas kernels, gather_attend(): pl.pallas_call(gather_attend_kernel, out_shape=[jax.ShapeDtypeStruct(quer...  65.1 us
    unnamed x119, local copies, waits for them, and re-layouts  24.1 us
    pallas_call x1, Pallas kernels, small_sums(): pl.pallas_call(small_sum_kernel, out_shape=jax.ShapeDtypeStruct((seq, row...  23 us
    pallas_call x1, Pallas kernels, edges(): pl.pallas_call(functools.partial(edge_kernel, samp, seq), out_shape=[jax....  19.6 us
    dot_general x4, matrix products, dot_back(): jnp.einsum('...n,kn->...k', grad_op, weight, preferred_element_type=f32)  18.5 us
  transfers between devices with their start and end apart: 2, of which 0 were waited for; matrix products, arithmetic and copies ran while one was open for 1% of the time, Pallas kernels for 0%

profile of v3, /device:TPU:0, one launch (start us, length us, event | category | flops | bytes accessed | tf_op | source)
XLA Modules:
  0.0 539.4 jit_solution(17959455018987580739)
XLA Ops:
  4.2 0.9 broadcast_add_fusion
  6.7 2.1 concatenate.54
  13.9 19.6 %edges.1 = (bf16[128,2176]{1,0:T(8,128)(2,1)}, bf16[64,128]{1,0:T(8,128)(2,1)}, bf16[8,704,128]{2,1,0:T(8,128)(2,1)}) custom-call(bf16[32,2176]{1,0:T(8,128)(2,1)} %copy-done.31, bf16[16,128]{1,0:T(8,128)(2,1)} %pad_bitcast_fusion.1.tiny_ref, bf16[8,512,128]{2,1,0:T(8,128)(2,1)} %rows_ref.3), custom_call_target="tpu_custom_call" | custom-call | tf_op jit(solution)/shard_map/edges/pallas_call | solution.py:440
  34.5 0.8 slice.136
  35.3 1.8 slice.135.wide_ref
  42.4 0.9 broadcast_in_dim.47.blocked_ref
  43.3 95.0 %atom_forward.1 = (f32[8,64,768]{2,1,0:T(8,128)}, bf16[8,512,128]{2,1,0:T(8,128)(2,1)}, bf16[8,704,256]{2,1,0:T(8,128)(2,1)}, f32[8,512,128]{2,1,0:T(8,128)}, bf...) custom-call(s32[16]{0:T(128)} %add_add_fusion.starts, ...), custom_call_target="tpu_custom_call" | custom-call | tf_op jit(solution)/shard_map/atom_forward/pallas_call | solution.py:1028
  138.4 1.8 fusion.59
  140.8 2.7 convolution_add_fusion
  144.1 2.6 fusion.6
  147.3 1.5 slice.293.own_ref
  148.9 1.6 copy-done.1
  150.5 1.1 fusion.30.query_ref
  151.5 65.1 %gather_attend.1 = (f32[8,64,768]{2,1,0:T(8,128)}, bf16[8,16,64,512]{3,2,1,0:T(8,128)(2,1)}, bf16[8,8,64,1536]{3,2,1,0:T(8,128)(2,1)}, f32[2,8,8,512]{3,2,1,0:T(8,128)}) custom-call(bf16[8,64,768]{2,1,0:T(8,128)(2,1)} %fusion.30.query_ref, bf16[8,64,1536]{2,1,0:T(8,128)(2,1)} %slice.293.own_ref, bf16[64,512,128]{2,1,0:T(8,128)(2,1)} %pair_ref.3, ...), custom_call_target="tpu_custom_call" | custom-call | tf_op jit(solution)/shard_map/gather_attend/pallas_call | solution.py:1652
  216.7 2.4 multiply_convert_fusion.9
  219.1 3.7 fusion.58
  223.9 3.6 fusion.16
  227.6 2.6 fusion.2
  230.3 2.7 multiply_convert_fusion.1
  233.0 5.8 %fusion.54 = (f32[8,64]{1,0:T(8,128)S(1)}, f32[8,64]{1,0:T(8,128)S(1)}, f32[8,64,768]{2,1,0:T(8,128)S(1)}, f32[8,64,768]{2,1,0:T(8,128)}) fusion(f32[8,64]{1,0:T(8,128)S(1)} %add_rsqrt_fusion, f32[8,64,768]{2,1,0:T(8,128)S(1)} %get-tuple-element.145, f32[8,64]{1,0:T(8,128)S(1)} %broadcast_multiply_fusion.5, f32[8,64,4608]{2,1,0:T(8,128)} %copy-done, ...), kind=kOutput, calls=%fused_computation.151 | convolution fusion | flops 2425748480 | bytes 14163968 | tf_op jit(solution)/shard_map/...n,kn->...k/dot_general | solution.py:30
  238.8 5.1 multiply_convert_fusion.8
  244.0 3.9 multiply_convert_fusion.7
  247.9 2.1 pad_maximum_fusion.upper_ref
  250.0 67.2 %attend_back_scatter.1 = (f32[8,64,768]{2,1,0:T(8,128)}, bf16[8,64,1536]{2,1,0:T(8,128)(2,1)}, f32[16,128]{1,0:T(8,128)}, f32[16,512]{1,0:T(8,128)}, bf16[768,30...) custom-call(bf16[8,64,768]{2,1,0:T(8,128)(2,1)} %fusion.30.query_ref, ...), custom_call_target="tpu_custom_call" | custom-call | tf_op jit(solution)/shard_map/attend_back_scatter/pallas_call | solution.py:1887
  317.2 2.2 fusion.60
  319.7 6.1 %fusion.53 = (f32[8,64]{1,0:T(8,128)S(1)}, f32[8,64]{1,0:T(8,128)S(1)}, f32[8,64,768]{2,1,0:T(8,128)S(1)}, f32[8,64,768]{2,1,0:T(8,128)S(1)}) fusion(f32[8,64]{1,0:T(8,128)S(1)} %add_rsqrt_fusion.1, f32[8,64,768]{2,1,0:T(8,128)S(1)} %get-tuple-element.147, f32[8,64]{1,0:T(8,128)S(1)} %broadcast_multiply_fusion.6, f32[8,64,4608]{2,1,0:T(8,128)} %copy-done, ...), kind=kOutput, calls=%fused_computation.150 | convolution fusion | flops 2428894208 | bytes 14163968 | tf_op jit(solution)/shard_map/...n,kn->...k/dot_general | solution.py:30
  325.8 1.9 pad_maximum_fusion.1
  328.5 1.2 copy-done.9
  330.2 1.0 constant_dynamic-update-slice_fusion.15
  332.5 1.3 copy-done.17
  334.7 1.6 copy-done.10
  336.3 0.9 fusion.43.cond_ref
  337.2 1.9 multiply_add_fusion.grad_ref
  339.2 17.1 %weight_grads.1.refs_0_ = bf16[8,4,336,768]{3,2,1,0:T(8,128)(2,1)} custom-call(bf16[512,768]{1,0:T(8,128)(2,1)} %bitcast.120, bf16[512,3072]{1,0:T(8,128)(2,1)} %bitcast.116, bf16[512,384]{1,0:T(8,128)(2,1)} %fusion.43.cond_ref, bf16[512,4608]{1,0:T(8,128)(2,1)} %copy-done.6, bf16[768,3072]{1,0:T(8,128)(2,1)} %get-tuple-element.84.upw_ref, ...), custom_call_target="tpu_custom_call" | custom-call | tf_op jit(solution)/shard_map/weight_grads/pallas_call | solution.py:498
  356.3 120.7 %atom_backward.1 = (bf16[8,512,256]{2,1,0:T(8,128)(2,1)}, f32[8,512,256]{2,1,0:T(8,128)}, bf16[8,96,256]{2,1,0:T(8,128)(2,1)}, bf16[8,96,256]{2,1,0:T(8,128)(2,1...) custom-call(s32[16]{0:T(128)} %add_add_fusion.starts, ...), custom_call_target="tpu_custom_call" | custom-call | tf_op jit(solution)/shard_map/atom_backward/pallas_call | solution.py:1251
  477.0 2.6 collective-permute-start
  479.6 1.3 collective-permute-start.1
  481.5 3.4 reduce_sum.159
  487.9 10.0 %atom_input_backward.1 = (f32[8,512,128]{2,1,0:T(8,128)}, f32[128,512]{1,0:T(8,128)}) custom-call(bf16[8,512,128]{2,1,0:T(8,128)(2,1)} %rows_ref.3, bf16[8,512,256]{2,1,0:T(8,128)(2,1)} %get-tuple-element.87.mix_ref, f32[8,512,256]{2,1,0:T(8,128)} %get-tuple-element.88.own_ref, bf16[8,96,256]{2,1,0:T(8,128)(2,1)} %copy-done.27, ...), custom_call_target="tpu_custom_call" | custom-call | tf_op jit(solution)/shard_map/atom_input_backward/pallas_call | solution.py:1302
  497.9 1.0 convert_element_type.157
  499.0 1.0 copy.63
  500.0 23.0 %small_sums.1 = f32[8,16,768]{2,1,0:T(8,128)} custom-call(bf16[8,4,16,768]{3,2,1,0:T(8,128)(2,1)} %bitcast.129), custom_call_target="tpu_custom_call" | custom-call | tf_op jit(solution)/shard_map/small_sums/pallas_call | solution.py:853
  523.0 1.6 fusion.61
  530.9 1.2 copy.85
  532.1 1.1 copy-done.14
  533.2 1.4 copy.86
  536.1 1.4 copy.88
  538.2 1.0 copy.89
  (208 shorter events, 34.7 us)
Async XLA Ops:
  0.7 12.5 %copy-start.36 = (bf16[64,128]{1,0:T(8,128)(2,1)S(1)}, bf16[64,128]{1,0:T(8,128)(2,1)}, u32[]{:S(2)}) copy-start(bf16[64,128]{1,0:T(8,128)(2,1)} %param.39) | copy-start | bytes 49156
  5.1 32.1 %copy-start.41 = (s32[16]{0:T(128)S(1)}, s32[16]{0:T(128)}, u32[]{:S(2)}) copy-start(s32[16]{0:T(128)} %param.28) | copy-start | bytes 196
  43.3 95.0 %copy-start.23 = (bf16[8,64,768]{2,1,0:T(8,128)(2,1)S(1)}, bf16[8,64,768]{2,1,0:T(8,128)(2,1)}, u32[]{:S(2)}) copy-start(bf16[8,64,768]{2,1,0:T(8,128)(2,1)} %param.26) | copy-start | bytes 2359300
  138.3 2.5 copy-start.38
  140.1 3.9 slice-start.3
  140.8 3.3 slice-start.4
  143.5 3.6 copy-start
  144.1 3.2 copy-start.4
  147.3 3.1 copy-start.1
  216.7 2.4 copy-start.40
  219.1 3.7 copy-start.12
  222.8 4.8 slice-start.5
  223.9 3.7 slice-start.6
  227.5 2.7 copy-start.3
  227.6 2.7 copy-start.11
  227.6 2.7 copy-start.39
  233.0 5.8 %copy-start.16 = (bf16[8,64,1536]{2,1,0:T(8,128)(2,1)}, bf16[8,64,1536]{2,1,0:T(8,128)(2,1)S(1)}, u32[]{:S(2)}) copy-start(bf16[8,64,1536]{2,1,0:T(8,128)(2,1)S(1)} %get-tuple-element.156) | copy-start | bytes 4718596
  238.8 5.2 copy-start.8
  238.8 5.2 copy-start.18
  243.9 3.9 copy-start.24
  317.2 2.4 copy-start.19
  317.2 2.5 copy-start.22
  317.2 10.5 %slice-start = ((s8[9437184]{0:T(1024)(128)(4,1)}), s8[4194304]{0:T(1024)(128)(4,1)S(1)}, s32[]{:S(2)}) async-start(s8[9437184]{0:T(1024)(128)(4,1)} %bitcast.114), calls=%async_computation | async-start | bytes 8388608
  319.7 8.0 %slice-start.1 = ((s8[9437184]{0:T(1024)(128)(4,1)}), s8[4194304]{0:T(1024)(128)(4,1)S(1)}, s32[]{:S(2)}) async-start(s8[9437184]{0:T(1024)(128)(4,1)} %bitcast.114), calls=%async_computation.1 | async-start | bytes 8388608
  319.7 8.0 %slice-start.2 = ((s8[9437184]{0:T(1024)(128)(4,1)}), s8[1048576]{0:T(1024)(128)(4,1)S(1)}, s32[]{:S(2)}) async-start(s8[9437184]{0:T(1024)(128)(4,1)} %bitcast.114), calls=%async_computation.2 | async-start | bytes 2097152
  328.3 1.4 copy-start.9
  328.4 1.9 copy-start.20
  330.2 1.4 copy-start.7
  332.4 1.4 copy-start.17
  334.4 4.8 copy-start.5
  334.6 1.7 copy-start.10
  334.7 4.5 copy-start.6
  356.3 124.7 %copy-start.35 = (f32[16,512]{1,0:T(8,128)S(1)}, f32[16,512]{1,0:T(8,128)}, u32[]{:S(2)}) copy-start(f32[16,512]{1,0:T(8,128)} %get-tuple-element.102) | copy-start | bytes 98308
  356.3 124.8 %copy-start.37 = (f32[16,128]{1,0:T(8,128)S(1)}, f32[16,128]{1,0:T(8,128)}, u32[]{:S(2)}) copy-start(f32[16,128]{1,0:T(8,128)} %get-tuple-element.101) | copy-start | bytes 24580
  477.0 10.0 %collective-permute-start = (bf16[8,96,256]{2,1,0:T(8,128)(2,1)}, bf16[8,96,256]{2,1,0:T(8,128)(2,1)S(1)}, u32[]{:S(2)}, u32[]{:S(2)}) collective-permute-start(bf16[8,96,256]{2,1,0:T(8,128)(2,1)} %get-tuple-element.89), channel_id=1, source_target_pairs={{0,1},{1,2},{2,3},{3,4},{4,5},{5,6},{6,7},{8,9},{9,10},{10,11},{11... | collective-permute-start | bytes 1179656 | tf_op jit(solution)/shard_map/ppermute | solution.py:2206
  479.6 7.4 %collective-permute-start.1 = (bf16[8,96,256]{2,1,0:T(8,128)(2,1)}, bf16[8,96,256]{2,1,0:T(8,128)(2,1)S(1)}, u32[]{:S(2)}, u32[]{:S(2)}) collective-permute-start(bf16[8,96,256]{2,1,0:T(8,128)(2,1)} %get-tuple-element.90), channel_id=1, source_target_pairs={{1,0},{2,1},{3,2},{4,3},{5,4},{6,5},{7,6},{9,8},{10,9},{11,10},{12... | collective-permute-start | bytes 1179656 | tf_op jit(solution)/shard_map/ppermute | solution.py:2205
  481.4 3.4 copy-start.42
  481.5 3.5 copy-start.34
  481.5 3.8 copy-start.30
  484.8 1.9 copy-start.33
  485.0 1.8 copy-start.32
  485.3 1.5 copy-start.29
  485.5 1.4 copy-start.26
  500.0 30.9 %copy-start.15 = (f32[96,4608]{1,0:T(8,128)S(1)}, f32[96,4608]{1,0:T(8,128)}, u32[]{:S(2)}) copy-start(f32[96,4608]{1,0:T(8,128)} %get-tuple-element.205) | copy-start | bytes 5308420
  530.9 2.3 copy-start.14
  533.2 1.4 copy-start.25
  533.2 2.9 copy-start.13
  536.1 2.1 copy-start.21
  (4 other events, 3.4 us)
